TPU v7x, 128 devices: a whole 4x4x4 slice. The times are simulated.
128 devices in a mesh: rows: 8 (over y, core), seq: 16 (over z, x).
Axes of the slice: x: 4, y: 4, z: 4, core: 2. Of those that a mesh axis runs over, the one named last changes fastest.
Arguments:
- tokens: bfloat16 [8, 2048, 2048], P('rows', 'seq'), may hold values from -6 to 6
- grad_out: bfloat16 [8, 2048, 2048], P('rows', 'seq'), may hold values from -6 to 6
- lengths: int32 [8, 4], P('rows'), may hold values from 1 to 1984, 2048 in all within a row
- ln1_gain: bfloat16 [2048], P(('rows', 'seq')), may hold values from 0.5 to 1.5
- ln1_bias: bfloat16 [2048], P(('rows', 'seq')), may hold values from -3 to 3
- w_qkv: bfloat16 [2048, 6144], P(('rows', 'seq')), may hold values from -0.125 to 0.125
- b_qv: bfloat16 [4096], P(('rows', 'seq')), may hold values from -4 to 4
- w_out: bfloat16 [2048, 2048], P(('rows', 'seq')), may hold values from -2 to 2
- b_out: bfloat16 [2048], P(('rows', 'seq')), may hold values from -4 to 4
- ln2_gain: bfloat16 [2048], P(('rows', 'seq')), may hold values from 0.5 to 1.5
- ln2_bias: bfloat16 [2048], P(('rows', 'seq')), may hold values from -3 to 3
- w_up: bfloat16 [2048, 8192], P(('rows', 'seq')), may hold values from -0.125 to 0.125
- b_up: bfloat16 [8192], P(('rows', 'seq')), may hold values from -6 to 6
- w_down: bfloat16 [8192, 2048], P(('rows', 'seq')), may hold values from -0.0625 to 0.0625
- b_down: bfloat16 [2048], P(('rows', 'seq')), may hold values from -4 to 4
Outputs:
- out: bfloat16 [8, 2048, 2048], P('rows', 'seq')
- grad_tokens: float32 [8, 2048, 2048], P('rows', 'seq')
- g_ln1_gain: float32 [2048], P(('rows', 'seq'))
- g_ln1_bias: float32 [2048], P(('rows', 'seq'))
- g_w_qkv: float32 [2048, 6144], P(('rows', 'seq'))
- g_b_qv: float32 [4096], P(('rows', 'seq'))
- g_w_out: float32 [2048, 2048], P(('rows', 'seq'))
- g_b_out: float32 [2048], P(('rows', 'seq'))
- g_ln2_gain: float32 [2048], P(('rows', 'seq'))
- g_ln2_bias: float32 [2048], P(('rows', 'seq'))
- g_w_up: float32 [2048, 8192], P(('rows', 'seq'))
- g_b_up: float32 [8192], P(('rows', 'seq'))
- g_w_down: float32 [8192, 2048], P(('rows', 'seq'))
- g_b_down: float32 [2048], P(('rows', 'seq'))
Inputs may be any that keep to these rules, and one draw needn't show every extreme that they name: Each row's 4 lengths sum to 2048, and the longest is exactly 1984.
All inputs are finite; a program needn't handle non-finite values.
Results may differ from a plain program's by a relative error of at most 0.015.
Values may be sent and summed in bfloat16 or wider, within the bound.
A program may use at most 448 MiB of HBM per device.

v0:
```python
import math

import jax
import jax.numpy as jnp
from jax import lax
from jax.sharding import PartitionSpec as P

HEADS = 16
HEAD = 128
W = 256


EPSILON = 1e-05
NEG_FILL = -1e30


def shifted(array, axis, by):
    count = lax.axis_size(axis)
    pairs = [(i, i + by) for i in range(count) if 0 <= i + by < count]
    return lax.ppermute(array, axis, pairs)


def layer_norm(values, gain, shift):
    center = jnp.mean(values, axis=-1, keepdims=True)
    centred = values - center
    spread = jnp.mean(centred * centred, axis=-1, keepdims=True)
    return centred * lax.rsqrt(spread + EPSILON) * gain + shift


def gelu_exact(values):
    return jax.nn.gelu(values, approximate=False)


def doc_number(positions, doc_ends):
    hits = (doc_ends[:, None, :] <= positions[None, :, None]).astype(jnp.int32)
    return jnp.sum(hits, axis=2)


def masked_scores(query_heads, key_heads, visible, scale_factor):
    scores = (
        jnp.einsum("rqhd,rkhd->rhqk", query_heads, key_heads, preferred_element_type=jnp.float32)
        * scale_factor
    )
    return jnp.where(visible[:, None], scores, NEG_FILL)


def block_plan(
    tokens,
    grad_out,
    lengths,
    ln1_gain,
    ln1_bias,
    w_qkv,
    b_qv,
    w_out,
    b_out,
    ln2_gain,
    ln2_bias,
    w_up,
    b_up,
    w_down,
    b_down,
):
    row_count, blk_len, hidden_width = tokens.shape
    token_count = row_count * blk_len
    reach_blocks = W // blk_len
    key_span = (reach_blocks + 1) * blk_len
    scale_factor = 1.0 / math.sqrt(HEAD)
    seq_place = lax.axis_index("seq")
    attn_params = (
        lax.all_gather(ln1_gain, ("rows", "seq"), axis=0, tiled=True),
        lax.all_gather(ln1_bias, ("rows", "seq"), axis=0, tiled=True),
        lax.all_gather(w_qkv, ("rows", "seq"), axis=0, tiled=True),
        lax.all_gather(b_qv, ("rows", "seq"), axis=0, tiled=True),
        lax.all_gather(w_out, ("rows", "seq"), axis=0, tiled=True),
        lax.all_gather(b_out, ("rows", "seq"), axis=0, tiled=True),
    )
    gain_one, bias_one, weight_qkv, bias_qv, weight_out, bias_out = attn_params
    doc_ends = jnp.cumsum(lengths, axis=1)
    q_pos = seq_place * blk_len + jnp.arange(blk_len, dtype=jnp.int32)
    k_pos = (seq_place - reach_blocks) * blk_len + jnp.arange(key_span, dtype=jnp.int32)
    q_doc = doc_number(q_pos, doc_ends)
    k_doc = doc_number(k_pos, doc_ends)
    ordered = (
        (k_pos[None, :] <= q_pos[:, None])
        & (q_pos[:, None] - k_pos[None, :] < W)
        & (k_pos[None, :] >= 0)
    )
    visible = (q_doc[:, :, None] == k_doc[:, None, :]) & ordered[None]
    inputs = tokens.astype(jnp.float32).reshape(token_count, hidden_width)
    gain_f1 = gain_one.astype(jnp.float32)
    shift_f1 = bias_one.astype(jnp.float32)
    normed_one = layer_norm(inputs, gain_f1, shift_f1).astype(jnp.bfloat16)
    zero_bias = jnp.zeros((hidden_width,), jnp.float32)
    bias_full = jnp.concatenate(
        [
            bias_qv[:hidden_width].astype(jnp.float32),
            zero_bias,
            bias_qv[hidden_width:].astype(jnp.float32),
        ]
    )
    projected = (
        jnp.dot(normed_one, weight_qkv, preferred_element_type=jnp.float32) + bias_full
    ).astype(jnp.bfloat16)
    query_low = projected[:, :hidden_width]
    key_low = projected[:, hidden_width : 2 * hidden_width]
    value_low = projected[:, 2 * hidden_width :]
    own_kv = jnp.stack([key_low, value_low]).reshape(2, row_count, blk_len, hidden_width)
    kv_parts = []
    for offset in range(reach_blocks, 0, -1):
        kv_parts.append(shifted(own_kv, "seq", offset))
    kv_parts.append(own_kv)
    all_kv = jnp.concatenate(kv_parts, axis=2)
    query_heads = query_low.reshape(row_count, blk_len, HEADS, HEAD)
    key_heads = all_kv[0].reshape(row_count, key_span, HEADS, HEAD)
    value_heads = all_kv[1].reshape(row_count, key_span, HEADS, HEAD)
    masked = masked_scores(query_heads, key_heads, visible, scale_factor)
    peak = jnp.max(masked, axis=-1, keepdims=True)
    log_total = peak + jnp.log(jnp.sum(jnp.exp(masked - peak), axis=-1, keepdims=True))
    probs_low = jnp.exp(masked - log_total).astype(jnp.bfloat16)
    mixed = jnp.einsum(
        "rhqk,rkhd->rqhd", probs_low, value_heads, preferred_element_type=jnp.float32
    )
    mixed = mixed.reshape(token_count, hidden_width).astype(jnp.bfloat16)
    residual = (
        inputs
        + jnp.dot(mixed, weight_out, preferred_element_type=jnp.float32)
        + bias_out.astype(jnp.float32)
    )
    mlp_params = (
        lax.all_gather(ln2_gain, ("rows", "seq"), axis=0, tiled=True),
        lax.all_gather(ln2_bias, ("rows", "seq"), axis=0, tiled=True),
        lax.all_gather(w_up, ("rows", "seq"), axis=0, tiled=True),
        lax.all_gather(b_up, ("rows", "seq"), axis=0, tiled=True),
        lax.all_gather(w_down, ("rows", "seq"), axis=0, tiled=True),
        lax.all_gather(b_down, ("rows", "seq"), axis=0, tiled=True),
    )
    gain_two, bias_two, weight_up, bias_up, weight_down, bias_down = mlp_params
    gain_f2 = gain_two.astype(jnp.float32)
    shift_f2 = bias_two.astype(jnp.float32)
    normed_two = layer_norm(residual, gain_f2, shift_f2).astype(jnp.bfloat16)
    upper = jnp.dot(normed_two, weight_up, preferred_element_type=jnp.float32) + bias_up.astype(
        jnp.float32
    )
    activated = gelu_exact(upper).astype(jnp.bfloat16)
    result = (
        residual
        + jnp.dot(activated, weight_down, preferred_element_type=jnp.float32)
        + bias_down.astype(jnp.float32)
    )
    out = result.astype(jnp.bfloat16).reshape(row_count, blk_len, hidden_width)
    mlp_params = (
        lax.all_gather(ln2_gain, ("rows", "seq"), axis=0, tiled=True),
        lax.all_gather(ln2_bias, ("rows", "seq"), axis=0, tiled=True),
        lax.all_gather(w_up, ("rows", "seq"), axis=0, tiled=True),
        lax.all_gather(b_up, ("rows", "seq"), axis=0, tiled=True),
        lax.all_gather(w_down, ("rows", "seq"), axis=0, tiled=True),
        lax.all_gather(b_down, ("rows", "seq"), axis=0, tiled=True),
    )
    gain_two, bias_two, weight_up, bias_up, weight_down, bias_down = mlp_params
    cotangent = grad_out.reshape(token_count, hidden_width)
    cot_float = cotangent.astype(jnp.float32)
    grad_wdown = jnp.einsum("nf,nd->fd", activated, cotangent, preferred_element_type=jnp.float32)
    grad_bdown = jnp.sum(cot_float, axis=0)
    d_act = jnp.einsum("nd,fd->nf", cotangent, weight_down, preferred_element_type=jnp.float32)
    gelu_pull = jax.vjp(gelu_exact, upper)[1]
    d_upper = gelu_pull(d_act)[0].astype(jnp.bfloat16)
    grad_wup = jnp.einsum("nd,nf->df", normed_two, d_upper, preferred_element_type=jnp.float32)
    grad_bup = jnp.sum(d_upper.astype(jnp.float32), axis=0)
    d_normed2 = jnp.einsum("nf,df->nd", d_upper, weight_up, preferred_element_type=jnp.float32)
    norm_pull2 = jax.vjp(layer_norm, residual, gain_f2, shift_f2)[1]
    d_resnorm, grad_gain2, grad_shift2 = norm_pull2(d_normed2)
    d_hidden = cot_float + d_resnorm
    mlp_grads = (
        lax.psum_scatter(grad_gain2, ("rows", "seq"), scatter_dimension=0, tiled=True),
        lax.psum_scatter(grad_shift2, ("rows", "seq"), scatter_dimension=0, tiled=True),
        lax.psum_scatter(grad_wup, ("rows", "seq"), scatter_dimension=0, tiled=True),
        lax.psum_scatter(grad_bup, ("rows", "seq"), scatter_dimension=0, tiled=True),
        lax.psum_scatter(grad_wdown, ("rows", "seq"), scatter_dimension=0, tiled=True),
        lax.psum_scatter(grad_bdown, ("rows", "seq"), scatter_dimension=0, tiled=True),
    )
    attn_params = (
        lax.all_gather(ln1_gain, ("rows", "seq"), axis=0, tiled=True),
        lax.all_gather(ln1_bias, ("rows", "seq"), axis=0, tiled=True),
        lax.all_gather(w_qkv, ("rows", "seq"), axis=0, tiled=True),
        lax.all_gather(b_qv, ("rows", "seq"), axis=0, tiled=True),
        lax.all_gather(w_out, ("rows", "seq"), axis=0, tiled=True),
        lax.all_gather(b_out, ("rows", "seq"), axis=0, tiled=True),
    )
    gain_one, bias_one, weight_qkv, bias_qv, weight_out, bias_out = attn_params
    d_attn = d_hidden.astype(jnp.bfloat16)
    grad_wout = jnp.einsum("nd,ne->de", mixed, d_attn, preferred_element_type=jnp.float32)
    grad_bout = jnp.sum(d_attn.astype(jnp.float32), axis=0)
    d_mixed = jnp.einsum(
        "ne,de->nd", d_attn, weight_out, preferred_element_type=jnp.float32
    ).astype(jnp.bfloat16)
    d_heads = d_mixed.reshape(row_count, blk_len, HEADS, HEAD)
    masked = masked_scores(query_heads, key_heads, visible, scale_factor)
    probs = jnp.exp(masked - log_total)
    probs_low = probs.astype(jnp.bfloat16)
    d_probs = jnp.einsum(
        "rqhd,rkhd->rhqk", d_heads, value_heads, preferred_element_type=jnp.float32
    )
    d_score = (probs * (d_probs - jnp.sum(d_probs * probs, axis=-1, keepdims=True))).astype(
        jnp.bfloat16
    )
    d_query = (
        jnp.einsum("rhqk,rkhd->rqhd", d_score, key_heads, preferred_element_type=jnp.float32)
        * scale_factor
    )
    d_keys = (
        jnp.einsum("rhqk,rqhd->rkhd", d_score, query_heads, preferred_element_type=jnp.float32)
        * scale_factor
    )
    d_values = jnp.einsum("rhqk,rqhd->rkhd", probs_low, d_heads, preferred_element_type=jnp.float32)
    d_kv = jnp.stack([d_keys, d_values]).reshape(2, row_count, key_span, hidden_width)
    local_gradient = d_kv[:, :, reach_blocks * blk_len :]
    for offset in range(1, reach_blocks + 1):
        slot_start = (reach_blocks - offset) * blk_len
        edge_part = d_kv[:, :, slot_start : slot_start + blk_len]
        local_gradient = local_gradient + shifted(
            edge_part.astype(jnp.bfloat16), "seq", -offset
        ).astype(edge_part.dtype)
    grad_query_lowered = d_query.reshape(token_count, hidden_width).astype(jnp.bfloat16)
    grad_key_lowered = local_gradient[0].reshape(token_count, hidden_width).astype(jnp.bfloat16)
    grad_value_lowered = local_gradient[1].reshape(token_count, hidden_width).astype(jnp.bfloat16)
    grad_query_key_value = jnp.concatenate(
        [grad_query_lowered, grad_key_lowered, grad_value_lowered], axis=1
    )
    grad_wqkv = jnp.einsum(
        "nd,ne->de", normed_one, grad_query_key_value, preferred_element_type=jnp.float32
    )
    grad_bqv = jnp.concatenate(
        [
            jnp.sum(grad_query_lowered.astype(jnp.float32), axis=0),
            jnp.sum(grad_value_lowered.astype(jnp.float32), axis=0),
        ]
    )
    d_normed1 = jnp.einsum(
        "ne,de->nd", grad_query_key_value, weight_qkv, preferred_element_type=jnp.float32
    )
    norm_pull1 = jax.vjp(layer_norm, inputs, gain_f1, shift_f1)[1]
    d_innorm, grad_gain1, grad_shift1 = norm_pull1(d_normed1)
    grad_tokens = (d_hidden + d_innorm).reshape(row_count, blk_len, hidden_width)
    attn_grads = (
        lax.psum_scatter(grad_gain1, ("rows", "seq"), scatter_dimension=0, tiled=True),
        lax.psum_scatter(grad_shift1, ("rows", "seq"), scatter_dimension=0, tiled=True),
        lax.psum_scatter(grad_wqkv, ("rows", "seq"), scatter_dimension=0, tiled=True),
        lax.psum_scatter(grad_bqv, ("rows", "seq"), scatter_dimension=0, tiled=True),
        lax.psum_scatter(grad_wout, ("rows", "seq"), scatter_dimension=0, tiled=True),
        lax.psum_scatter(grad_bout, ("rows", "seq"), scatter_dimension=0, tiled=True),
    )
    return (
        out,
        grad_tokens,
        attn_grads[0],
        attn_grads[1],
        attn_grads[2],
        attn_grads[3],
        attn_grads[4],
        attn_grads[5],
        mlp_grads[0],
        mlp_grads[1],
        mlp_grads[2],
        mlp_grads[3],
        mlp_grads[4],
        mlp_grads[5],
    )


def local(
    tokens,
    grad_out,
    lengths,
    ln1_gain,
    ln1_bias,
    w_qkv,
    b_qv,
    w_out,
    b_out,
    ln2_gain,
    ln2_bias,
    w_up,
    b_up,
    w_down,
    b_down,
):
    return block_plan(
        tokens,
        grad_out,
        lengths,
        ln1_gain,
        ln1_bias,
        w_qkv,
        b_qv,
        w_out,
        b_out,
        ln2_gain,
        ln2_bias,
        w_up,
        b_up,
        w_down,
        b_down,
    )


def solution(mesh):
    in_specs = (
        P("rows", "seq", None),
        P("rows", "seq", None),
        P("rows", None),
        P(("rows", "seq")),
        P(("rows", "seq")),
        P(("rows", "seq"), None),
        P(("rows", "seq")),
        P(("rows", "seq"), None),
        P(("rows", "seq")),
        P(("rows", "seq")),
        P(("rows", "seq")),
        P(("rows", "seq"), None),
        P(("rows", "seq")),
        P(("rows", "seq"), None),
        P(("rows", "seq")),
    )
    out_specs = (
        P("rows", "seq", None),
        P("rows", "seq", None),
        P(("rows", "seq")),
        P(("rows", "seq")),
        P(("rows", "seq"), None),
        P(("rows", "seq")),
        P(("rows", "seq"), None),
        P(("rows", "seq")),
        P(("rows", "seq")),
        P(("rows", "seq")),
        P(("rows", "seq"), None),
        P(("rows", "seq")),
        P(("rows", "seq"), None),
        P(("rows", "seq")),
    )
    return jax.shard_map(local, mesh=mesh, in_specs=in_specs, out_specs=out_specs, check_vma=False)
```

profile of v0, /device:TPU:1, one launch (start us, length us, event | category | flops | bytes accessed | tf_op | source)
XLA Modules:
  0.0 3316.8 jit_solution(8910368475781295104)
XLA Ops:
  16.8 71.1 %all-reduce.17 = (bf16[4096]{0:T(1024)(128)(2,1)S(1)}, bf16[2048]{0:T(1024)(128)(2,1)S(1)}, bf16[2048]{0:T(1024)(128)(2,1)S(1)}, bf16[2048]{0:T(1024)(128)(2,1)S...) all-reduce(bf16[4096]{0:T(1024)(128)(2,1)S(1)} %dynamic-update-slic, ...), channel_id=1, replica_groups=mesh['rows'=8,'seq'=16] {'rows','seq'}, use_global_device_ids=true, to_apply=%add.2 | all-reduce | flops 24576 | bytes 98304
  89.1 1.3 fusion.36
  90.5 18.4 all-gather.5.cloned.1.call-done
  108.8 11.9 fusion
  121.0 3.2 collective-permute-start.1
  124.2 5.5 collective-permute-start
  131.3 15.6 collective-permute-done.1
  146.9 24.6 collective-permute-done
  171.4 1.4 pad_maximum_fusion.1
  173.2 1.6 copy.56
  174.8 1.6 copy.54
  176.4 2.5 fusion.11
  180.0 2.3 fusion.27
  182.3 24.2 all-gather.7.cloned.1.call-done
  206.4 4.9 fusion.71
  212.6 101.2 %all-gather.9.cloned.1.call-done = bf16[2048,8192]{1,0:T(8,128)(2,1)} async-done(((bf16[16,8192]{1,0:T(8,128)(2,1)}), bf16[2048,8192]{1,0:T(8,128)(2,1)}) %all-gather.9.cloned.1.call-update) | async-done | bytes 33554448 | tf_op jit(solution)/shard_map/all_gather | solution.py:133
  313.8 17.5 convolution_add_fusion
  331.3 91.6 %all-gather.11.cloned.1.call-done = bf16[8192,2048]{1,0:T(8,128)(2,1)} async-done(((bf16[64,2048]{1,0:T(8,128)(2,1)}), bf16[8192,2048]{1,0:T(8,128)(2,1)}) %all-gather.11.cloned.1.call-update) | async-done | bytes 33554448 | tf_op jit(solution)/shard_map/all_gather | solution.py:135
  422.9 27.1 convert_reduce_fusion
  450.1 19.9 multiply_reduce_fusion.1
  470.0 1.9 fusion.67
  472.9 1.9 convert_reduce_fusion.3
  475.6 7.1 convolution_convert_fusion
  482.7 2.0 copy.55
  484.8 3.5 multiply_reduce_fusion
  491.7 1.4 collective-permute-start.3
  493.1 1.3 collective-permute-start.2
  495.3 24.4 collective-permute-done.3
  521.0 21.4 fusion.65
  542.4 2.4 fusion.35
  544.8 3.6 convert_reduce_fusion.1
  549.0 8.1 fusion.72
  558.4 21.0 fusion.39
  581.3 23.3 fusion.64
  605.6 29.1 fusion.41
  635.4 20.5 fusion.12
  655.9 56.6 %all-reduce.20.cloned.1.call-done = (f32[2048]{0:T(1024)}, f32[2048]{0:T(1024)}, f32[4096]{0:T(1024)}, f32[2048]{0:T(1024)}, f32[2048]{0:T(1024)}, /*index=5*/f32[2048]{0:T(1024)}, f32[8192]{0:T(1024)}, f32[2048]{0:T(1024)}) async-done(((f32[2048]{0:T(1024)}, f32[2048]{0:T(1024)}, f32[4096]{0:T(1024)}, f32[2048]{0:T(1024)}, f32[2048]{0:T(1024)}, /*index=5*/f32[2048]{0:T(1024)}, f32[8192]{0:T(1024)}, ...) | async-done | bytes 98320
  712.5 1.3 dynamic-slice
  715.0 1.3 dynamic-slice.3
  716.3 1.3 dynamic-slice.4
  717.5 1.3 dynamic-slice.5
  718.8 1.3 dynamic-slice.7
  720.0 1.3 dynamic-slice.2
  721.3 1.3 dynamic-slice.6
  722.5 637.2 %reduce-scatter.7.cloned.1.call-done = f32[16,2048]{1,0:T(8,128)} async-done(((f32[2048,2048]{1,0:T(8,128)}), f32[16,2048]{1,0:T(8,128)}) %reduce-scatter.7.cloned.1.call-update) | async-done | bytes 131088 | tf_op jit(solution)/shard_map/reduce_scatter | solution.py:250
  1359.8 341.0 %reduce-scatter.5.cloned.1.call-done = f32[16,6144]{1,0:T(8,128)} async-done(((f32[2048,6144]{1,0:T(8,128)}), f32[16,6144]{1,0:T(8,128)}) %reduce-scatter.5.cloned.1.call-update) | async-done | bytes 393232 | tf_op jit(solution)/shard_map/reduce_scatter | solution.py:248
  1700.7 788.0 %reduce-scatter.9.cloned.1.call-done = f32[16,8192]{1,0:T(8,128)} async-done(((f32[2048,8192]{1,0:T(8,128)}), f32[16,8192]{1,0:T(8,128)}) %reduce-scatter.9.cloned.1.call-update) | async-done | bytes 524304 | tf_op jit(solution)/shard_map/reduce_scatter | solution.py:177
  2488.7 821.3 %reduce-scatter.11.cloned.1.call-done = f32[64,2048]{1,0:T(8,128)} async-done(((f32[8192,2048]{1,0:T(8,128)}), f32[64,2048]{1,0:T(8,128)}) %reduce-scatter.11.cloned.1.call-update) | async-done | bytes 524304 | tf_op jit(solution)/shard_map/reduce_scatter | solution.py:179
  (119 shorter events, 29.2 us)
Async XLA Ops:
  7.2 101.7 %all-gather.5.cloned.1.call-start = ((), (), s32[]{:S(2)}) async-start(), calls=%async_computation.4 | async-start | bytes 25362432 | tf_op jit(solution)/shard_map/all_gather | solution.py:73
  7.9 198.5 %all-gather.7.cloned.1.call-start = ((), (), s32[]{:S(2)}) async-start(), calls=%async_computation.5 | async-start | bytes 8454144 | tf_op jit(solution)/shard_map/all_gather | solution.py:75
  8.7 305.2 %all-gather.9.cloned.1.call-start = ((), (), s32[]{:S(2)}) async-start(), calls=%async_computation.6 | async-start | bytes 33816576 | tf_op jit(solution)/shard_map/all_gather | solution.py:133
  9.4 413.6 %all-gather.11.cloned.1.call-start = ((), (), s32[]{:S(2)}) async-start(), calls=%async_computation.7 | async-start | bytes 33816576 | tf_op jit(solution)/shard_map/all_gather | solution.py:135
  10.0 702.5 %all-reduce.20.cloned.1.call-start = ((), (), s32[]{:S(2)}) async-start(), calls=%async_computation.12 | async-start | bytes 196608
  120.7 9.0 copy-start.19
  121.0 25.9 collective-permute-start.1
  124.2 47.3 %collective-permute-start = (bf16[2,1,128,2048]{3,2,0,1:T(8,128)(2,1)S(1)}, bf16[2,1,128,2048]{3,2,0,1:T(8,128)(2,1)}, u32[]{:S(2)}, u32[]{:S(2)}) collective-permute-start(bf16[2,1,128,2048]{3,2,0,1:T(8,128)(2,1)S(1)} %maximum_bitcast_fusion), channel_id=1, source_target_pairs={{0,2},{1,3},{2,4},{3,5},{4,6},{5,7},{6,8},{7,9},{8,10},{9,11},{10,... | collective-permute-start | bytes 3145736 | tf_op jit(solution)/shard_map/ppermute | solution.py:20
  176.4 3.6 copy-start.6
  211.4 1.0 copy-start
  472.0 1.0 copy-start.4
  474.8 0.8 copy-start.8
  484.8 3.5 copy-start.11
  489.2 1.1 copy-start.10
  491.3 3.1 copy-start.7
  491.7 28.0 collective-permute-start.3
  493.1 26.6 collective-permute-start.2
  495.3 25.1 copy-start.16
  495.3 25.7 copy-start.2
  520.2 0.8 copy-start.13
  521.0 23.8 copy-start.5
  542.3 6.7 copy-start.9
  542.3 6.7 copy-start.12
  549.0 810.8 %reduce-scatter.7.cloned.1.call-start = ((), (), s32[]{:S(2)}) async-start(), calls=%async_computation.9 | async-start | bytes 16908288 | tf_op jit(solution)/shard_map/reduce_scatter | solution.py:250
  557.2 1.0 copy-start.14
  557.2 1.2 copy-start.17
  557.2 1143.6 %reduce-scatter.5.cloned.1.call-start = ((), (), s32[]{:S(2)}) async-start(), calls=%async_computation.8 | async-start | bytes 50724864 | tf_op jit(solution)/shard_map/reduce_scatter | solution.py:248
  579.3 1.2 copy-start.1
  579.3 1.9 copy-start.3
  579.4 1909.4 %reduce-scatter.9.cloned.1.call-start = ((), (), s32[]{:S(2)}) async-start(), calls=%async_computation.10 | async-start | bytes 67633152 | tf_op jit(solution)/shard_map/reduce_scatter | solution.py:177
  604.5 1.0 copy-start.15
  604.6 2705.5 %reduce-scatter.11.cloned.1.call-start = ((), (), s32[]{:S(2)}) async-start(), calls=%async_computation.11 | async-start | bytes 67633152 | tf_op jit(solution)/shard_map/reduce_scatter | solution.py:179
  634.7 0.7 copy-start.18
Sparse Core Ops, SparseCore 0:
  11.1 97.7 all-gather.4
  112.0 94.3 all-gather.6
  209.6 104.2 all-gather.8
  316.8 106.0 all-gather.10
  549.1 163.3 all-reduce.19
  715.4 644.3 reduce-scatter.6
  1366.7 334.0 reduce-scatter.4
  1703.8 784.8 reduce-scatter.8
  2491.9 818.1 reduce-scatter.10
where the time goes:
time: 3360 us; the launch traced here: 3320 us
  waiting for transfers between devices  2950 us (88%)
  matrix products  222 us (7%)
  blocking collectives  71.1 us (2%)
    reduce_scatter x1, waiting for transfers between devices, block_plan(): lax.psum_scatter(grad_wdown, ('rows', 'seq'), scatter_dimension=0, tiled=...  821 us
    reduce_scatter x1, waiting for transfers between devices, block_plan(): lax.psum_scatter(grad_wup, ('rows', 'seq'), scatter_dimension=0, tiled=True)  788 us
    reduce_scatter x1, waiting for transfers between devices, block_plan(): lax.psum_scatter(grad_wout, ('rows', 'seq'), scatter_dimension=0, tiled=T...  637 us
    reduce_scatter x1, waiting for transfers between devices, block_plan(): lax.psum_scatter(grad_wqkv, ('rows', 'seq'), scatter_dimension=0, tiled=T...  341 us
    all_gather x1, waiting for transfers between devices, block_plan(): lax.all_gather(w_up, ('rows', 'seq'), axis=0, tiled=True)  101 us
    all_gather x1, waiting for transfers between devices, block_plan(): lax.all_gather(w_down, ('rows', 'seq'), axis=0, tiled=True)  91.6 us
    unnamed x1, blocking collectives  71.1 us
  transfers between devices with their start and end apart: 13, of which 12 were waited for; matrix products, arithmetic and copies ran while one was open for 5% of the time, Pallas kernels for 0%

commit v1 on v0

v1 whole, which is shorter than its diff:
```python
import functools
import math

import jax
import jax.numpy as jnp
from jax import lax
from jax.experimental import pallas as pl
from jax.experimental.pallas import tpu as pltpu
from jax.sharding import Mesh, PartitionSpec as P

HEADS = 16
HEAD = 128
W = 256
EPSILON = 1e-05
NEG_FILL = -1e30

AXES = ("y", "core", "z", "x")
SIZE = {"y": 4, "core": 2, "z": 4, "x": 4}
BF = jnp.bfloat16
F32 = jnp.float32
SEMS = 96


def coords():
    return {a: lax.axis_index(a) for a in AXES}


def peer(**delta):
    me = coords()
    return tuple(lax.rem(me[a] + delta.get(a, 0) % SIZE[a], SIZE[a]) for a in AXES)


class Comm:
    def __init__(self, send_sem, recv_sem):
        self.send_sem, self.recv_sem = send_sem, recv_sem
        self.count, self.open = 0, []

    def push(self, src, dst, to):
        copy = pltpu.make_async_remote_copy(
            src_ref=src,
            dst_ref=dst,
            send_sem=self.send_sem.at[self.count],
            recv_sem=self.recv_sem.at[self.count],
            device_id=to,
            device_id_type=pl.DeviceIdType.MESH,
        )
        self.count += 1
        copy.start()
        self.open.append([copy, True, True])
        return self.open[-1]

    def local(self, src, dst):
        copy = pltpu.make_async_copy(src, dst, self.send_sem.at[self.count])
        self.count += 1
        copy.start()
        self.open.append([copy, False, True])
        return self.open[-1]

    def arrived(self, entries):
        for entry in entries:
            if entry[2]:
                if entry[1]:
                    entry[0].wait_recv()
                else:
                    entry[0].wait()
                entry[2] = False

    def drain(self):
        self.arrived(self.open)
        for copy, remote, _ in self.open:
            if remote:
                copy.wait_send()


def greet(devices):
    barrier = pltpu.get_barrier_semaphore()
    for device in devices:
        pl.semaphore_signal(barrier, inc=1, device_id=device, device_id_type=pl.DeviceIdType.MESH)
    pl.semaphore_wait(barrier, len(devices))


def exchange(name, collective_id, body, peers, ins, outs):
    def kernel(*refs):
        in_refs = refs[: len(ins)]
        out_refs = refs[len(ins) : len(ins) + len(outs)]
        comm = Comm(*refs[len(ins) + len(outs) :])
        greet(peers())
        body(comm, in_refs, out_refs)
        comm.drain()

    return pl.pallas_call(
        kernel,
        out_shape=tuple(jax.ShapeDtypeStruct(s, d) for s, d in outs),
        in_specs=[pl.BlockSpec(memory_space=pl.ANY)] * len(ins),
        out_specs=tuple(pl.BlockSpec(memory_space=pl.ANY) for _ in outs),
        scratch_shapes=[pltpu.SemaphoreType.DMA((SEMS,)), pltpu.SemaphoreType.DMA((SEMS,))],
        compiler_params=pltpu.CompilerParams(collective_id=collective_id, has_side_effects=True),
        name=name,
    )(*ins)


def ring(axis):
    return [peer(**{axis: k}) for k in (1, 3, 2)]


def near():
    return [peer(core=1)]


def scattered():
    me = coords()
    return (lax.rem(me["z"] + 1, 4), me["core"], me["x"], me["y"])


def collected():
    me = coords()
    return (me["x"], me["core"], lax.rem(me["y"] + 3, 4), me["z"])


def spread_x(comm, src, dst):
    x = lax.axis_index("x")
    sent = [comm.push(src, dst.at[x], to) for to in ring("x")]
    return sent + [comm.local(src, dst.at[x])]


def split_x(comm, src, dst):
    x = lax.axis_index("x")
    return [
        comm.push(src.at[lax.rem(x + k, 4)], dst.at[k - 1], peer(x=k)) for k in (1, 3, 2)
    ]


def halves(rows, cols):
    every = slice(None)
    if rows >= 32:
        return [(slice(0, rows // 2), every), (slice(rows // 2, rows), every)]
    return [(every, slice(0, cols // 2)), (every, slice(cols // 2, cols))]


class Gather:
    def __init__(self, comm, w, by_core):
        self.comm, self.w, self.by_core = comm, w, by_core
        self.cut = halves(*w.shape[3:])

    def at(self, y, core, z, half):
        slot = (core, y, z) if self.by_core else (y, core, z)
        return self.w.at[slot + self.cut[half]]

    def place(self):
        me = coords()
        y = lax.rem(me["y"] + 3, 4) if self.by_core else me["y"]
        return y, me["core"], me["z"]

    def first(self):
        y, c, z = self.place()
        a, b = self.at(y, c, z, 0), self.at(y, c, z, 1)
        self.a = [self.comm.push(a, a, to) for to in ring("z")]
        self.b = [self.comm.push(b, b, to) for to in ring("y")]

    def second(self):
        y, c, z = self.place()
        every = slice(None)
        self.comm.arrived(self.a)
        a = self.at(y, c, every, 0)
        self.a2 = [self.comm.push(a, a, to) for to in ring("y")]
        self.comm.arrived(self.b)
        b = self.at(every, c, z, 1)
        self.b2 = [self.comm.push(b, b, to) for to in ring("z")]

    def third(self):
        _, c, _ = self.place()
        every = slice(None)
        self.comm.arrived(self.a2)
        a = self.at(every, c, every, 0)
        self.comm.push(a, a, peer(core=1))
        self.comm.arrived(self.b2)
        b = self.at(every, c, every, 1)
        self.comm.push(b, b, peer(core=1))


def gather_peers():
    return ring("x") + ring("y") + ring("z") + near()


def into_slot(comm, src, w):
    me = coords()
    slot = w.at[me["y"], me["core"], me["z"], pl.ds(me["x"] * 16, 16)]
    sent = [
        comm.push(src.at[lax.rem(me["x"] + k, 4)], slot, peer(x=k)) for k in (1, 3, 2)
    ]
    return sent + [comm.local(src.at[me["x"]], slot)]


def into_scattered(comm, src, w):
    me = coords()
    return [comm.push(src, w.at[me["core"], me["z"], me["x"]], scattered())]


def swap_cores(comm, g, dst, by_core):
    other = 1 - lax.axis_index("core")
    src = g.at[other] if by_core else g.at[:, other]
    return [comm.push(src, dst, peer(core=1))]


def reduce_first(comm, s, dst_a, dst_b, by_core):
    y, z = lax.axis_index("y"), lax.axis_index("z")
    cut = halves(*s.shape[2:])
    for k in (1, 3, 2):
        to = lax.rem(z + k, 4)
        comm.push(s.at[(slice(None), to) + cut[0]], dst_a.at[k - 1], peer(z=k))
    for k in (1, 3, 2):
        to = lax.rem(y + k + (3 if by_core else 0), 4)
        comm.push(s.at[(to, slice(None)) + cut[1]], dst_b.at[k - 1], peer(y=k))


def reduce_second(comm, sa, sb, dst_a, dst_b, by_core):
    y, z = lax.axis_index("y"), lax.axis_index("z")
    for k in (1, 3, 2):
        to = lax.rem(y + k + (3 if by_core else 0), 4)
        comm.push(sa.at[to], dst_a.at[k - 1], peer(y=k))
    for k in (1, 3, 2):
        comm.push(sb.at[lax.rem(z + k, 4)], dst_b.at[k - 1], peer(z=k))


def pick(array, index, axis=0):
    return lax.dynamic_index_in_dim(array, index, axis, keepdims=False)


def after_cores(g, received, by_core):
    own = pick(g, lax.axis_index("core"), 0 if by_core else 1)
    return (own.astype(F32) + received.astype(F32)).astype(BF)


def slot_y(by_core):
    y = lax.axis_index("y")
    return lax.rem(y + 3, 4) if by_core else y


def after_first(s, ra, rb, by_core):
    every = slice(None)
    cut = halves(*s.shape[2:])
    own_a = pick(s[(every, every) + cut[0]], lax.axis_index("z"), 1).astype(F32)
    own_b = pick(s[(every, every) + cut[1]], slot_y(by_core), 0).astype(F32)
    return (
        (own_a + ra.astype(F32).sum(0)).astype(BF),
        (own_b + rb.astype(F32).sum(0)).astype(BF),
    )


def after_second(sa, sb, ra, rb, by_core):
    own_a = pick(sa, slot_y(by_core)).astype(F32)
    own_b = pick(sb, lax.axis_index("z")).astype(F32)
    return jnp.concatenate(
        [own_a + ra.astype(F32).sum(0), own_b + rb.astype(F32).sum(0)],
        axis=0 if sa.shape[1] == 32 else 1,
    ).astype(BF)


def layer_norm(values, gain, shift):
    center = jnp.mean(values, axis=-1, keepdims=True)
    centred = values - center
    spread = jnp.mean(centred * centred, axis=-1, keepdims=True)
    return centred * lax.rsqrt(spread + EPSILON) * gain + shift


def gelu_exact(values):
    return jax.nn.gelu(values, approximate=False)


def doc_number(positions, doc_ends):
    return jnp.sum((doc_ends[None, :] <= positions[:, None]).astype(jnp.int32), axis=1)


def dot(a, b, dims):
    return lax.dot_general(a, b, (dims, ((), ())), preferred_element_type=F32)


NN = ((1,), (0,))
NT = ((1,), (1,))
TN = ((0,), (0,))


def local(
    tokens,
    grad_out,
    lengths,
    ln1_gain,
    ln1_bias,
    w_qkv,
    b_qv,
    w_out,
    b_out,
    ln2_gain,
    ln2_bias,
    w_up,
    b_up,
    w_down,
    b_down,
):
    blk, width = tokens.shape[1:]
    span = 4 * blk
    part = width // 4
    hidden = w_up.shape[1] // 4
    heads = HEADS // 4
    x_at, z_at = lax.axis_index("x"), lax.axis_index("z")
    scale = 1.0 / math.sqrt(HEAD)

    tok = tokens.reshape(blk, width)
    dy = grad_out.reshape(blk, width)
    small = jnp.concatenate([ln1_gain, ln1_bias, b_qv, b_out, ln2_gain, ln2_bias, b_up, b_down])
    small = jnp.pad(small.astype(F32), (0, 1024 - small.shape[0])).reshape(8, 128)
    qkv_parts = w_qkv.reshape(16, 3, 4, part).transpose(2, 0, 1, 3).reshape(4, 16, 3 * part)
    up_parts = w_up.reshape(16, 4, hidden).transpose(1, 0, 2)

    def first_body(comm, ins, outs):
        tok_r, dy_r, small_r, qkv_r, out_r = ins
        tok_g, small_g, dy_g, wq, wo = outs
        me = coords()
        slot = into_slot(comm, qkv_r, wq)
        spot = into_scattered(comm, out_r, wo)
        at = (me["y"], me["core"], me["z"])
        s0 = [comm.push(small_r, small_g.at[at + (me["x"],)], to) for to in ring("x")]
        s0.append(comm.local(small_r, small_g.at[at + (me["x"],)]))
        spread_x(comm, tok_r, tok_g)
        q, o = Gather(comm, wq, False), Gather(comm, wo, True)
        comm.arrived(slot)
        q.first()
        comm.arrived(s0)
        mine = small_g.at[at]
        s1 = [comm.push(mine, mine, to) for to in ring("z")]
        comm.arrived(spot)
        o.first()
        spread_x(comm, dy_r, dy_g)
        comm.arrived(s1)
        mine = small_g.at[me["y"], me["core"]]
        s2 = [comm.push(mine, mine, to) for to in ring("y")]
        q.second()
        o.second()
        comm.arrived(s2)
        mine = small_g.at[:, me["core"]]
        comm.push(mine, mine, peer(core=1))
        q.third()
        o.third()

    tok_g, small_g, dy_g, wqkv_g, wout_g = exchange(
        "gather_attn",
        0,
        first_body,
        lambda: gather_peers() + [scattered(), collected()],
        [tok, dy, small, qkv_parts, w_out],
        [
            ((4, blk, width), BF),
            ((4, 2, 4, 4, 8, 128), F32),
            ((4, blk, width), BF),
            ((4, 2, 4, 64, 3 * part), BF),
            ((2, 4, 4, 16, width), BF),
        ],
    )
    small_g = small_g.reshape(128, 1024)
    vectors, start = [], 0
    for size in (16, 16, 32, 16, 16, 16, 64, 16):
        vectors.append(small_g[:, start : start + size].reshape(128 * size))
        start += size
    gain1, shift1, bias_qv, bias_out, gain2, shift2, bias_up, bias_down = vectors
    weight_qkv = wqkv_g.reshape(width, 3 * part)
    weight_out = wout_g.reshape(part, width)
    dy_all = dy_g.reshape(span, width)

    inputs = tok_g.reshape(span, width).astype(F32)
    normed1 = layer_norm(inputs, gain1, shift1).astype(BF)
    bias_q = lax.dynamic_slice_in_dim(bias_qv, x_at * part, part)
    bias_v = lax.dynamic_slice_in_dim(bias_qv, width + x_at * part, part)
    bias_full = jnp.concatenate([bias_q, jnp.zeros((part,), F32), bias_v])
    projected = (dot(normed1, weight_qkv, NN) + bias_full).astype(BF)

    def second_body(comm, ins, outs):
        p_r, up_r, down_r = ins
        edge, wu, wd = outs
        comm.push(p_r.at[pl.ds(span - W, W), pl.ds(part, 2 * part)], edge, peer(z=1))
        slot = into_slot(comm, up_r, wu)
        spot = into_scattered(comm, down_r, wd)
        u = Gather(comm, wu, False)
        comm.arrived(slot)
        u.first()
        comm.arrived(spot)
        u.second()
        u.third()

    edge_kv, wup_g, wdown_s = exchange(
        "edge_and_up",
        1,
        second_body,
        lambda: gather_peers() + [scattered(), collected()],
        [projected, up_parts, w_down],
        [
            ((W, 2 * part), BF),
            ((4, 2, 4, 64, hidden), BF),
            ((2, 4, 4, 64, width), BF),
        ],
    )

    row_ends = jnp.cumsum(lengths.reshape(-1))
    q_pos = z_at * span + jnp.arange(span, dtype=jnp.int32)
    k_pos = z_at * span - W + jnp.arange(span + W, dtype=jnp.int32)
    q_doc, k_doc = doc_number(q_pos, row_ends), doc_number(k_pos, row_ends)
    reach = W + blk

    def windows(array):
        return jnp.stack([array[b * blk : b * blk + reach] for b in range(4)])

    qp, qd = q_pos.reshape(4, blk, 1), q_doc.reshape(4, blk, 1)
    kp, kd = windows(k_pos)[:, None, :], windows(k_doc)[:, None, :]
    visible = (qd == kd) & (kp <= qp) & (qp - kp < W) & (kp >= 0)

    keys = jnp.concatenate([edge_kv[:, :part], projected[:, part : 2 * part]])
    values = jnp.concatenate([edge_kv[:, part:], projected[:, 2 * part :]])
    q_heads = projected[:, :part].reshape(4, blk, heads, HEAD)
    k_heads = windows(keys).reshape(4, reach, heads, HEAD)
    v_heads = windows(values).reshape(4, reach, heads, HEAD)
    scores = jnp.einsum("bqhd,bkhd->bhqk", q_heads, k_heads, preferred_element_type=F32) * scale
    masked = jnp.where(visible[:, None], scores, NEG_FILL)
    peak = jnp.max(masked, axis=-1, keepdims=True)
    log_total = peak + jnp.log(jnp.sum(jnp.exp(masked - peak), axis=-1, keepdims=True))
    probs = jnp.exp(masked - log_total)
    probs_low = probs.astype(BF)
    mixed = jnp.einsum("bhqk,bkhd->bqhd", probs_low, v_heads, preferred_element_type=F32)
    mixed = mixed.reshape(span, part).astype(BF)
    attn_part = dot(mixed, weight_out, NN).reshape(4, blk, width)

    def third_body(comm, ins, outs):
        part_r, wd_in = ins
        got, wd = outs
        me = coords()
        split_x(comm, part_r, got)
        slot = (me["core"], lax.rem(me["y"] + 3, 4), me["z"])
        comm.arrived([comm.local(wd_in.at[slot], wd.at[slot])])
        d = Gather(comm, wd, True)
        d.first()
        d.second()
        d.third()

    attn_got, wdown_g = exchange(
        "sum_attn_and_down",
        2,
        third_body,
        gather_peers,
        [attn_part.astype(BF), wdown_s],
        [((3, blk, width), BF), ((2, 4, 4, 64, width), BF)],
    )
    weight_up = wup_g.reshape(width, hidden)
    weight_down = wdown_g.reshape(hidden, width)

    own_tok = tok.astype(F32)
    residual = own_tok + pick(attn_part, x_at) + attn_got.astype(F32).sum(0) + bias_out
    normed2 = layer_norm(residual, gain2, shift2).astype(BF)

    (normed2_g,) = exchange(
        "spread_a2",
        3,
        lambda comm, ins, outs: spread_x(comm, ins[0], outs[0]),
        lambda: ring("x"),
        [normed2],
        [((4, blk, width), BF)],
    )
    a2 = normed2_g.reshape(span, width)
    bias_up_own = lax.dynamic_slice_in_dim(bias_up, x_at * hidden, hidden)
    upper = dot(a2, weight_up, NN) + bias_up_own
    activated = gelu_exact(upper).astype(BF)
    d_act = dot(dy_all, weight_down, NT)
    d_upper = jax.vjp(gelu_exact, upper)[1](d_act)[0].astype(BF)
    d_a2_part = dot(d_upper, weight_up, NT).reshape(4, blk, width)
    out_part = dot(activated, weight_down, NN).reshape(4, blk, width)
    g_wdown = dot(activated, dy_all, TN).astype(BF).reshape(2, 4, 4, 64, width)
    g_wup = dot(a2, d_upper, TN).astype(BF).reshape(4, 2, 4, 64, hidden)
    g_bup = jnp.sum(d_upper.astype(F32), axis=0)

    def fifth_body(comm, ins, outs):
        split_x(comm, ins[0], outs[0])
        split_x(comm, ins[1], outs[1])
        swap_cores(comm, ins[2], outs[2], False)
        swap_cores(comm, ins[3], outs[3], True)

    d_a2_got, out_got, up_c, down_c = exchange(
        "sum_ff",
        4,
        fifth_body,
        lambda: ring("x") + near(),
        [d_a2_part.astype(BF), out_part.astype(BF), g_wup, g_wdown],
        [
            ((3, blk, width), BF),
            ((3, blk, width), BF),
            ((4, 4, 64, hidden), BF),
            ((4, 4, 64, width), BF),
        ],
    )
    out = residual + pick(out_part, x_at) + out_got.astype(F32).sum(0) + bias_down
    d_a2 = pick(d_a2_part, x_at) + d_a2_got.astype(F32).sum(0)
    d_resnorm, g_gain2, g_shift2 = jax.vjp(layer_norm, residual, gain2, shift2)[1](d_a2)
    d_hidden = dy.astype(F32) + d_resnorm
    d_attn_own = d_hidden.astype(BF)
    up_s, down_s = after_cores(g_wup, up_c, False), after_cores(g_wdown, down_c, True)

    def sixth_body(comm, ins, outs):
        spread_x(comm, ins[0], outs[0])
        reduce_first(comm, ins[1], outs[1], outs[2], False)
        reduce_first(comm, ins[2], outs[3], outs[4], True)

    d_attn_g, up_a, up_b, down_a, down_b = exchange(
        "spread_d_attn",
        5,
        sixth_body,
        lambda: ring("x") + ring("y") + ring("z"),
        [d_attn_own, up_s, down_s],
        [
            ((4, blk, width), BF),
            ((3, 4, 32, hidden), BF),
            ((3, 4, 32, hidden), BF),
            ((3, 4, 32, width), BF),
            ((3, 4, 32, width), BF),
        ],
    )
    d_attn = d_attn_g.reshape(span, width)
    d_mixed = dot(d_attn, weight_out, NT).astype(BF)
    d_heads = d_mixed.reshape(4, blk, heads, HEAD)
    d_probs = jnp.einsum("bqhd,bkhd->bhqk", d_heads, v_heads, preferred_element_type=F32)
    d_score = (probs * (d_probs - jnp.sum(d_probs * probs, axis=-1, keepdims=True))).astype(BF)
    d_query = jnp.einsum("bhqk,bkhd->bqhd", d_score, k_heads, preferred_element_type=F32) * scale
    d_kwin = jnp.einsum("bhqk,bqhd->bkhd", d_score, q_heads, preferred_element_type=F32) * scale
    d_vwin = jnp.einsum("bhqk,bqhd->bkhd", probs_low, d_heads, preferred_element_type=F32)

    def unwindow(array):
        array = array.reshape(4, reach, part)
        total = jnp.zeros((span + W, part), F32)
        for b in range(4):
            total = total + jnp.pad(array[b], ((b * blk, span + W - b * blk - reach), (0, 0)))
        return total

    d_keys, d_values = unwindow(d_kwin), unwindow(d_vwin)
    d_edge = jnp.concatenate([d_keys[:W], d_values[:W]], axis=1).astype(BF)
    up_sa, up_sb = after_first(up_s, up_a, up_b, False)
    down_sa, down_sb = after_first(down_s, down_a, down_b, True)

    def seventh_body(comm, ins, outs):
        comm.push(ins[0], outs[0], peer(z=3))
        reduce_second(comm, ins[1], ins[2], outs[1], outs[2], False)
        reduce_second(comm, ins[3], ins[4], outs[3], outs[4], True)

    d_edge_got, up_a2, up_b2, down_a2, down_b2 = exchange(
        "edge_back",
        6,
        seventh_body,
        lambda: ring("y") + ring("z"),
        [d_edge, up_sa, up_sb, down_sa, down_sb],
        [
            ((W, 2 * part), BF),
            ((3, 32, hidden), BF),
            ((3, 32, hidden), BF),
            ((3, 32, width), BF),
            ((3, 32, width), BF),
        ],
    )
    up_f = after_second(up_sa, up_sb, up_a2, up_b2, False)
    down_f = after_second(down_sa, down_sb, down_a2, down_b2, True)
    d_kv = jnp.concatenate([d_keys[W:], d_values[W:]], axis=1)
    d_kv = d_kv + jnp.pad(d_edge_got.astype(F32), ((span - W, 0), (0, 0)))
    d_qkv = jnp.concatenate([d_query.reshape(span, part), d_kv], axis=1).astype(BF)
    d_a1_part = dot(d_qkv, weight_qkv, NT).reshape(4, blk, width)
    g_wqkv = dot(normed1, d_qkv, TN).astype(BF).reshape(4, 2, 4, 64, 3 * part)
    g_wout = dot(mixed, d_attn, TN).astype(BF).reshape(2, 4, 4, 16, width)
    g_bqkv = jnp.sum(d_qkv.astype(F32), axis=0)

    def eighth_body(comm, ins, outs):
        split_x(comm, ins[0], outs[0])
        swap_cores(comm, ins[1], outs[1], False)
        swap_cores(comm, ins[2], outs[2], True)
        split_x(comm, ins[3], outs[3])
        comm.push(ins[4], outs[4], collected())

    d_a1_got, qkv_c, wout_c, up_x, g_down_own = exchange(
        "sum_d_a1",
        7,
        eighth_body,
        lambda: ring("x") + near() + [scattered(), collected()],
        [d_a1_part.astype(BF), g_wqkv, g_wout, up_f.reshape(4, 16, hidden), down_f],
        [
            ((3, blk, width), BF),
            ((4, 4, 64, 3 * part), BF),
            ((4, 4, 16, width), BF),
            ((3, 16, hidden), BF),
            ((64, width), BF),
        ],
    )
    d_a1 = pick(d_a1_part, x_at) + d_a1_got.astype(F32).sum(0)
    d_in, g_gain1, g_shift1 = jax.vjp(layer_norm, own_tok, gain1, shift1)[1](d_a1)
    grad_tokens = d_hidden + d_in
    qkv_s, wout_s = after_cores(g_wqkv, qkv_c, False), after_cores(g_wout, wout_c, True)

    def placed(vector, offset, whole):
        return lax.dynamic_update_slice(jnp.zeros((whole,), F32), vector, (offset,))

    g_bqv = placed(g_bqkv[:part], x_at * part, 2 * width) + placed(
        g_bqkv[2 * part :], width + x_at * part, 2 * width
    )
    g_small = jnp.concatenate(
        [
            v.reshape(128, -1)
            for v in (
                g_gain1,
                g_shift1,
                g_bqv,
                jnp.sum(d_attn_own.astype(F32), axis=0),
                g_gain2,
                g_shift2,
                placed(g_bup, x_at * hidden, 4 * hidden),
                jnp.sum(dy.astype(F32), axis=0),
            )
        ],
        axis=1,
    )
    g_small = jnp.pad(g_small, ((0, 0), (0, 256 - g_small.shape[1]))).reshape(4, 2, 4, 8, 128)

    def ninth_body(comm, ins, outs):
        reduce_first(comm, ins[0], outs[0], outs[1], False)
        reduce_first(comm, ins[1], outs[2], outs[3], True)
        me = coords()
        for k in range(1, 8):
            c, zz = lax.rem(me["core"] + k // 4, 2), lax.rem(me["z"] + k % 4, 4)
            comm.push(ins[2].at[:, c, zz], outs[4].at[k - 1], (me["y"], c, zz, me["x"]))

    def across():
        me = coords()
        return [
            (me["y"], lax.rem(me["core"] + k // 4, 2), lax.rem(me["z"] + k % 4, 4), me["x"])
            for k in range(1, 8)
        ]

    qkv_a, qkv_b, wout_a, wout_b, small_a = exchange(
        "reduce_attn_1",
        8,
        ninth_body,
        lambda: ring("y") + across(),
        [qkv_s, wout_s, g_small],
        [
            ((3, 4, 32, 3 * part), BF),
            ((3, 4, 32, 3 * part), BF),
            ((3, 4, 16, width // 2), BF),
            ((3, 4, 16, width // 2), BF),
            ((7, 4, 8, 128), F32),
        ],
    )
    qkv_sa, qkv_sb = after_first(qkv_s, qkv_a, qkv_b, False)
    wout_sa, wout_sb = after_first(wout_s, wout_a, wout_b, True)
    small_s = pick(pick(g_small, lax.axis_index("core"), 1), z_at, 1) + small_a.sum(0)

    def tenth_body(comm, ins, outs):
        reduce_second(comm, ins[0], ins[1], outs[0], outs[1], False)
        reduce_second(comm, ins[2], ins[3], outs[2], outs[3], True)
        y = lax.axis_index("y")
        for k in (1, 3, 2):
            comm.push(ins[4].at[lax.rem(y + k, 4)], outs[4].at[k - 1], peer(y=k))

    qkv_a2, qkv_b2, wout_a2, wout_b2, small_b = exchange(
        "reduce_attn_2",
        9,
        tenth_body,
        lambda: ring("y") + ring("z"),
        [qkv_sa, qkv_sb, wout_sa, wout_sb, small_s],
        [
            ((3, 32, 3 * part), BF),
            ((3, 32, 3 * part), BF),
            ((3, 16, width // 2), BF),
            ((3, 16, width // 2), BF),
            ((3, 8, 128), F32),
        ],
    )
    qkv_f = after_second(qkv_sa, qkv_sb, qkv_a2, qkv_b2, False)
    wout_f = after_second(wout_sa, wout_sb, wout_a2, wout_b2, True)
    small_f = pick(small_s, lax.axis_index("y")) + small_b.sum(0)

    def last_body(comm, ins, outs):
        split_x(comm, ins[0], outs[0])
        comm.push(ins[1], outs[1], collected())
        for k in (1, 3, 2):
            comm.push(ins[2], outs[2].at[k - 1], peer(x=k))

    qkv_x, g_out_own, small_x = exchange(
        "hand_back",
        10,
        last_body,
        lambda: ring("x") + [scattered(), collected()],
        [qkv_f.reshape(4, 16, 3 * part), wout_f, small_f],
        [((3, 16, 3 * part), BF), ((16, width), BF), ((3, 8, 128), F32)],
    )

    def columns(own, received, groups):
        every = jnp.concatenate([received, pick(own, x_at)[None]])
        order = jnp.stack([lax.rem(x_at - s + 7, 4) for s in range(4)])
        every = jnp.take(every, order, axis=0).reshape(4, 16, groups, -1)
        return every.transpose(1, 2, 0, 3).reshape(16, -1).astype(F32)

    g_qkv_own = columns(qkv_f.reshape(4, 16, 3 * part), qkv_x, 3)
    g_up_own = columns(up_f.reshape(4, 16, hidden), up_x, 1)
    small_all = (small_f + small_x.sum(0)).reshape(4, 256)
    mine = pick(small_all, x_at)
    cuts, start = [], 0
    for size in (16, 16, 32, 16, 16, 16, 64, 16):
        cuts.append(mine[start : start + size])
        start += size
    return (
        out.astype(BF).reshape(1, blk, width),
        grad_tokens.reshape(1, blk, width),
        cuts[0],
        cuts[1],
        g_qkv_own,
        cuts[2],
        g_out_own.astype(F32),
        cuts[3],
        cuts[4],
        cuts[5],
        g_up_own,
        cuts[6],
        g_down_own.astype(F32),
        cuts[7],
    )


def solution(mesh):
    fine = Mesh(mesh.devices.reshape(4, 2, 4, 4), AXES)
    rows, seq = ("y", "core"), ("z", "x")
    every = rows + seq
    token = P(rows, seq, None)
    vec, mat = P(every), P(every, None)
    in_specs = (token, token, P(rows, None), vec, vec, mat, vec, mat, vec, vec, vec, mat, vec, mat, vec)
    out_specs = (token, token, vec, vec, mat, vec, mat, vec, vec, vec, mat, vec, mat, vec)
    return jax.shard_map(local, mesh=fine, in_specs=in_specs, out_specs=out_specs, check_vma=False)
```

time: 3360 us -> 736 us (0.22)
  waiting for transfers between devices: 2950 us -> 0 us
  Pallas kernels: 0 us -> 436 us
  matrix products: 222 us -> 109 us
  other arithmetic: 18.3 us -> 101 us
  blocking collectives: 71.1 us -> 0 us
  local copies, waits for them, and re-layouts: 32 us -> 76.5 us
    reduce_scatter x4 -> x0, waiting for transfers between devices: 2590 us -> none  [the longest x1 821 us: block_plan(): lax.psum_scatter(grad_wdown, ('rows', 'seq'), scatter_dimension=0, tiled=...]
    pallas_call x0 -> x11, Pallas kernels: none -> 436 us  [exchange(): pl.pallas_call(kernel, out_shape=tuple((jax.ShapeDtypeStruct(s, d) for s,...]
    all_gather x4 -> x0, waiting for transfers between devices: 235 us -> none  [the longest x1 101 us: block_plan(): lax.all_gather(w_up, ('rows', 'seq'), axis=0, tiled=True)]
    dot_general x18, matrix products: 222 us -> 109 us  [the longest x12 97.4 us: dot(): return lax.dot_general(a, b, (dims, ((), ())), preferred_element_type=F32)]
    unnamed x1 -> x0, blocking collectives: 71.1 us -> none
    ppermute x4 -> x0, waiting for transfers between devices: 64.6 us -> none  [shifted(): return lax.ppermute(array, axis, pairs)]
    unnamed x10 -> x0, waiting for transfers between devices: 59.3 us -> none
    convert_element_type x9 -> x22, other arithmetic: 1.07 us -> 36.1 us  [the longest x4 12.8 us: after_cores(): return (own.astype(F32) + received.astype(F32)).astype(BF)]
  transfers between devices with their start and end apart: 13 -> 0, of which waited for: 12 -> 0; matrix products, arithmetic and copies ran while one was open for 5% -> 0% of each run, Pallas kernels for 0% -> 0%
where the time goes in v1:
time: 736 us; the launch traced here: 725 us
  Pallas kernels  436 us (59%)
  matrix products  109 us (15%)
  other arithmetic  101 us (14%)
  local copies, waits for them, and re-layouts  76.5 us (10%)
    pallas_call x11, Pallas kernels, exchange(): pl.pallas_call(kernel, out_shape=tuple((jax.ShapeDtypeStruct(s, d) for s,...  436 us
    dot_general x12, matrix products, dot(): return lax.dot_general(a, b, (dims, ((), ())), preferred_element_type=F32)  97.4 us

profile of v1, /device:TPU:1, one launch (start us, length us, event | category | flops | bytes accessed | tf_op | source)
XLA Modules:
  0.0 724.7 jit_solution(13429908898241168711)
XLA Ops:
  0.6 5.4 concatenate.83
  8.8 60.8 %gather_attn.1 = (bf16[4,128,2048]{2,1,0:T(8,128)(2,1)}, f32[4,2,4,4,8,128]{5,4,3,2,1,0:T(8,128)}, bf16[4,128,2048]{2,1,0:T(8,128)(2,1)}, bf16[4,2,4,64,1536]{4,...) custom-call(bf16[128,2048]{1,0:T(8,128)(2,1)} %bitcast.283, bf16[128,2048]{1,0:T(8,128)(2,1)} %bitcast.288, ...), custom_call_target="tpu_custom_call" | custom-call | tf_op jit(solution)/shard_map/gather_attn/pallas_call | solution.py:91
  75.2 2.2 add_convert_fusion.1
  77.6 6.8 fusion.13.refs_0_
  88.3 67.0 %edge_and_up.1 = (bf16[256,1024]{1,0:T(8,128)(2,1)}, bf16[4,2,4,64,2048]{4,3,2,1,0:T(8,128)(2,1)}, bf16[2,4,4,64,2048]{4,3,2,1,0:T(8,128)(2,1)}) custom-call(bf16[512,1536]{1,0:T(8,128)(2,1)} %copy-done.8, bf16[4,16,2048]{2,1,0:T(8,128)(2,1)} %bitcast.320, bf16[64,2048]{1,0:T(8,128)(2,1)} %refs_2_.1), custom_call_target="tpu_custom_call" | custom-call | tf_op jit(solution)/shard_map/edge_and_up/pallas_call | solution.py:91
  165.5 2.6 fusion.14
  169.3 2.4 convolution_convert_fusion.5
  171.8 4.0 fusion.103
  175.8 52.8 %sum_attn_and_down.1 = (bf16[3,128,2048]{2,1,0:T(8,128)(2,1)}, bf16[2,4,4,64,2048]{4,3,2,1,0:T(8,128)(2,1)}) custom-call(bf16[4,128,2048]{2,1,0:T(8,128)(2,1)} %get-tuple-element.182.refs_0_, bf16[2,4,4,64,2048]{4,3,2,1,0:T(8,128)(2,1)} %get-tuple-element.61.refs_1_), custom_call_target="tpu_custom_call" | custom-call | tf_op jit(solution)/shard_map/sum_attn_and_down/pallas_call | solution.py:91
  228.6 2.7 convert_reduce_fusion.10
  231.3 3.4 fusion.88
  237.6 2.3 add_convert_fusion.2.refs_0_
  239.9 28.3 %spread_a2.1 = bf16[4,128,2048]{2,1,0:T(8,128)(2,1)} custom-call(bf16[128,2048]{1,0:T(8,128)(2,1)} %add_convert_fusion.2.refs_0_), custom_call_target="tpu_custom_call" | custom-call | tf_op jit(solution)/shard_map/spread_a2/pallas_call | solution.py:91
  268.2 10.5 %fusion.107 = f32[512,2048]{1,0:T(8,128)} fusion(bf16[512,2048]{1,0:T(8,128)(2,1)} %bitcast.304, bf16[2048,2048]{1,0:T(8,128)(2,1)} %bitcast.344), kind=kOutput, calls=%fused_computation.276 | convolution fusion | flops 4294967296 | bytes 14680064 | tf_op jit(solution)/shard_map/dot_general | solution.py:275
  279.7 17.5 %convert_reduce_fusion = (f32[2048]{0:T(1024)}, bf16[512,2048]{1,0:T(8,128)(2,1)S(1)}, f32[512,2048]{1,0:T(8,128)S(1)}) fusion(f32[512,2048]{1,0:T(8,128)} %fusion.107, f32[2048]{0:T(1024)S(1)} %dynamic_slice.120, bf16[512,2048]{1,0:T(8,128)(2,1)} %bitcast.350, bf16[2048,2048]{1,0:T(8,128)(2,1)} %bitcast.346), kind=kOutput, calls=%fused_computation.19 | convolution fusion | flops 4373608448 | bytes 20987904 | tf_op jit(solution)/shard_map/dot_general | solution.py:275
  297.2 10.1 %fusion.104 = (bf16[4,128,2048]{2,1,0:T(8,128)(2,1)}, f32[4,128,2048]{2,1,0:T(8,128)}) fusion(bf16[4,128,2048]{2,1,0:T(8,128)(2,1)S(1)} %bitcast.355, bf16[2048,2048,1]{1,0,2:T(8,128)(2,1)} %bitcast.345), kind=kOutput, calls=%fused_computation.273 | convolution fusion | flops 4296015872 | bytes 16777216 | tf_op jit(solution)/shard_map/dot_general | solution.py:275
  308.4 10.0 %fusion.105 = (bf16[4,128,2048]{2,1,0:T(8,128)(2,1)}, f32[4,128,2048]{2,1,0:T(8,128)}) fusion(bf16[4,128,2048]{2,1,0:T(8,128)(2,1)S(1)} %bitcast.316, bf16[2048,2048,1]{1,0,2:T(8,128)(2,1)} %bitcast.347), kind=kOutput, calls=%fused_computation.274 | convolution fusion | flops 4296015872 | bytes 16777216 | tf_op jit(solution)/shard_map/dot_general | solution.py:275
  318.4 6.8 convolution_convert_fusion.2
  325.3 7.2 %convolution_convert_fusion.1 = bf16[2048,2048]{1,0:T(8,128)(2,1)} fusion(bf16[512,2048]{1,0:T(8,128)(2,1)S(1)} %multiply_convert_fusion, bf16[512,2048]{1,0:T(8,128)(2,1)S(1)} %bitcast.351), kind=kOutput, calls=%fused_computation.7 | convolution fusion | flops 4299161600 | bytes 12582912 | tf_op jit(solution)/shard_map/dot_general | solution.py:275
  332.5 50.0 %sum_ff.1 = (bf16[3,128,2048]{2,1,0:T(8,128)(2,1)}, bf16[3,128,2048]{2,1,0:T(8,128)(2,1)}, bf16[4,4,64,2048]{3,2,1,0:T(8,128)(2,1)}, bf16[4,4,64,2048]{3,2,1,0:T(8,128)(2,1)}) custom-call(bf16[4,128,2048]{2,1,0:T(8,128)(2,1)} %get-tuple-element.184.refs_0_, bf16[4,128,2048]{2,1,0:T(8,128)(2,1)} %get-tuple-element.186.refs_1_, ...), custom_call_target="tpu_custom_call" | custom-call | tf_op jit(solution)/shard_map/sum_ff/pallas_call | solution.py:91
  382.5 2.8 convert_reduce_fusion.9
  385.4 3.7 fusion.51
  389.4 2.7 multiply_reduce_fusion.2
  394.2 4.3 fusion.1
  398.5 2.3 copy.147.refs_1_
  403.6 6.1 fusion.refs_2_
  409.7 49.3 %spread_d_attn.1 = (bf16[4,128,2048]{2,1,0:T(8,128)(2,1)}, bf16[3,4,32,2048]{3,2,1,0:T(8,128)(2,1)}, bf16[3,4,32,2048]{3,2,1,0:T(8,128)(2,1)}, bf16[3,4,32,2048]{3,2,1,0:T(8,128)(2,1)}, bf16[3,4,32,2048]{3,2,1,0:T(8,128)(2,1)}) custom-call(bf16[128,2048]{1,0:T(8,128)(2,1)} %get-tuple-element.112.refs_0_, bf16[4,4,64,2048]{3,2,1,0:T(8,128)(2,1)} %copy.147.refs_1_, ...), custom_call_target="tpu_custom_call" | custom-call | tf_op jit(solution)/shard_map/spread_d_attn/pallas_call | solution.py:91
  459.0 4.3 convolution_convert_fusion.4
  471.1 2.3 copy.183
  473.4 2.3 copy.182
  475.7 2.3 copy.181
  478.0 2.3 copy.180
  480.3 2.3 pad_add_fusion
  494.5 2.1 pad_add_fusion.1
  501.3 2.1 fusion.45.refs_1_
  504.6 2.3 convert_reduce_fusion.5
  512.6 22.0 %edge_back.1 = (bf16[256,1024]{1,0:T(8,128)(2,1)}, bf16[3,32,2048]{2,1,0:T(8,128)(2,1)}, bf16[3,32,2048]{2,1,0:T(8,128)(2,1)}, bf16[3,32,2048]{2,1,0:T(8,128)(2,1)}, bf16[3,32,2048]{2,1,0:T(8,128)(2,1)}) custom-call(bf16[256,1024]{1,0:T(8,128)(2,1)} %pad_maximum_fusion.3.refs_0_, bf16[4,32,2048]{2,1,0:T(8,128)(2,1)} %fusion.45.refs_1_, ...), custom_call_target="tpu_custom_call" | custom-call | tf_op jit(solution)/shard_map/edge_back/pallas_call | solution.py:91
  534.6 2.6 fusion.15
  537.2 2.3 fusion.26
  539.8 8.3 %fusion.106 = (bf16[4,128,2048]{2,1,0:T(8,128)(2,1)}, f32[4,128,2048]{2,1,0:T(8,128)}) fusion(bf16[2048,1536,1]{1,0,2:T(8,128)(2,1)} %bitcast.349, bf16[4,128,1024]{2,1,0:T(8,128)(2,1)S(1)} %bitcast.293, bf16[4,128,512]{2,1,0:T(8,128)(2,1)S(1)} %copy.161), kind=kOutput, calls=%fused_computation.275 | convolution fusion | flops 3225419776 | bytes 14155776 | tf_op jit(solution)/shard_map/dot_general | solution.py:275
  548.1 2.1 fusion.7
  550.7 7.4 %convolution_convert_fusion = bf16[2048,1536]{1,0:T(8,128)(2,1)} fusion(bf16[512,2048]{1,0:T(8,128)(2,1)} %fusion.7, bf16[512,1024]{1,0:T(8,128)(2,1)S(1)} %copy-done.20, bf16[512,512]{1,0:T(8,128)(2,1)S(1)} %bitcast.309), kind=kOutput, calls=%fused_computation.6 | convolution fusion | flops 3227516928 | bytes 9961472 | tf_op jit(solution)/shard_map/dot_general | solution.py:275
  558.5 4.3 convolution_convert_fusion.3
  568.3 33.3 %sum_d_a1.1 = (bf16[3,128,2048]{2,1,0:T(8,128)(2,1)}, bf16[4,4,64,1536]{3,2,1,0:T(8,128)(2,1)}, bf16[4,4,16,2048]{3,2,1,0:T(8,128)(2,1)}, bf16[3,16,2048]{2,1,0:T(8,128)(2,1)}, bf16[64,2048]{1,0:T(8,128)(2,1)}) custom-call(bf16[4,128,2048]{2,1,0:T(8,128)(2,1)} %get-tuple-element.190.refs_0_, bf16[4,2,4,64,1536]{4,3,2,1,0:T(8,128)(2,1)} %bitcast.284, ...), custom_call_target="tpu_custom_call" | custom-call | tf_op jit(solution)/shard_map/sum_d_a1/pallas_call | solution.py:91
  605.9 3.9 fusion.39
  622.7 46.5 %reduce_attn_1.1 = (bf16[3,4,32,1536]{3,2,1,0:T(8,128)(2,1)}, bf16[3,4,32,1536]{3,2,1,0:T(8,128)(2,1)}, bf16[3,4,16,1024]{3,2,1,0:T(8,128)(2,1)}, bf16[3,4,16,1024]{3,2,1,0:T(8,128)(2,1)}, f32[7,4,8,128]{3,2,1,0:T(8,128)}) custom-call(bf16[4,4,64,1536]{3,2,1,0:T(8,128)(2,1)} %copy.166.refs_0_, bf16[4,4,16,2048]{3,2,1,0:T(8,128)(2,1)} %fusion.16.refs_1_, ...), custom_call_target="tpu_custom_call" | custom-call | tf_op jit(solution)/shard_map/reduce_attn_1/pallas_call | solution.py:91
  676.1 13.9 %reduce_attn_2.1 = (bf16[3,32,1536]{2,1,0:T(8,128)(2,1)}, bf16[3,32,1536]{2,1,0:T(8,128)(2,1)}, bf16[3,16,1024]{2,1,0:T(8,128)(2,1)}, bf16[3,16,1024]{2,1,0:T(8,128)(2,1)}, f32[3,8,128]{2,1,0:T(8,128)}) custom-call(bf16[4,32,1536]{2,1,0:T(8,128)(2,1)} %fusion.53.refs_0_, bf16[4,32,1536]{2,1,0:T(8,128)(2,1)} %fusion.52.refs_1_, ...), custom_call_target="tpu_custom_call" | custom-call | tf_op jit(solution)/shard_map/reduce_attn_2/pallas_call | solution.py:91
  700.7 12.4 %hand_back.1 = (bf16[3,16,1536]{2,1,0:T(8,128)(2,1)}, bf16[16,2048]{1,0:T(8,128)(2,1)}, f32[3,8,128]{2,1,0:T(8,128)}) custom-call(bf16[4,16,1536]{2,1,0:T(8,128)(2,1)} %bitcast.321, bf16[16,2048]{1,0:T(8,128)(2,1)} %pad_maximum_fusion.13.refs_1_, f32[8,128]{1,0:T(8,128)} %get-tuple-element.106.refs_2_), custom_call_target="tpu_custom_call" | custom-call | tf_op jit(solution)/shard_map/hand_back/pallas_call | solution.py:91
  (332 shorter events, 116.8 us)
Async XLA Ops:
  69.6 4.3 copy-start.3
  70.9 6.4 copy-start.29
  71.3 6.1 copy-start.56
  71.4 6.0 copy-start.51
  84.4 3.9 copy-start.8
  165.5 3.8 copy-start.37
  165.5 3.8 copy-start.39
  165.5 3.8 copy-start.41
  165.5 3.8 copy-start.43
  171.8 4.0 copy-start.26
  297.2 10.1 %copy-start.22 = (f32[512,2048]{1,0:T(8,128)S(1)}, f32[512,2048]{1,0:T(8,128)}, u32[]{:S(2)}) copy-start(f32[512,2048]{1,0:T(8,128)} %fusion.107) | copy-start | bytes 12582916
  308.4 10.1 %copy-start.25 = (bf16[4,128,2048]{2,1,0:T(8,128)(2,1)S(1)}, bf16[4,128,2048]{2,1,0:T(8,128)(2,1)}, u32[]{:S(2)}) copy-start(bf16[4,128,2048]{2,1,0:T(8,128)(2,1)} %spread_a2.1) | copy-start | bytes 6291460
  318.4 6.8 copy-start.67
  385.4 3.7 copy-start.34
  385.4 4.0 copy-start.5
  398.5 4.1 copy-start.1
  398.5 5.1 copy-start.21
  480.3 3.5 copy-start.38
  480.3 3.5 copy-start.40
  480.3 3.5 copy-start.42
  480.3 3.5 copy-start.44
  494.5 4.1 copy-start.33
  510.3 24.3 %slice-start.2 = ((f32[768,512]{1,0:T(8,128)}), f32[512,512]{1,0:T(8,128)S(1)}, s32[]{:S(2)}) async-start(f32[768,512]{1,0:T(8,128)} %copy-done.14), calls=%async_computation.2 | async-start | bytes 2097152 | tf_op jit(solution)/shard_map/slice | solution.py:564
  512.6 24.6 %copy-start.10 = (bf16[4,4,128,384]{3,2,1,0:T(8,128)(2,1)S(1)}, bf16[4,4,128,384]{3,2,1,0:T(8,128)(2,1)}, u32[]{:S(2)}) copy-start(bf16[4,4,128,384]{3,2,1,0:T(8,128)(2,1)} %copy-done.9) | copy-start | bytes 4718596
  539.7 8.3 %copy-start.4 = (bf16[4,128,2048]{2,1,0:T(8,128)(2,1)S(1)}, bf16[4,128,2048]{2,1,0:T(8,128)(2,1)}, u32[]{:S(2)}) copy-start(bf16[4,128,2048]{2,1,0:T(8,128)(2,1)} %get-tuple-element.56) | copy-start | bytes 6291460
  539.8 8.3 %copy-start.52 = (f32[2048]{0:T(1024)S(1)}, f32[2048]{0:T(1024)}, u32[]{:S(2)}) copy-start(f32[2048]{0:T(1024)} %copy-done.51) | copy-start | bytes 24580
  539.8 8.3 %copy-start.57 = (f32[2048]{0:T(1024)S(1)}, f32[2048]{0:T(1024)}, u32[]{:S(2)}) copy-start(f32[2048]{0:T(1024)} %copy-done.56) | copy-start | bytes 24580
  539.8 8.3 %copy-start.63 = (f32[512]{0:T(512)S(1)}, f32[512]{0:T(512)}, u32[]{:S(2)}) copy-start(f32[512]{0:T(512)} %get-tuple-element.168) | copy-start | bytes 6148
  539.8 8.3 %copy-start.64 = (f32[512]{0:T(512)S(1)}, f32[512]{0:T(512)}, u32[]{:S(2)}) copy-start(f32[512]{0:T(512)} %get-tuple-element.170) | copy-start | bytes 6148
  550.6 7.5 %copy-start.28 = (bf16[64,8,4,128]{3,1,2,0:T(8,128)(2,1)}, bf16[64,8,4,128]{3,1,2,0:T(8,128)(2,1)S(1)}, u32[]{:S(2)}) copy-start(bf16[64,8,4,128]{3,1,2,0:T(8,128)(2,1)S(1)} %copy.211) | copy-start | bytes 1572868
  550.7 7.5 %copy-start.27 = (bf16[4,4,128,128]{3,2,1,0:T(8,128)(2,1)S(1)}, bf16[4,4,128,128]{3,2,1,0:T(8,128)(2,1)}, u32[]{:S(2)}) copy-start(bf16[4,4,128,128]{3,2,1,0:T(8,128)(2,1)} %copy-done.26) | copy-start | bytes 1572868
  558.4 4.3 copy-start.48
  558.5 5.3 copy-start.47
  558.5 7.1 copy-start.46
  562.7 3.8 copy-start.45
  568.3 35.1 %copy-start.66 = (f32[128]{0:T(128)S(1)}, f32[128]{0:T(128)}, u32[]{:S(2)}) copy-start(f32[128]{0:T(128)} %get-tuple-element.149) | copy-start | bytes 1540
  568.3 35.1 %copy-start.6 = (bf16[1,128,2048]{2,1,0:T(8,128)(2,1)S(1)}, bf16[1,128,2048]{2,1,0:T(8,128)(2,1)}, u32[]{:S(2)}) copy-start(bf16[1,128,2048]{2,1,0:T(8,128)(2,1)} %param.15) | copy-start | bytes 1572868
  603.4 6.3 slice-start
  605.8 3.9 slice-start.1
  605.8 3.9 copy-start.23
  612.8 4.6 copy-start.62
  612.8 4.7 copy-start.60
  612.8 5.4 copy-start.59
  612.8 6.1 copy-start.65
  612.8 7.3 %copy-start.61 = (f32[2048]{0:T(1024)S(1)}, f32[2048]{0:T(1024)}, u32[]{:S(2)}) copy-start(f32[2048]{0:T(1024)} %get-tuple-element.148) | copy-start | bytes 24580
  693.0 27.7 %copy-start.54 = (bf16[3,16,2048]{2,1,0:T(8,128)(2,1)S(1)}, bf16[3,16,2048]{2,1,0:T(8,128)(2,1)}, u32[]{:S(2)}) copy-start(bf16[3,16,2048]{2,1,0:T(8,128)(2,1)} %get-tuple-element.96) | copy-start | bytes 589828
  713.1 6.1 copy-start.58
  717.3 6.1 copy-start.53
  (24 other events, 57.3 us)

commit v2 on v1

--- a/solution.py
+++ b/solution.py
@@ -247,6 +247,10 @@
     )
 
 
+def summed(own, received):
+    return (own.astype(F32) + received.astype(F32).sum(0)).astype(BF)
+
+
 def after_second(sa, sb, ra, rb, by_core):
     own_a = pick(sa, slot_y(by_core)).astype(F32)
     own_b = pick(sb, lax.axis_index("z")).astype(F32)
@@ -263,10 +267,6 @@
     return centred * lax.rsqrt(spread + EPSILON) * gain + shift
 
 
-def gelu_exact(values):
-    return jax.nn.gelu(values, approximate=False)
-
-
 def doc_number(positions, doc_ends):
     return jnp.sum((doc_ends[None, :] <= positions[:, None]).astype(jnp.int32), axis=1)
 
@@ -278,6 +278,313 @@
 NN = ((1,), (0,))
 NT = ((1,), (1,))
 TN = ((0,), (0,))
+
+
+ORDER = (0, 1, 3, 2)
+
+
+def remote(src, dst, sems, index, to):
+    send, recv = sems
+    return pltpu.make_async_remote_copy(
+        src_ref=src,
+        dst_ref=dst,
+        send_sem=send.at[index],
+        recv_sem=recv.at[index],
+        device_id=to,
+        device_id_type=pl.DeviceIdType.MESH,
+    )
+
+
+def feed_forward_body(
+    a2_in,
+    res_in,
+    dy_in,
+    gain_in,
+    bias_in,
+    dyg_hbm,
+    wup_hbm,
+    wdn_hbm,
+    dattn_hbm,
+    dhid_out,
+    outp_hbm,
+    up_a_own,
+    up_b_own,
+    dn_a_own,
+    dn_b_own,
+    up_a_got,
+    up_b_got,
+    dn_a_got,
+    dn_b_got,
+    small_out,
+    wup,
+    wdn,
+    a2g,
+    dyg,
+    dact,
+    act,
+    dup,
+    part,
+    own,
+    got,
+    outp,
+    up_c,
+    dn_c,
+    datt,
+    local_sem,
+    send_sem,
+    recv_sem,
+):
+    sems = (send_sem, recv_sem)
+    me = coords()
+    x, y, z, core = me["x"], me["y"], me["z"], me["core"]
+    other = 1 - core
+    blk, width = a2_in.shape
+    span = 4 * blk
+    hidden = act.shape[1]
+
+    load_down = pltpu.make_async_copy(wdn_hbm, wdn, local_sem.at[0])
+    load_down.start()
+    load_dy = []
+    for p, k in enumerate(ORDER):
+        load_dy.append(
+            pltpu.make_async_copy(
+                dyg_hbm.at[lax.rem(x + 4 - k, 4)], dyg.at[p], local_sem.at[1 + p]
+            )
+        )
+        load_dy[-1].start()
+    load_up = pltpu.make_async_copy(wup_hbm, wup, local_sem.at[5])
+    load_up.start()
+
+    greet(ring("x") + ring("y") + ring("z") + near())
+
+    spread = [
+        remote(a2_in, a2g.at[p], sems, p, peer(x=ORDER[p])) for p in (1, 2, 3)
+    ]
+    for copy in spread:
+        copy.start()
+    a2g[0] = a2_in[...]
+
+    load_down.wait()
+    for copy in load_dy:
+        copy.wait()
+
+    @pl.loop(0, 4)
+    def _(j):
+        tile = wdn[j // 2, pl.ds(2 * lax.rem(j, 2), 2)].reshape(512, width)
+        cols = pl.ds(pl.multiple_of(j * 512, 512), 512)
+        dact[:, cols] = dot(dyg[...].reshape(span, width), tile, NT)
+
+    load_up.wait()
+    for copy in spread:
+        copy.wait_recv()
+
+    @pl.loop(0, hidden // 256)
+    def _(j):
+        cols = pl.ds(pl.multiple_of(j * 256, 256), 256)
+        u = dot(a2g[...].reshape(span, width), wup[:, :, :, :, cols].reshape(width, 256), NN)
+        u = u + bias_in[:, cols]
+        phi = 0.5 + 0.5 * lax.erf(u * math.sqrt(0.5))
+        act[:, cols] = (u * phi).astype(BF)
+        slope = phi + u * (jnp.exp(-0.5 * u * u) * (1.0 / math.sqrt(2.0 * math.pi)))
+        d_up = (dact[:, cols] * slope).astype(BF)
+        dup[:, cols] = d_up
+        small_out[3:4, cols] = jnp.sum(d_up.astype(F32), axis=0, keepdims=True)
+
+    def sends(j):
+        cols = pl.ds(pl.multiple_of(j * 512, 512), 512)
+        return [
+            remote(
+                part.at[p - 1, :, cols],
+                got.at[p - 1, :, cols],
+                sems,
+                4 + 3 * j + p - 1,
+                peer(x=-ORDER[p]),
+            )
+            for p in (3, 1, 2)
+        ]
+
+    @pl.loop(0, 4)
+    def _(j):
+        cols = pl.ds(pl.multiple_of(j * 512, 512), 512)
+        d = dot(dup[...], wup[j].reshape(512, hidden), NT)
+        own[:, cols] = d[:blk]
+        for p in (1, 2, 3):
+            part[p - 1, :, cols] = d[p * blk : (p + 1) * blk].astype(BF)
+        for copy in sends(j):
+            copy.start()
+
+    @pl.loop(0, 4)
+    def _(j):
+        cols = pl.ds(pl.multiple_of(j * 512, 512), 512)
+        o = dot(act[...], wdn[:, :, :, :, cols].reshape(hidden, 512), NN)
+        outp[:, :, cols] = o.astype(BF).reshape(4, blk, 512)
+
+    keep_out = pltpu.make_async_copy(outp, outp_hbm, local_sem.at[6])
+    keep_out.start()
+
+    def grad_down(c, t):
+        cols = pl.ds(pl.multiple_of(c * (hidden // 2) + t * 256, 256), 256)
+        return dot(act[:, cols], dyg[...].reshape(span, width), TN)
+
+    def grad_up(t, c):
+        cols = pl.ds(pl.multiple_of(t * 512 + c * 256, 256), 256)
+        return dot(a2g[:, :, cols].reshape(span, 256), dup[...], TN)
+
+    def swap_down(t):
+        return remote(wdn.at[other, t], dn_c.at[t], sems, 16 + t, peer(core=1))
+
+    def swap_up(t):
+        return remote(wup.at[t, other], up_c.at[t], sems, 20 + t, peer(core=1))
+
+    @pl.loop(0, 4)
+    def _(t):
+        wdn[other, t] = grad_down(other, t).astype(BF).reshape(4, 64, width)
+        swap_down(t).start()
+
+    @pl.loop(0, 4)
+    def _(t):
+        wup[t, other] = grad_up(t, other).astype(BF).reshape(4, 64, hidden)
+        swap_up(t).start()
+
+    @pl.loop(0, 4)
+    def _(t):
+        swap_down(t).wait_recv()
+        total = grad_down(core, t) + dn_c[t].reshape(256, width).astype(F32)
+        wdn[core, t] = total.astype(BF).reshape(4, 64, width)
+
+    first = []
+
+    def stage(src, dst, index, to):
+        first.append(remote(src, dst, sems, index, to))
+        first[-1].start()
+
+    low, high = slice(0, 32), slice(32, 64)
+    for k in (1, 3, 2):
+        zz, yy = lax.rem(z + k, 4), lax.rem(y + k + 3, 4)
+        stage(wdn.at[core, :, zz, low], dn_a_got.at[k - 1], 24 + k, peer(z=k))
+        stage(wdn.at[core, yy, :, high], dn_b_got.at[k - 1], 28 + k, peer(y=k))
+
+    @pl.loop(0, 4)
+    def _(t):
+        swap_up(t).wait_recv()
+        total = grad_up(t, core) + up_c[t].reshape(256, hidden).astype(F32)
+        wup[t, core] = total.astype(BF).reshape(4, 64, hidden)
+
+    for k in (1, 3, 2):
+        zz, yy = lax.rem(z + k, 4), lax.rem(y + k, 4)
+        stage(wup.at[:, core, zz, low], up_a_got.at[k - 1], 32 + k, peer(z=k))
+        stage(wup.at[yy, core, :, high], up_b_got.at[k - 1], 36 + k, peer(y=k))
+
+    @pl.loop(0, 4)
+    def _(j):
+        for copy in sends(j):
+            copy.wait_recv()
+
+    small_out[0:3, :] = jnp.zeros((3, width), F32)
+    small_out[4:8, :] = jnp.zeros((4, width), F32)
+    gain = gain_in[...]
+
+    @pl.loop(0, blk // 16)
+    def _(i):
+        rows = pl.ds(pl.multiple_of(i * 16, 16), 16)
+        d = own[rows, :]
+        for p in range(3):
+            d = d + got[p, rows, :].astype(F32)
+        v = res_in[rows, :]
+        centred = v - jnp.mean(v, axis=-1, keepdims=True)
+        s = lax.rsqrt(jnp.mean(centred * centred, axis=-1, keepdims=True) + EPSILON)
+        n = centred * s
+        dn = d * gain
+        d_res = s * (
+            dn
+            - jnp.mean(dn, axis=-1, keepdims=True)
+            - n * jnp.mean(dn * n, axis=-1, keepdims=True)
+        )
+        dy_own = dy_in[rows, :].astype(F32)
+        hid = dy_own + d_res
+        low_hid = hid.astype(BF)
+        dhid_out[rows, :] = hid
+        datt[rows, :] = low_hid
+        small_out[0:1, :] += jnp.sum(d * n, axis=0, keepdims=True)
+        small_out[1:2, :] += jnp.sum(d, axis=0, keepdims=True)
+        small_out[2:3, :] += jnp.sum(low_hid.astype(F32), axis=0, keepdims=True)
+        small_out[4:5, :] += jnp.sum(dy_own, axis=0, keepdims=True)
+
+    attn = [
+        remote(datt, dattn_hbm.at[x], sems, 40 + k, peer(x=k)) for k in (1, 3, 2)
+    ]
+    for copy in attn:
+        copy.start()
+    kept = [keep_out, pltpu.make_async_copy(datt, dattn_hbm.at[x], local_sem.at[7])]
+    zy = lax.rem(y + 3, 4)
+    kept.append(pltpu.make_async_copy(wdn.at[core, :, z, low], dn_a_own, local_sem.at[8]))
+    kept.append(pltpu.make_async_copy(wdn.at[core, zy, :, high], dn_b_own, local_sem.at[9]))
+    kept.append(pltpu.make_async_copy(wup.at[:, core, z, low], up_a_own, local_sem.at[10]))
+    kept.append(pltpu.make_async_copy(wup.at[y, core, :, high], up_b_own, local_sem.at[11]))
+    for copy in kept[1:]:
+        copy.start()
+
+    for copy in first + attn:
+        copy.wait_recv()
+    for copy in spread + first + attn:
+        copy.wait_send()
+
+    @pl.loop(0, 4)
+    def _(j):
+        for copy in sends(j):
+            copy.wait_send()
+        swap_down(j).wait_send()
+        swap_up(j).wait_send()
+
+    for copy in kept:
+        copy.wait()
+
+
+def feed_forward(collective_id, a2, residual, dy, gain, bias, dy_g, wup, wdn):
+    blk, width = a2.shape
+    hidden = wup.shape[-1]
+    span = 4 * blk
+    vmem = pl.BlockSpec(memory_space=pltpu.VMEM)
+    hbm = pl.BlockSpec(memory_space=pl.ANY)
+    quarter = (4, 32, width)
+    outs = (
+        [((4, blk, width), BF, hbm), ((blk, width), F32, vmem), ((4, blk, width), BF, hbm)]
+        + [(quarter, BF, hbm)] * 4
+        + [((3,) + quarter, BF, hbm)] * 4
+        + [((8, width), F32, vmem)]
+    )
+    scratch = [
+        ((4, 2, 4, 64, hidden), BF),
+        ((2, 4, 4, 64, width), BF),
+        ((4, blk, width), BF),
+        ((4, blk, width), BF),
+        ((span, hidden), F32),
+        ((span, hidden), BF),
+        ((span, hidden), BF),
+        ((3, blk, width), BF),
+        ((blk, width), F32),
+        ((3, blk, width), BF),
+        ((4, blk, width), BF),
+        ((4, 4, 64, hidden), BF),
+        ((4, 4, 64, width), BF),
+        ((blk, width), BF),
+    ]
+    return pl.pallas_call(
+        feed_forward_body,
+        out_shape=tuple(jax.ShapeDtypeStruct(s, d) for s, d, _ in outs),
+        in_specs=[vmem] * 5 + [hbm] * 3,
+        out_specs=tuple(o[2] for o in outs),
+        scratch_shapes=[pltpu.VMEM(s, d) for s, d in scratch]
+        + [
+            pltpu.SemaphoreType.DMA((12,)),
+            pltpu.SemaphoreType.DMA((44,)),
+            pltpu.SemaphoreType.DMA((44,)),
+        ],
+        compiler_params=pltpu.CompilerParams(
+            collective_id=collective_id, has_side_effects=True, vmem_limit_bytes=62 << 20
+        ),
+        name="feed_forward",
+    )(a2, residual, dy, gain.reshape(1, width), bias.reshape(1, hidden), dy_g, wup, wdn)
 
 
 def local(
@@ -364,7 +671,6 @@
     gain1, shift1, bias_qv, bias_out, gain2, shift2, bias_up, bias_down = vectors
     weight_qkv = wqkv_g.reshape(width, 3 * part)
     weight_out = wout_g.reshape(part, width)
-    dy_all = dy_g.reshape(span, width)
 
     inputs = tok_g.reshape(span, width).astype(F32)
     normed1 = layer_norm(inputs, gain1, shift1).astype(BF)
@@ -447,78 +753,28 @@
         [attn_part.astype(BF), wdown_s],
         [((3, blk, width), BF), ((2, 4, 4, 64, width), BF)],
     )
-    weight_up = wup_g.reshape(width, hidden)
-    weight_down = wdown_g.reshape(hidden, width)
 
     own_tok = tok.astype(F32)
     residual = own_tok + pick(attn_part, x_at) + attn_got.astype(F32).sum(0) + bias_out
     normed2 = layer_norm(residual, gain2, shift2).astype(BF)
 
-    (normed2_g,) = exchange(
-        "spread_a2",
-        3,
-        lambda comm, ins, outs: spread_x(comm, ins[0], outs[0]),
-        lambda: ring("x"),
-        [normed2],
-        [((4, blk, width), BF)],
-    )
-    a2 = normed2_g.reshape(span, width)
     bias_up_own = lax.dynamic_slice_in_dim(bias_up, x_at * hidden, hidden)
-    upper = dot(a2, weight_up, NN) + bias_up_own
-    activated = gelu_exact(upper).astype(BF)
-    d_act = dot(dy_all, weight_down, NT)
-    d_upper = jax.vjp(gelu_exact, upper)[1](d_act)[0].astype(BF)
-    d_a2_part = dot(d_upper, weight_up, NT).reshape(4, blk, width)
-    out_part = dot(activated, weight_down, NN).reshape(4, blk, width)
-    g_wdown = dot(activated, dy_all, TN).astype(BF).reshape(2, 4, 4, 64, width)
-    g_wup = dot(a2, d_upper, TN).astype(BF).reshape(4, 2, 4, 64, hidden)
-    g_bup = jnp.sum(d_upper.astype(F32), axis=0)
-
-    def fifth_body(comm, ins, outs):
-        split_x(comm, ins[0], outs[0])
-        split_x(comm, ins[1], outs[1])
-        swap_cores(comm, ins[2], outs[2], False)
-        swap_cores(comm, ins[3], outs[3], True)
-
-    d_a2_got, out_got, up_c, down_c = exchange(
-        "sum_ff",
-        4,
-        fifth_body,
-        lambda: ring("x") + near(),
-        [d_a2_part.astype(BF), out_part.astype(BF), g_wup, g_wdown],
-        [
-            ((3, blk, width), BF),
-            ((3, blk, width), BF),
-            ((4, 4, 64, hidden), BF),
-            ((4, 4, 64, width), BF),
-        ],
-    )
-    out = residual + pick(out_part, x_at) + out_got.astype(F32).sum(0) + bias_down
-    d_a2 = pick(d_a2_part, x_at) + d_a2_got.astype(F32).sum(0)
-    d_resnorm, g_gain2, g_shift2 = jax.vjp(layer_norm, residual, gain2, shift2)[1](d_a2)
-    d_hidden = dy.astype(F32) + d_resnorm
-    d_attn_own = d_hidden.astype(BF)
-    up_s, down_s = after_cores(g_wup, up_c, False), after_cores(g_wdown, down_c, True)
-
-    def sixth_body(comm, ins, outs):
-        spread_x(comm, ins[0], outs[0])
-        reduce_first(comm, ins[1], outs[1], outs[2], False)
-        reduce_first(comm, ins[2], outs[3], outs[4], True)
-
-    d_attn_g, up_a, up_b, down_a, down_b = exchange(
-        "spread_d_attn",
-        5,
-        sixth_body,
-        lambda: ring("x") + ring("y") + ring("z"),
-        [d_attn_own, up_s, down_s],
-        [
-            ((4, blk, width), BF),
-            ((3, 4, 32, hidden), BF),
-            ((3, 4, 32, hidden), BF),
-            ((3, 4, 32, width), BF),
-            ((3, 4, 32, width), BF),
-        ],
-    )
+    (
+        d_attn_g,
+        d_hidden,
+        out_part,
+        up_a_own,
+        up_b_own,
+        down_a_own,
+        down_b_own,
+        up_a,
+        up_b,
+        down_a,
+        down_b,
+        ff_small,
+    ) = feed_forward(3, normed2, residual, dy, gain2, bias_up_own, dy_g, wup_g, wdown_g)
+    up_sa, up_sb = summed(up_a_own, up_a), summed(up_b_own, up_b)
+    down_sa, down_sb = summed(down_a_own, down_a), summed(down_b_own, down_b)
     d_attn = d_attn_g.reshape(span, width)
     d_mixed = dot(d_attn, weight_out, NT).astype(BF)
     d_heads = d_mixed.reshape(4, blk, heads, HEAD)
@@ -537,28 +793,30 @@
 
     d_keys, d_values = unwindow(d_kwin), unwindow(d_vwin)
     d_edge = jnp.concatenate([d_keys[:W], d_values[:W]], axis=1).astype(BF)
-    up_sa, up_sb = after_first(up_s, up_a, up_b, False)
-    down_sa, down_sb = after_first(down_s, down_a, down_b, True)
 
     def seventh_body(comm, ins, outs):
         comm.push(ins[0], outs[0], peer(z=3))
         reduce_second(comm, ins[1], ins[2], outs[1], outs[2], False)
         reduce_second(comm, ins[3], ins[4], outs[3], outs[4], True)
-
-    d_edge_got, up_a2, up_b2, down_a2, down_b2 = exchange(
+        for p in (1, 2, 3):
+            comm.push(ins[5].at[p], outs[5].at[p - 1], peer(x=-ORDER[p]))
+
+    d_edge_got, up_a2, up_b2, down_a2, down_b2, out_got = exchange(
         "edge_back",
         6,
         seventh_body,
-        lambda: ring("y") + ring("z"),
-        [d_edge, up_sa, up_sb, down_sa, down_sb],
+        lambda: ring("x") + ring("y") + ring("z"),
+        [d_edge, up_sa, up_sb, down_sa, down_sb, out_part],
         [
             ((W, 2 * part), BF),
             ((3, 32, hidden), BF),
             ((3, 32, hidden), BF),
             ((3, 32, width), BF),
             ((3, 32, width), BF),
+            ((3, blk, width), BF),
         ],
     )
+    out = residual + out_part[0].astype(F32) + out_got.astype(F32).sum(0) + bias_down
     up_f = after_second(up_sa, up_sb, up_a2, up_b2, False)
     down_f = after_second(down_sa, down_sb, down_a2, down_b2, True)
     d_kv = jnp.concatenate([d_keys[W:], d_values[W:]], axis=1)
@@ -608,11 +866,11 @@
                 g_gain1,
                 g_shift1,
                 g_bqv,
-                jnp.sum(d_attn_own.astype(F32), axis=0),
-                g_gain2,
-                g_shift2,
-                placed(g_bup, x_at * hidden, 4 * hidden),
-                jnp.sum(dy.astype(F32), axis=0),
+                ff_small[2],
+                ff_small[0],
+                ff_small[1],
+                placed(ff_small[3], x_at * hidden, 4 * hidden),
+                ff_small[4],
             )
         ],
         axis=1,

time: 736 us -> 612 us (0.83)
  matrix products: 109 us -> 38.1 us
  other arithmetic: 101 us -> 72.7 us
  Pallas kernels: 436 us -> 414 us
    pallas_call x11 -> x8, Pallas kernels: 436 us -> 310 us  [exchange(): pl.pallas_call(kernel, out_shape=tuple((jax.ShapeDtypeStruct(s, d) for s,...]
    pallas_call x0 -> x1, Pallas kernels: none -> 104 us  [feed_forward(): pl.pallas_call(feed_forward_body, out_shape=tuple((jax.ShapeDtypeStruct(s...]
    dot_general x12 -> x6, matrix products: 97.4 us -> 30.5 us  [dot(): return lax.dot_general(a, b, (dims, ((), ())), preferred_element_type=F32)]
where the time goes in v2:
time: 612 us; the launch traced here: 600 us
  Pallas kernels  414 us (68%)
  local copies, waits for them, and re-layouts  73.2 us (12%)
  other arithmetic  72.7 us (12%)
  matrix products  38.1 us (6%)
    pallas_call x8, Pallas kernels, exchange(): pl.pallas_call(kernel, out_shape=tuple((jax.ShapeDtypeStruct(s, d) for s,...  310 us
    pallas_call x1, Pallas kernels, feed_forward(): pl.pallas_call(feed_forward_body, out_shape=tuple((jax.ShapeDtypeStruct(s...  104 us
    dot_general x6, matrix products, dot(): return lax.dot_general(a, b, (dims, ((), ())), preferred_element_type=F32)  30.5 us
    squeeze x8, local copies, waits for them, and re-layouts, unwindow(): array[b]  14.9 us

profile of v2, /device:TPU:1, one launch (start us, length us, event | category | flops | bytes accessed | tf_op | source)
XLA Modules:
  0.0 600.4 jit_solution(3379817426453194153)
XLA Ops:
  1.6 5.4 concatenate.83
  10.5 1.7 copy.196
  12.2 60.8 %gather_attn.1 = (bf16[4,128,2048]{2,1,0:T(8,128)(2,1)}, f32[4,2,4,4,8,128]{5,4,3,2,1,0:T(8,128)}, bf16[4,128,2048]{2,1,0:T(8,128)(2,1)}, bf16[4,2,4,64,1536]{4,...) custom-call(bf16[128,2048]{1,0:T(8,128)(2,1)} %bitcast.223, bf16[128,2048]{1,0:T(8,128)(2,1)} %bitcast.242, ...), custom_call_target="tpu_custom_call" | custom-call | tf_op jit(solution)/shard_map/gather_attn/pallas_call | solution.py:91
  74.3 1.9 convert_reduce_fusion
  79.3 2.1 fusion.4
  82.3 6.2 %fusion.5.refs_0_ = bf16[512,1536]{1,0:T(8,128)(2,1)S(1)} fusion(bf16[512,2048]{1,0:T(8,128)(2,1)S(1)} %bitcast.241, bf16[2048,1536]{1,0:T(8,128)(2,1)} %bitcast.282, f32[1536]{0:T(1024)S(1)} %pad_maximum_fusion.14), kind=kOutput, calls=%fused_computation.30 | convolution fusion | flops 3222798336 | bytes 9967616 | tf_op jit(solution)/shard_map/dot_general | solution.py:275
  90.8 1.8 stack.107
  95.9 67.2 %edge_and_up.1 = (bf16[256,1024]{1,0:T(8,128)(2,1)}, bf16[4,2,4,64,2048]{4,3,2,1,0:T(8,128)(2,1)}, bf16[2,4,4,64,2048]{4,3,2,1,0:T(8,128)(2,1)}) custom-call(bf16[512,1536]{1,0:T(8,128)(2,1)} %copy-done.6, bf16[4,16,2048]{2,1,0:T(8,128)(2,1)} %bitcast.256, bf16[64,2048]{1,0:T(8,128)(2,1)} %refs_2_.1), custom_call_target="tpu_custom_call" | custom-call | tf_op jit(solution)/shard_map/edge_and_up/pallas_call | solution.py:91
  166.1 2.0 copy.161
  170.8 1.6 exponential_reduce_fusion
  173.3 2.3 convolution_convert_fusion.3
  176.6 4.0 fusion.76
  180.7 52.8 %sum_attn_and_down.1 = (bf16[3,128,2048]{2,1,0:T(8,128)(2,1)}, bf16[2,4,4,64,2048]{4,3,2,1,0:T(8,128)(2,1)}) custom-call(bf16[4,128,2048]{2,1,0:T(8,128)(2,1)} %get-tuple-element.179.refs_0_, bf16[2,4,4,64,2048]{4,3,2,1,0:T(8,128)(2,1)} %get-tuple-element.65.refs_1_), custom_call_target="tpu_custom_call" | custom-call | tf_op jit(solution)/shard_map/sum_attn_and_down/pallas_call | solution.py:91
  233.4 1.9 convert_reduce_fusion.8
  235.3 1.9 fusion.63
  238.6 104.1 %feed_forward.1 = (bf16[4,128,2048]{2,1,0:T(8,128)(2,1)}, f32[128,2048]{1,0:T(8,128)}, bf16[4,128,2048]{2,1,0:T(8,128)(2,1)}, bf16[4,32,2048]{2,1,0:T(8,128)(2,1...) custom-call(bf16[128,2048]{1,0:T(8,128)(2,1)} %add_convert_fusion.5., ...), custom_call_target="tpu_custom_call" | custom-call | tf_op jit(solution)/shard_map/feed_forward/pallas_call | solution.py:572
  342.8 3.7 convolution_convert_fusion.2
  346.4 2.6 convolution_convert_fusion.1
  352.6 1.9 convert_reduce_fusion.7
  354.5 2.0 add_convert_fusion.4.refs_1_
  362.0 1.6 multiply_reduce_fusion.1
  365.9 1.4 convolution_bitcast_fusion
  367.3 1.4 fusion.67
  368.7 2.3 copy.168
  371.0 2.3 copy.171
  377.9 1.9 pad_add_fusion
  381.9 1.5 fusion.66
  383.4 2.3 copy.164
  385.7 2.3 copy.167
  387.9 2.3 copy.166
  391.4 2.2 pad_add_fusion.1
  395.5 26.8 %edge_back.1 = (bf16[256,1024]{1,0:T(8,128)(2,1)}, bf16[3,32,2048]{2,1,0:T(8,128)(2,1)}, bf16[3,32,2048]{2,1,0:T(8,128)(2,1)}, bf16[3,32,2048]{2,1,0:T(8,128)(2,...) custom-call(bf16[256,1024]{1,0:T(8,128)(2,1)} %pad_maximum_fusion.3.refs_0_, ...), custom_call_target="tpu_custom_call" | custom-call | tf_op jit(solution)/shard_map/edge_back/pallas_call | solution.py:91
  422.4 1.7 fusion.7
  425.3 2.6 fusion.26
  428.0 8.3 %fusion.77 = (bf16[4,128,2048]{2,1,0:T(8,128)(2,1)}, f32[4,128,2048]{2,1,0:T(8,128)}) fusion(bf16[2048,1536,1]{1,0,2:T(8,128)(2,1)} %bitcast.283, bf16[4,128,1024]{2,1,0:T(8,128)(2,1)S(1)} %bitcast.230, bf16[4,128,512]{2,1,0:T(8,128)(2,1)S(1)} %copy-done.34), kind=kOutput, calls=%fused_computation.220 | convolution fusion | flops 3225419776 | bytes 14155776 | tf_op jit(solution)/shard_map/dot_general | solution.py:275
  442.6 5.7 convolution_convert_fusion
  448.3 31.0 %sum_d_a1.1 = (bf16[3,128,2048]{2,1,0:T(8,128)(2,1)}, bf16[4,4,64,1536]{3,2,1,0:T(8,128)(2,1)}, bf16[4,4,16,2048]{3,2,1,0:T(8,128)(2,1)}, bf16[3,16,2048]{2,1,0:T(8,128)(2,1)}, bf16[64,2048]{1,0:T(8,128)(2,1)}) custom-call(bf16[4,128,2048]{2,1,0:T(8,128)(2,1)} %get-tuple-element.183.refs_0_, bf16[4,2,4,64,1536]{4,3,2,1,0:T(8,128)(2,1)} %bitcast.224, ...), custom_call_target="tpu_custom_call" | custom-call | tf_op jit(solution)/shard_map/sum_d_a1/pallas_call | solution.py:91
  479.4 2.7 fusion.8.refs_1_
  482.1 3.0 fusion
  486.2 1.8 fusion.62
  488.5 1.4 add_bitcast_fusion
  500.0 2.0 copy.154.refs_0_
  502.0 46.1 %reduce_attn_1.1 = (bf16[3,4,32,1536]{3,2,1,0:T(8,128)(2,1)}, bf16[3,4,32,1536]{3,2,1,0:T(8,128)(2,1)}, bf16[3,4,16,1024]{3,2,1,0:T(8,128)(2,1)}, bf16[3,4,16,1024]{3,2,1,0:T(8,128)(2,1)}, f32[7,4,8,128]{3,2,1,0:T(8,128)}) custom-call(bf16[4,4,64,1536]{3,2,1,0:T(8,128)(2,1)} %copy.154.refs_0_, bf16[4,4,16,2048]{3,2,1,0:T(8,128)(2,1)} %fusion.8.refs_1_, ...), custom_call_target="tpu_custom_call" | custom-call | tf_op jit(solution)/shard_map/reduce_attn_1/pallas_call | solution.py:91
  551.3 1.6 fusion.39.refs_2_
  553.0 1.7 fusion.38.refs_3_
  556.7 13.0 %reduce_attn_2.1 = (bf16[3,32,1536]{2,1,0:T(8,128)(2,1)}, bf16[3,32,1536]{2,1,0:T(8,128)(2,1)}, bf16[3,16,1024]{2,1,0:T(8,128)(2,1)}, bf16[3,16,1024]{2,1,0:T(8,128)(2,1)}, f32[3,8,128]{2,1,0:T(8,128)}) custom-call(bf16[4,32,1536]{2,1,0:T(8,128)(2,1)} %fusion.30.refs_0_, bf16[4,32,1536]{2,1,0:T(8,128)(2,1)} %fusion.29.refs_1_, ...), custom_call_target="tpu_custom_call" | custom-call | tf_op jit(solution)/shard_map/reduce_attn_2/pallas_call | solution.py:91
  580.4 12.4 %hand_back.1 = (bf16[3,16,1536]{2,1,0:T(8,128)(2,1)}, bf16[16,2048]{1,0:T(8,128)(2,1)}, f32[3,8,128]{2,1,0:T(8,128)}) custom-call(bf16[4,16,1536]{2,1,0:T(8,128)(2,1)} %bitcast.258, bf16[16,2048]{1,0:T(8,128)(2,1)} %pad_maximum_fusion.13.refs_1_, f32[8,128]{1,0:T(8,128)} %get-tuple-element.115.refs_2_), custom_call_target="tpu_custom_call" | custom-call | tf_op jit(solution)/shard_map/hand_back/pallas_call | solution.py:91
  595.3 1.5 convert_element_type.424
  (282 shorter events, 85.4 us)
Async XLA Ops:
  73.0 3.3 copy-start.2
  88.5 6.0 copy-start.6
  95.5 68.6 %copy-start.22 = (bf16[512,512]{1,0:T(8,128)(2,1)S(1)}, bf16[512,512]{1,0:T(8,128)(2,1)}, u32[]{:S(2)}) copy-start(bf16[512,512]{1,0:T(8,128)(2,1)} %get-tuple-element.138) | copy-start | bytes 1572868
  95.9 73.8 %copy-start.15 = (bf16[4,128,4,128]{1,3,2,0:T(8,128)(2,1)}, bf16[4,128,4,128]{1,3,2,0:T(8,128)(2,1)S(1)}, u32[]{:S(2)}) copy-start(bf16[4,128,4,128]{1,3,2,0:T(8,128)(2,1)S(1)} %copy.138) | copy-start | bytes 1572868
  166.1 3.3 copy-start.28
  170.8 4.8 copy-start
  170.8 1.7 copy-start.39
  170.8 1.7 copy-start.41
  170.8 2.1 copy-start.43
  170.8 2.5 copy-start.45
  173.3 3.4 copy-start.19
  233.4 1.9 copy-start.3
  235.3 2.2 copy-start.9
  342.7 3.7 copy-start.35
  342.8 3.7 copy-start.55
  352.6 3.9 copy-start.25
  354.5 2.3 copy-start.38
  356.5 1.5 copy-start.24
  356.8 1.5 copy-start.37
  358.0 1.5 copy-start.23
  358.3 1.5 copy-start.36
  359.5 2.1 copy-start.1
  359.5 2.2 copy-start.40
  359.5 2.3 copy-start.42
  359.5 2.4 copy-start.44
  359.5 2.5 copy-start.46
  363.6 1.4 copy-start.13
  365.1 2.2 copy-start.7
  379.8 1.4 copy-start.8
  379.8 1.5 copy-start.16
  422.3 1.9 copy-start.27
  425.3 2.6 copy-start.34
  427.9 8.3 %copy-start.21 = (bf16[64,8,4,128]{3,1,2,0:T(8,128)(2,1)S(1)}, bf16[64,8,4,128]{3,1,2,0:T(8,128)(2,1)}, u32[]{:S(2)}) copy-start(bf16[64,8,4,128]{3,1,2,0:T(8,128)(2,1)} %copy.194) | copy-start | bytes 1572868
  428.0 8.9 %copy-start.50 = (bf16[3,32,2048]{2,1,0:T(8,128)(2,1)S(1)}, bf16[3,32,2048]{2,1,0:T(8,128)(2,1)}, u32[]{:S(2)}) copy-start(bf16[3,32,2048]{2,1,0:T(8,128)(2,1)} %get-tuple-element.83) | copy-start | bytes 1179652
  436.2 1.7 copy-start.49
  436.2 3.6 copy-start.48
  436.9 4.0 copy-start.47
  438.0 4.6 copy-start.20
  439.1 9.2 %copy-start.29 = (bf16[64,2048]{1,0:T(8,128)(2,1)}, bf16[64,2048]{1,0:T(8,128)(2,1)S(1)}, u32[]{:S(2)}) copy-start(bf16[64,2048]{1,0:T(8,128)(2,1)S(1)} %pad_maximum_fusion.8) | copy-start | bytes 786436
  448.3 31.0 %copy-start.14 = (bf16[512,2048]{1,0:T(8,128)(2,1)S(1)}, bf16[512,2048]{1,0:T(8,128)(2,1)}, u32[]{:S(2)}) copy-start(bf16[512,2048]{1,0:T(8,128)(2,1)} %convolution_convert_fusion.1) | copy-start | bytes 6291460
  479.3 2.8 copy-start.18
  482.1 3.0 copy-start.26
  486.2 2.3 copy-start.32
  495.4 2.6 copy-start.53
  495.4 3.5 copy-start.11
  550.3 2.7 copy-start.51
  550.5 4.2 copy-start.31
  553.0 2.7 copy-start.30
  (8 other events, 8.5 us)

commit v3 on v2

--- a/solution.py
+++ b/solution.py
@@ -587,6 +587,511 @@
     )(a2, residual, dy, gain.reshape(1, width), bias.reshape(1, hidden), dy_g, wup, wdn)
 
 
+def norm_backward(d, v, gain):
+    centred = v - jnp.mean(v, axis=-1, keepdims=True)
+    s = lax.rsqrt(jnp.mean(centred * centred, axis=-1, keepdims=True) + EPSILON)
+    n = centred * s
+    dn = d * gain
+    d_v = s * (
+        dn - jnp.mean(dn, axis=-1, keepdims=True) - n * jnp.mean(dn * n, axis=-1, keepdims=True)
+    )
+    return d_v, n
+
+
+def attention_backward_body(
+    gain_in,
+    bdown_in,
+    ffsmall_in,
+    dattn_hbm,
+    wout_hbm,
+    proj_hbm,
+    edge_hbm,
+    bias_hbm,
+    a1_hbm,
+    mixed_hbm,
+    wqkv_hbm,
+    tok_hbm,
+    dhid_hbm,
+    res_hbm,
+    outp_hbm,
+    ffo0,
+    ffo1,
+    ffo2,
+    ffo3,
+    ffg0,
+    ffg1,
+    ffg2,
+    ffg3,
+    out_o,
+    gtok_o,
+    gqkv_o,
+    gout_o,
+    gup_o,
+    gdn_o,
+    small_o,
+    dattn,
+    wout,
+    proj,
+    kv,
+    bias,
+    a1,
+    mixed,
+    wqkv,
+    tok,
+    dhid,
+    res,
+    outown,
+    outgot,
+    fo,
+    fg,
+    fs,
+    fg2,
+    fup,
+    fdn,
+    dmix,
+    dkv,
+    dqkv,
+    dedge,
+    dedge_got,
+    part,
+    got,
+    qkv_c,
+    out_c,
+    qa,
+    qb,
+    oa,
+    ob,
+    qs,
+    os_,
+    qa2,
+    qb2,
+    oa2,
+    ob2,
+    fq,
+    fout,
+    sm,
+    smc,
+    smz,
+    smy,
+    local_sem,
+    send_sem,
+    recv_sem,
+):
+    sems = (send_sem, recv_sem)
+    me = coords()
+    x, y, z, core = me["x"], me["y"], me["z"], me["core"]
+    other = 1 - core
+    zy = lax.rem(y + 3, 4)
+    blk, width = tok.shape
+    span = 4 * blk
+    partw = mixed.shape[1]
+    heads = partw // HEAD
+    scale = 1.0 / math.sqrt(HEAD)
+    reach = W + blk
+    used = [0]
+    pending = []
+
+    def load(src, dst):
+        copy = pltpu.make_async_copy(src, dst, local_sem.at[used[0]])
+        used[0] += 1
+        copy.start()
+        return copy
+
+    def push(src, dst, index, to):
+        copy = remote(src, dst, sems, index, to)
+        copy.start()
+        pending.append(copy)
+        return copy
+
+    l_dattn, l_wout = load(dattn_hbm, dattn), load(wout_hbm, wout)
+    l_attn = [
+        load(proj_hbm, proj),
+        load(edge_hbm, kv.at[pl.ds(0, W)]),
+        load(proj_hbm.at[:, pl.ds(partw, 2 * partw)], kv.at[pl.ds(W, span)]),
+        load(bias_hbm, bias),
+    ]
+    l_ff = [load(s, fo.at[i]) for i, s in enumerate((ffo0, ffo1, ffo2, ffo3))]
+    l_ff += [load(s, fg.at[i]) for i, s in enumerate((ffg0, ffg1, ffg2, ffg3))]
+    l_wqkv, l_a1, l_mixed = load(wqkv_hbm, wqkv), load(a1_hbm, a1), load(mixed_hbm, mixed)
+    l_end = [load(outp_hbm.at[0], outown), load(res_hbm, res)]
+    l_end += [load(tok_hbm, tok), load(dhid_hbm, dhid)]
+
+    greet(ring("x") + ring("y") + ring("z") + near() + [scattered(), collected()])
+
+    p_out = [
+        push(outp_hbm.at[p], outgot.at[p - 1], p, peer(x=-ORDER[p])) for p in (1, 2, 3)
+    ]
+
+    dkv[...] = jnp.zeros(dkv.shape, F32)
+    l_dattn.wait()
+    l_wout.wait()
+    dmix[...] = dot(
+        dattn[...].reshape(span, width), wout[...].reshape(partw, width), NT
+    ).astype(BF)
+    for copy in l_attn:
+        copy.wait()
+
+    def block(b):
+        rows = pl.ds(pl.multiple_of(b * blk, blk), blk)
+        window = pl.ds(pl.multiple_of(b * blk, blk), reach)
+        for h in range(heads):
+            cols = pl.ds(h * HEAD, HEAD)
+            vcols = pl.ds(partw + h * HEAD, HEAD)
+            q, k, v = proj[rows, cols], kv[window, cols], kv[window, vcols]
+            s = dot(q, k, NT) * scale + bias[b]
+            e = jnp.exp(s - jnp.max(s, axis=-1, keepdims=True))
+            p = e * (1.0 / jnp.sum(e, axis=-1, keepdims=True))
+            do = dmix[rows, cols]
+            dp = dot(do, v, NT)
+            ds = (p * (dp - jnp.sum(dp * p, axis=-1, keepdims=True))).astype(BF)
+            dqkv[rows, cols] = (dot(ds, k, NN) * scale).astype(BF)
+            dkv[window, cols] += dot(ds, q, TN) * scale
+            dkv[window, vcols] += dot(p.astype(BF), do, TN)
+
+    pl.loop(0, 2)(block)
+    dedge[...] = dkv[0:W, :].astype(BF)
+    p_edge = push(dedge, dedge_got, 4, peer(z=3))
+    pl.loop(2, 4)(block)
+
+    for copy in l_ff:
+        copy.wait()
+
+    @pl.loop(0, 4)
+    def _(i):
+        for c in range(4):
+            total = fo[i, c].astype(F32)
+            for g in range(3):
+                total = total + fg[i, g, c].astype(F32)
+            fs[i, c] = total.astype(BF)
+
+    p_ff = []
+    for k in (1, 3, 2):
+        tz, ty, tyc = lax.rem(z + k, 4), lax.rem(y + k, 4), lax.rem(y + k + 3, 4)
+        p_ff.append(push(fs.at[0, ty], fg2.at[0, k - 1], 4 + k, peer(y=k)))
+        p_ff.append(push(fs.at[1, tz], fg2.at[1, k - 1], 7 + k, peer(z=k)))
+        p_ff.append(push(fs.at[2, tyc], fg2.at[2, k - 1], 10 + k, peer(y=k)))
+        p_ff.append(push(fs.at[3, tz], fg2.at[3, k - 1], 13 + k, peer(z=k)))
+
+    p_edge.wait_recv()
+    dqkv[0 : span - W, partw:] = dkv[W:span, :].astype(BF)
+    dqkv[span - W :, partw:] = (dkv[span:, :] + dedge_got[...].astype(F32)).astype(BF)
+    l_wqkv.wait()
+
+    def sends(j):
+        cols = pl.ds(pl.multiple_of(j * 512, 512), 512)
+        return [
+            remote(
+                part.at[lax.rem(x + k, 4), :, cols],
+                got.at[k - 1, :, cols],
+                sems,
+                20 + 3 * j + k - 1,
+                peer(x=k),
+            )
+            for k in (2, 1, 3)
+        ]
+
+    @pl.loop(0, 4)
+    def _(j):
+        cols = pl.ds(pl.multiple_of(j * 512, 512), 512)
+        d = dot(dqkv[...], wqkv[j].reshape(512, 3 * partw), NT)
+        part[:, :, cols] = d.astype(BF).reshape(4, blk, 512)
+        for copy in sends(j):
+            copy.start()
+
+    def grad_qkv(t, c):
+        cols = pl.ds(pl.multiple_of(t * 512 + c * 256, 256), 256)
+        return dot(a1[:, cols], dqkv[...], TN)
+
+    def grad_out(c):
+        cols = pl.ds(pl.multiple_of(c * 256, 256), 256)
+        return dot(mixed[:, cols], dattn[...].reshape(span, width), TN)
+
+    def swap(t):
+        return remote(wqkv.at[t, other], qkv_c.at[t], sems, 32 + t, peer(core=1))
+
+    l_a1.wait()
+
+    @pl.loop(0, 4)
+    def _(t):
+        wqkv[t, other] = grad_qkv(t, other).astype(BF).reshape(4, 64, 3 * partw)
+        swap(t).start()
+
+    l_mixed.wait()
+    wout[other] = grad_out(other).astype(BF).reshape(4, 4, 16, width)
+    p_oc = push(wout.at[other], out_c, 36, peer(core=1))
+
+    @pl.loop(0, 4)
+    def _(t):
+        swap(t).wait_recv()
+        total = grad_qkv(t, core) + qkv_c[t].reshape(256, 3 * partw).astype(F32)
+        wqkv[t, core] = total.astype(BF).reshape(4, 64, 3 * partw)
+
+    low, high = slice(0, 32), slice(32, 64)
+    left, right = slice(0, width // 2), slice(width // 2, width)
+    p_q1, p_o1 = [], []
+    for k in (1, 3, 2):
+        tz, ty = lax.rem(z + k, 4), lax.rem(y + k, 4)
+        p_q1.append(push(wqkv.at[:, core, tz, low], qa.at[k - 1], 36 + k, peer(z=k)))
+        p_q1.append(push(wqkv.at[ty, core, :, high], qb.at[k - 1], 39 + k, peer(y=k)))
+
+    p_oc.wait_recv()
+    wout[core] = (
+        grad_out(core) + out_c[...].reshape(256, width).astype(F32)
+    ).astype(BF).reshape(4, 4, 16, width)
+    for k in (1, 3, 2):
+        tz, tyc = lax.rem(z + k, 4), lax.rem(y + k + 3, 4)
+        p_o1.append(push(wout.at[core, :, tz, :, left], oa.at[k - 1], 42 + k, peer(z=k)))
+        p_o1.append(push(wout.at[core, tyc, :, :, right], ob.at[k - 1], 45 + k, peer(y=k)))
+
+    for copy in p_ff:
+        copy.wait_recv()
+    at = (y, z, zy, z)
+    for i in range(4):
+        total = fs[i, at[i]].astype(F32)
+        for g in range(3):
+            total = total + fg2[i, g].astype(F32)
+        into, half = (fup, fdn)[i // 2], i % 2
+        if i < 2:
+            into[2 * half : 2 * half + 2] = total.astype(BF).reshape(2, 16, fup.shape[2])
+        else:
+            into[32 * half : 32 * half + 32, :] = total.astype(BF)
+    p_x = [
+        push(fup.at[lax.rem(x + k, 4)], gup_o.at[x], 48 + k, peer(x=k)) for k in (1, 3, 2)
+    ]
+    p_x.append(push(fdn, gdn_o, 52, collected()))
+    kept = [load(fup.at[x], gup_o.at[x])]
+
+    for copy in l_end:
+        copy.wait()
+    for copy in p_out:
+        copy.wait_recv()
+
+    @pl.loop(0, blk // 16)
+    def _(i):
+        rows = pl.ds(pl.multiple_of(i * 16, 16), 16)
+        total = res[rows, :] + bdown_in[...] + outown[rows, :].astype(F32)
+        for g in range(3):
+            total = total + outgot[g, rows, :].astype(F32)
+        out_o[rows, :] = total.astype(BF)
+
+    sm[0, 0:5, :] = ffsmall_in[0:5, :]
+    sm[0, 5:7, :] = jnp.zeros((2, width), F32)
+    sm[0, 7:8, :] = jnp.zeros((1, width), F32)
+    sm[0, 7:8, 0 : 3 * partw] = jnp.sum(dqkv[...].astype(F32), axis=0, keepdims=True)
+
+    @pl.loop(0, 4)
+    def _(j):
+        for copy in sends(j):
+            copy.wait_recv()
+
+    gain = gain_in[...]
+
+    @pl.loop(0, blk // 16)
+    def _(i):
+        rows = pl.ds(pl.multiple_of(i * 16, 16), 16)
+        d = part[x, rows, :].astype(F32)
+        for g in range(3):
+            d = d + got[g, rows, :].astype(F32)
+        d_in, n = norm_backward(d, tok[rows, :].astype(F32), gain)
+        gtok_o[rows, :] = dhid[rows, :] + d_in
+        sm[0, 5:6, :] += jnp.sum(d * n, axis=0, keepdims=True)
+        sm[0, 6:7, :] += jnp.sum(d, axis=0, keepdims=True)
+
+    p_sc = push(sm.at[0], smc, 53, peer(core=1))
+
+    for copy in p_q1:
+        copy.wait_recv()
+    for c in range(4):
+        ta, tb = wqkv[c, core, z, low].astype(F32), wqkv[y, core, c, high].astype(F32)
+        for g in range(3):
+            ta, tb = ta + qa[g, c].astype(F32), tb + qb[g, c].astype(F32)
+        qs[0, c], qs[1, c] = ta.astype(BF), tb.astype(BF)
+    p_q2 = []
+    for k in (1, 3, 2):
+        tz, ty = lax.rem(z + k, 4), lax.rem(y + k, 4)
+        p_q2.append(push(qs.at[0, ty], qa2.at[k - 1], 53 + k, peer(y=k)))
+        p_q2.append(push(qs.at[1, tz], qb2.at[k - 1], 56 + k, peer(z=k)))
+
+    p_sc.wait_recv()
+    sm[1] = sm[0] + smc[...]
+    p_sz = [push(sm.at[1], smz.at[k - 1], 59 + k, peer(z=k)) for k in (1, 3, 2)]
+
+    for copy in p_o1:
+        copy.wait_recv()
+    for c in range(4):
+        ta, tb = wout[core, c, z, :, left].astype(F32), wout[core, zy, c, :, right].astype(F32)
+        for g in range(3):
+            ta, tb = ta + oa[g, c].astype(F32), tb + ob[g, c].astype(F32)
+        os_[0, c], os_[1, c] = ta.astype(BF), tb.astype(BF)
+    p_o2 = []
+    for k in (1, 3, 2):
+        tz, tyc = lax.rem(z + k, 4), lax.rem(y + k + 3, 4)
+        p_o2.append(push(os_.at[0, tyc], oa2.at[k - 1], 62 + k, peer(y=k)))
+        p_o2.append(push(os_.at[1, tz], ob2.at[k - 1], 65 + k, peer(z=k)))
+
+    for copy in p_sz:
+        copy.wait_recv()
+    sm[2] = sm[1] + smz[0] + smz[1] + smz[2]
+    p_sy = [push(sm.at[2], smy.at[k - 1], 68 + k, peer(y=k)) for k in (1, 3, 2)]
+
+    for copy in p_q2:
+        copy.wait_recv()
+    ta, tb = qs[0, y].astype(F32), qs[1, z].astype(F32)
+    for g in range(3):
+        ta, tb = ta + qa2[g].astype(F32), tb + qb2[g].astype(F32)
+    fq[0:2] = ta.astype(BF).reshape(2, 16, 3 * partw)
+    fq[2:4] = tb.astype(BF).reshape(2, 16, 3 * partw)
+    p_x += [
+        push(fq.at[lax.rem(x + k, 4)], gqkv_o.at[x], 71 + k, peer(x=k)) for k in (1, 3, 2)
+    ]
+    kept.append(load(fq.at[x], gqkv_o.at[x]))
+
+    for copy in p_o2:
+        copy.wait_recv()
+    ta, tb = os_[0, zy].astype(F32), os_[1, z].astype(F32)
+    for g in range(3):
+        ta, tb = ta + oa2[g].astype(F32), tb + ob2[g].astype(F32)
+    fout[:, left], fout[:, right] = ta.astype(BF), tb.astype(BF)
+    p_x.append(push(fout, gout_o, 75, collected()))
+
+    for copy in p_sy:
+        copy.wait_recv()
+    sm[3] = sm[2] + smy[0] + smy[1] + smy[2]
+    p_x += [push(sm.at[3], small_o.at[x], 75 + k, peer(x=k)) for k in (1, 3, 2)]
+    kept.append(load(sm.at[3], small_o.at[x]))
+
+    for copy in p_x:
+        copy.wait_recv()
+    for copy in pending:
+        copy.wait_send()
+
+    @pl.loop(0, 4)
+    def _(j):
+        for copy in sends(j):
+            copy.wait_send()
+        swap(j).wait_send()
+
+    for copy in kept:
+        copy.wait()
+
+
+def attention_backward(
+    collective_id,
+    gain,
+    b_down,
+    ff_small,
+    d_attn,
+    wout,
+    projected,
+    edge,
+    bias,
+    a1,
+    mixed,
+    wqkv,
+    tok,
+    d_hidden,
+    residual,
+    out_part,
+    ff_own,
+    ff_got,
+):
+    blk, width = tok.shape
+    span, partw = mixed.shape
+    hidden = ff_own[0].shape[-1]
+    vmem = pl.BlockSpec(memory_space=pltpu.VMEM)
+    hbm = pl.BlockSpec(memory_space=pl.ANY)
+    outs = [
+        ((blk, width), BF, vmem),
+        ((blk, width), F32, vmem),
+        ((4, 16, 3 * partw), BF, hbm),
+        ((16, width), BF, hbm),
+        ((4, 16, hidden), BF, hbm),
+        ((64, width), BF, hbm),
+        ((4, 8, width), F32, hbm),
+    ]
+    half = width // 2
+    scratch = [
+        ((4, blk, width), BF),
+        ((2, 4, 4, 16, width), BF),
+        ((span, 3 * partw), BF),
+        ((span + W, 2 * partw), BF),
+        (bias.shape, F32),
+        ((span, width), BF),
+        ((span, partw), BF),
+        ((4, 2, 4, 64, 3 * partw), BF),
+        ((blk, width), BF),
+        ((blk, width), F32),
+        ((blk, width), F32),
+        ((blk, width), BF),
+        ((3, blk, width), BF),
+        ((4, 4, 32, width), BF),
+        ((4, 3, 4, 32, width), BF),
+        ((4, 4, 32, width), BF),
+        ((4, 3, 32, width), BF),
+        ((4, 16, hidden), BF),
+        ((64, width), BF),
+        ((span, partw), BF),
+        ((span + W, 2 * partw), F32),
+        ((span, 3 * partw), BF),
+        ((W, 2 * partw), BF),
+        ((W, 2 * partw), BF),
+        ((4, blk, width), BF),
+        ((3, blk, width), BF),
+        ((4, 4, 64, 3 * partw), BF),
+        ((4, 4, 16, width), BF),
+        ((3, 4, 32, 3 * partw), BF),
+        ((3, 4, 32, 3 * partw), BF),
+        ((3, 4, 16, half), BF),
+        ((3, 4, 16, half), BF),
+        ((2, 4, 32, 3 * partw), BF),
+        ((2, 4, 16, half), BF),
+        ((3, 32, 3 * partw), BF),
+        ((3, 32, 3 * partw), BF),
+        ((3, 16, half), BF),
+        ((3, 16, half), BF),
+        ((4, 16, 3 * partw), BF),
+        ((16, width), BF),
+        ((4, 8, width), F32),
+        ((8, width), F32),
+        ((3, 8, width), F32),
+        ((3, 8, width), F32),
+    ]
+    return pl.pallas_call(
+        attention_backward_body,
+        out_shape=tuple(jax.ShapeDtypeStruct(s, d) for s, d, _ in outs),
+        in_specs=[vmem] * 3 + [hbm] * 20,
+        out_specs=tuple(o[2] for o in outs),
+        scratch_shapes=[pltpu.VMEM(s, d) for s, d in scratch]
+        + [
+            pltpu.SemaphoreType.DMA((32,)),
+            pltpu.SemaphoreType.DMA((80,)),
+            pltpu.SemaphoreType.DMA((80,)),
+        ],
+        compiler_params=pltpu.CompilerParams(
+            collective_id=collective_id, has_side_effects=True, vmem_limit_bytes=62 << 20
+        ),
+        name="attention_backward",
+    )(
+        gain.reshape(1, width),
+        b_down.reshape(1, width),
+        ff_small,
+        d_attn,
+        wout,
+        projected,
+        edge,
+        bias,
+        a1,
+        mixed,
+        wqkv,
+        tok,
+        d_hidden,
+        residual,
+        out_part,
+        *ff_own,
+        *ff_got,
+    )
+
+
 def local(
     tokens,
     grad_out,
@@ -773,212 +1278,57 @@
         down_b,
         ff_small,
     ) = feed_forward(3, normed2, residual, dy, gain2, bias_up_own, dy_g, wup_g, wdown_g)
-    up_sa, up_sb = summed(up_a_own, up_a), summed(up_b_own, up_b)
-    down_sa, down_sb = summed(down_a_own, down_a), summed(down_b_own, down_b)
-    d_attn = d_attn_g.reshape(span, width)
-    d_mixed = dot(d_attn, weight_out, NT).astype(BF)
-    d_heads = d_mixed.reshape(4, blk, heads, HEAD)
-    d_probs = jnp.einsum("bqhd,bkhd->bhqk", d_heads, v_heads, preferred_element_type=F32)
-    d_score = (probs * (d_probs - jnp.sum(d_probs * probs, axis=-1, keepdims=True))).astype(BF)
-    d_query = jnp.einsum("bhqk,bkhd->bqhd", d_score, k_heads, preferred_element_type=F32) * scale
-    d_kwin = jnp.einsum("bhqk,bqhd->bkhd", d_score, q_heads, preferred_element_type=F32) * scale
-    d_vwin = jnp.einsum("bhqk,bqhd->bkhd", probs_low, d_heads, preferred_element_type=F32)
-
-    def unwindow(array):
-        array = array.reshape(4, reach, part)
-        total = jnp.zeros((span + W, part), F32)
-        for b in range(4):
-            total = total + jnp.pad(array[b], ((b * blk, span + W - b * blk - reach), (0, 0)))
-        return total
-
-    d_keys, d_values = unwindow(d_kwin), unwindow(d_vwin)
-    d_edge = jnp.concatenate([d_keys[:W], d_values[:W]], axis=1).astype(BF)
-
-    def seventh_body(comm, ins, outs):
-        comm.push(ins[0], outs[0], peer(z=3))
-        reduce_second(comm, ins[1], ins[2], outs[1], outs[2], False)
-        reduce_second(comm, ins[3], ins[4], outs[3], outs[4], True)
-        for p in (1, 2, 3):
-            comm.push(ins[5].at[p], outs[5].at[p - 1], peer(x=-ORDER[p]))
-
-    d_edge_got, up_a2, up_b2, down_a2, down_b2, out_got = exchange(
-        "edge_back",
-        6,
-        seventh_body,
-        lambda: ring("x") + ring("y") + ring("z"),
-        [d_edge, up_sa, up_sb, down_sa, down_sb, out_part],
-        [
-            ((W, 2 * part), BF),
-            ((3, 32, hidden), BF),
-            ((3, 32, hidden), BF),
-            ((3, 32, width), BF),
-            ((3, 32, width), BF),
-            ((3, blk, width), BF),
-        ],
+    bias = jnp.where(visible, 0.0, NEG_FILL).astype(F32)
+    out, grad_tokens, qkv_x, g_out_own, up_x, g_down_own, small_x = attention_backward(
+        4,
+        gain1,
+        bias_down,
+        ff_small,
+        d_attn_g,
+        wout_g,
+        projected,
+        edge_kv,
+        bias,
+        normed1,
+        mixed,
+        wqkv_g,
+        tok,
+        d_hidden,
+        residual,
+        out_part,
+        (up_a_own, up_b_own, down_a_own, down_b_own),
+        (up_a, up_b, down_a, down_b),
     )
-    out = residual + out_part[0].astype(F32) + out_got.astype(F32).sum(0) + bias_down
-    up_f = after_second(up_sa, up_sb, up_a2, up_b2, False)
-    down_f = after_second(down_sa, down_sb, down_a2, down_b2, True)
-    d_kv = jnp.concatenate([d_keys[W:], d_values[W:]], axis=1)
-    d_kv = d_kv + jnp.pad(d_edge_got.astype(F32), ((span - W, 0), (0, 0)))
-    d_qkv = jnp.concatenate([d_query.reshape(span, part), d_kv], axis=1).astype(BF)
-    d_a1_part = dot(d_qkv, weight_qkv, NT).reshape(4, blk, width)
-    g_wqkv = dot(normed1, d_qkv, TN).astype(BF).reshape(4, 2, 4, 64, 3 * part)
-    g_wout = dot(mixed, d_attn, TN).astype(BF).reshape(2, 4, 4, 16, width)
-    g_bqkv = jnp.sum(d_qkv.astype(F32), axis=0)
-
-    def eighth_body(comm, ins, outs):
-        split_x(comm, ins[0], outs[0])
-        swap_cores(comm, ins[1], outs[1], False)
-        swap_cores(comm, ins[2], outs[2], True)
-        split_x(comm, ins[3], outs[3])
-        comm.push(ins[4], outs[4], collected())
-
-    d_a1_got, qkv_c, wout_c, up_x, g_down_own = exchange(
-        "sum_d_a1",
-        7,
-        eighth_body,
-        lambda: ring("x") + near() + [scattered(), collected()],
-        [d_a1_part.astype(BF), g_wqkv, g_wout, up_f.reshape(4, 16, hidden), down_f],
-        [
-            ((3, blk, width), BF),
-            ((4, 4, 64, 3 * part), BF),
-            ((4, 4, 16, width), BF),
-            ((3, 16, hidden), BF),
-            ((64, width), BF),
-        ],
+
+    def columns(parts, groups):
+        parts = parts.reshape(4, 16, groups, -1)
+        return parts.transpose(1, 2, 0, 3).reshape(16, -1).astype(F32)
+
+    me = coords()
+    device = ((me["y"] * 2 + me["core"]) * 4 + me["z"]) * 4 + me["x"]
+    shared = small_x.sum(0)
+
+    def mine(vector, size):
+        return lax.dynamic_slice_in_dim(vector, device * size, size)
+
+    g_bqv = jnp.concatenate(
+        [small_x[:, 7, :part].reshape(width), small_x[:, 7, 2 * part : 3 * part].reshape(width)]
     )
-    d_a1 = pick(d_a1_part, x_at) + d_a1_got.astype(F32).sum(0)
-    d_in, g_gain1, g_shift1 = jax.vjp(layer_norm, own_tok, gain1, shift1)[1](d_a1)
-    grad_tokens = d_hidden + d_in
-    qkv_s, wout_s = after_cores(g_wqkv, qkv_c, False), after_cores(g_wout, wout_c, True)
-
-    def placed(vector, offset, whole):
-        return lax.dynamic_update_slice(jnp.zeros((whole,), F32), vector, (offset,))
-
-    g_bqv = placed(g_bqkv[:part], x_at * part, 2 * width) + placed(
-        g_bqkv[2 * part :], width + x_at * part, 2 * width
-    )
-    g_small = jnp.concatenate(
-        [
-            v.reshape(128, -1)
-            for v in (
-                g_gain1,
-                g_shift1,
-                g_bqv,
-                ff_small[2],
-                ff_small[0],
-                ff_small[1],
-                placed(ff_small[3], x_at * hidden, 4 * hidden),
-                ff_small[4],
-            )
-        ],
-        axis=1,
-    )
-    g_small = jnp.pad(g_small, ((0, 0), (0, 256 - g_small.shape[1]))).reshape(4, 2, 4, 8, 128)
-
-    def ninth_body(comm, ins, outs):
-        reduce_first(comm, ins[0], outs[0], outs[1], False)
-        reduce_first(comm, ins[1], outs[2], outs[3], True)
-        me = coords()
-        for k in range(1, 8):
-            c, zz = lax.rem(me["core"] + k // 4, 2), lax.rem(me["z"] + k % 4, 4)
-            comm.push(ins[2].at[:, c, zz], outs[4].at[k - 1], (me["y"], c, zz, me["x"]))
-
-    def across():
-        me = coords()
-        return [
-            (me["y"], lax.rem(me["core"] + k // 4, 2), lax.rem(me["z"] + k % 4, 4), me["x"])
-            for k in range(1, 8)
-        ]
-
-    qkv_a, qkv_b, wout_a, wout_b, small_a = exchange(
-        "reduce_attn_1",
-        8,
-        ninth_body,
-        lambda: ring("y") + across(),
-        [qkv_s, wout_s, g_small],
-        [
-            ((3, 4, 32, 3 * part), BF),
-            ((3, 4, 32, 3 * part), BF),
-            ((3, 4, 16, width // 2), BF),
-            ((3, 4, 16, width // 2), BF),
-            ((7, 4, 8, 128), F32),
-        ],
-    )
-    qkv_sa, qkv_sb = after_first(qkv_s, qkv_a, qkv_b, False)
-    wout_sa, wout_sb = after_first(wout_s, wout_a, wout_b, True)
-    small_s = pick(pick(g_small, lax.axis_index("core"), 1), z_at, 1) + small_a.sum(0)
-
-    def tenth_body(comm, ins, outs):
-        reduce_second(comm, ins[0], ins[1], outs[0], outs[1], False)
-        reduce_second(comm, ins[2], ins[3], outs[2], outs[3], True)
-        y = lax.axis_index("y")
-        for k in (1, 3, 2):
-            comm.push(ins[4].at[lax.rem(y + k, 4)], outs[4].at[k - 1], peer(y=k))
-
-    qkv_a2, qkv_b2, wout_a2, wout_b2, small_b = exchange(
-        "reduce_attn_2",
-        9,
-        tenth_body,
-        lambda: ring("y") + ring("z"),
-        [qkv_sa, qkv_sb, wout_sa, wout_sb, small_s],
-        [
-            ((3, 32, 3 * part), BF),
-            ((3, 32, 3 * part), BF),
-            ((3, 16, width // 2), BF),
-            ((3, 16, width // 2), BF),
-            ((3, 8, 128), F32),
-        ],
-    )
-    qkv_f = after_second(qkv_sa, qkv_sb, qkv_a2, qkv_b2, False)
-    wout_f = after_second(wout_sa, wout_sb, wout_a2, wout_b2, True)
-    small_f = pick(small_s, lax.axis_index("y")) + small_b.sum(0)
-
-    def last_body(comm, ins, outs):
-        split_x(comm, ins[0], outs[0])
-        comm.push(ins[1], outs[1], collected())
-        for k in (1, 3, 2):
-            comm.push(ins[2], outs[2].at[k - 1], peer(x=k))
-
-    qkv_x, g_out_own, small_x = exchange(
-        "hand_back",
-        10,
-        last_body,
-        lambda: ring("x") + [scattered(), collected()],
-        [qkv_f.reshape(4, 16, 3 * part), wout_f, small_f],
-        [((3, 16, 3 * part), BF), ((16, width), BF), ((3, 8, 128), F32)],
-    )
-
-    def columns(own, received, groups):
-        every = jnp.concatenate([received, pick(own, x_at)[None]])
-        order = jnp.stack([lax.rem(x_at - s + 7, 4) for s in range(4)])
-        every = jnp.take(every, order, axis=0).reshape(4, 16, groups, -1)
-        return every.transpose(1, 2, 0, 3).reshape(16, -1).astype(F32)
-
-    g_qkv_own = columns(qkv_f.reshape(4, 16, 3 * part), qkv_x, 3)
-    g_up_own = columns(up_f.reshape(4, 16, hidden), up_x, 1)
-    small_all = (small_f + small_x.sum(0)).reshape(4, 256)
-    mine = pick(small_all, x_at)
-    cuts, start = [], 0
-    for size in (16, 16, 32, 16, 16, 16, 64, 16):
-        cuts.append(mine[start : start + size])
-        start += size
     return (
-        out.astype(BF).reshape(1, blk, width),
+        out.reshape(1, blk, width),
         grad_tokens.reshape(1, blk, width),
-        cuts[0],
-        cuts[1],
-        g_qkv_own,
-        cuts[2],
+        mine(shared[5], 16),
+        mine(shared[6], 16),
+        columns(qkv_x, 3),
+        mine(g_bqv, 32),
         g_out_own.astype(F32),
-        cuts[3],
-        cuts[4],
-        cuts[5],
-        g_up_own,
-        cuts[6],
+        mine(shared[2], 16),
+        mine(shared[0], 16),
+        mine(shared[1], 16),
+        columns(up_x, 1),
+        mine(small_x[:, 3].reshape(4 * hidden), 64),
         g_down_own.astype(F32),
-        cuts[7],
+        mine(shared[4], 16),
     )
 
 

time: 612 us -> 459 us (0.75); the launches traced: 600 us -> 459 us
  other arithmetic: 72.7 us -> 22.7 us
  Pallas kernels: 414 us -> 378 us
  local copies, waits for them, and re-layouts: 73.2 us -> 41 us
  matrix products: 38.1 us -> 16 us
    pallas_call x8 -> x3, Pallas kernels: 310 us -> 181 us  [exchange(): pl.pallas_call(kernel, out_shape=tuple((jax.ShapeDtypeStruct(s, d) for s,...]
    pallas_call x0 -> x1, Pallas kernels: none -> 92.9 us  [attention_backward(): pl.pallas_call(attention_backward_body, out_shape=tuple((jax.ShapeDtypeSt...]
    convert_element_type x14 -> x1, other arithmetic: 20.5 us -> 0.04 us  [columns(): return parts.transpose(1, 2, 0, 3).reshape(16, -1).astype(F32)]
    dot_general x6 -> x2, matrix products: 30.5 us -> 10.7 us  [dot(): return lax.dot_general(a, b, (dims, ((), ())), preferred_element_type=F32)]
    squeeze x9 -> x0, local copies, waits for them, and re-layouts: 15 us -> none  [the longest x8 14.9 us: unwindow(): array[b]]
    reduce_sum x24 -> x1, other arithmetic: 12.8 us -> 1.03 us  [local(): shared = small_x.sum(0)]
    another operation x10 -> x1, other arithmetic: 9.88 us -> 0.18 us
    add x6 -> x0, other arithmetic: 6.88 us -> none  [the longest x2 4.11 us: unwindow(): total + jnp.pad(array[b], ((b * blk, span + W - b * blk - reach), (0, 0)))]
where the time goes in v3:
time: 459 us
  Pallas kernels  378 us (82%)
  local copies, waits for them, and re-layouts  41 us (9%)
  other arithmetic  22.7 us (5%)
  matrix products  16 us (3%)
    pallas_call x3, Pallas kernels, exchange(): pl.pallas_call(kernel, out_shape=tuple((jax.ShapeDtypeStruct(s, d) for s,...  181 us
    pallas_call x1, Pallas kernels, feed_forward(): pl.pallas_call(feed_forward_body, out_shape=tuple((jax.ShapeDtypeStruct(s...  104 us
    pallas_call x1, Pallas kernels, attention_backward(): pl.pallas_call(attention_backward_body, out_shape=tuple((jax.ShapeDtypeSt...  92.9 us
    dot_general x2, matrix products, dot(): return lax.dot_general(a, b, (dims, ((), ())), preferred_element_type=F32)  10.7 us
    another operation x20, local copies, waits for them, and re-layouts, windows(): return jnp.stack([array[b * blk:b * blk + reach] for b in range(4)])  9.56 us

profile of v3, /device:TPU:1, one launch (start us, length us, event | category | flops | bytes accessed | tf_op | source)
XLA Modules:
  0.0 458.6 jit_solution(16589434100224190047)
XLA Ops:
  0.7 5.4 %concatenate.21 = bf16[192]{0:T(256)(128)(2,1)S(1)} concatenate(bf16[16]{0:T(256)(128)(2,1)} %param.18, bf16[16]{0:T(256)(128)(2,1)} %param.19, bf16[32]{0:T(256)(128)(2,1)} %param.21, bf16[16]{0:T(256)(128)(2,1)} %param.23, bf16[16]{0:T(256)(128)(2,1)} %param.24, bf16[16]{0:T(256)(128)(2,1)} %param.25, bf16[64]{0:T(256)(128)(2,1)} %param.27, bf16[16]{0:T(256)(128)(2,1)} %param.29), dimensions={0} | concatenate | bytes 768 | tf_op jit(solution)/shard_map/concatenate | solution.py:1122
  6.7 1.1 reshape.291
  7.9 0.9 reshape.292.refs_3_
  8.8 60.8 %gather_attn.1 = (bf16[4,128,2048]{2,1,0:T(8,128)(2,1)}, f32[4,2,4,4,8,128]{5,4,3,2,1,0:T(8,128)}, bf16[4,128,2048]{2,1,0:T(8,128)(2,1)}, bf16[4,2,4,64,1536]{4,...) custom-call(bf16[128,2048]{1,0:T(8,128)(2,1)} %bitcast.100, bf16[128,2048]{1,0:T(8,128)(2,1)} %bitcast.104, ...), custom_call_target="tpu_custom_call" | custom-call | tf_op jit(solution)/shard_map/gather_attn/pallas_call | solution.py:91
  69.7 1.3 copy.104
  71.0 0.8 fusion.53
  74.4 1.0 fusion.32
  77.8 2.1 add_convert_fusion
  80.2 6.8 %fusion.4.refs_0_.proj_hbm = bf16[512,1536]{1,0:T(8,128)(2,1)S(1)} fusion(bf16[512,2048]{1,0:T(8,128)(2,1)} %bitcast.103, bf16[2048,1536]{1,0:T(8,128)(2,1)} %bitcast.99, f32[1536]{0:T(1024)S(1)} %pad_maximum_fusion.2), kind=kOutput, calls=%fused_computation.13 | convolution fusion | flops 3222798336 | bytes 9967616 | tf_op jit(solution)/shard_map/dot_general | solution.py:275
  87.1 0.9 fusion.52
  88.1 0.8 copy.80
  89.0 0.8 copy.79
  89.8 0.7 copy.105
  90.5 67.0 %edge_and_up.1 = (bf16[256,1024]{1,0:T(8,128)(2,1)}, bf16[4,2,4,64,2048]{4,3,2,1,0:T(8,128)(2,1)}, bf16[2,4,4,64,2048]{4,3,2,1,0:T(8,128)(2,1)}) custom-call(bf16[512,1536]{1,0:T(8,128)(2,1)} %copy-done.2, bf16[4,16,2048]{2,1,0:T(8,128)(2,1)} %bitcast.116, bf16[64,2048]{1,0:T(8,128)(2,1)} %refs_2_.1), custom_call_target="tpu_custom_call" | custom-call | tf_op jit(solution)/shard_map/edge_and_up/pallas_call | solution.py:91
  157.4 1.1 fusion.54
  158.6 1.0 fusion.34
  159.8 0.8 copy.78
  160.7 0.8 copy.77
  161.5 0.9 reshape.299
  162.4 2.5 fusion.5
  164.9 1.1 exponential_reduce_fusion
  166.7 1.9 copy.90
  168.6 0.9 copy.89
  169.5 1.2 copy.88
  170.7 1.9 copy.87
  172.6 2.8 fusion.26
  175.4 3.9 fusion.60
  179.4 52.8 %sum_attn_and_down.1 = (bf16[3,128,2048]{2,1,0:T(8,128)(2,1)}, bf16[2,4,4,64,2048]{4,3,2,1,0:T(8,128)(2,1)}) custom-call(bf16[4,128,2048]{2,1,0:T(8,128)(2,1)} %get-tuple-element.119.refs_0_, bf16[2,4,4,64,2048]{4,3,2,1,0:T(8,128)(2,1)} %get-tuple-element.48.refs_1_), custom_call_target="tpu_custom_call" | custom-call | tf_op jit(solution)/shard_map/sum_attn_and_down/pallas_call | solution.py:91
  232.2 1.8 convert_reduce_fusion.1
  234.0 1.5 fusion.49
  236.0 1.1 add_convert_fusion.1.a2_in
  237.0 0.7 broadcast_in_dim_reshape.2.gain_in
  237.7 1.0 slice.174
  239.4 104.0 %feed_forward.1 = (bf16[4,128,2048]{2,1,0:T(8,128)(2,1)}, f32[128,2048]{1,0:T(8,128)}, bf16[4,128,2048]{2,1,0:T(8,128)(2,1)}, bf16[4,32,2048]{2,1,0:T(8,128)(2,1...) custom-call(bf16[128,2048]{1,0:T(8,128)(2,1)} %add_convert_fusion.1., ...), custom_call_target="tpu_custom_call" | custom-call | tf_op jit(solution)/shard_map/feed_forward/pallas_call | solution.py:572
  343.5 1.2 broadcast_select_fusion.bias_hbm
  344.8 3.8 fusion.3.a1_hbm
  348.8 0.9 copy.103
  349.7 92.9 %attention_backward.1 = (bf16[128,2048]{1,0:T(8,128)(2,1)}, f32[128,2048]{1,0:T(8,128)}, bf16[4,16,1536]{2,1,0:T(8,128)(2,1)}, bf16[16,2048]{1,0:T(8,128)(2,1)},...) custom-call(f32[1,2048]{1,0:T(1,128)} %reshape_reshape.7.gain_in, ...), custom_call_target="tpu_custom_call" | custom-call | tf_op jit(solution)/shard_map/attention_backward/pallas_call | solution.py:1059
  442.7 1.0 reduce_sum.89
  444.9 1.3 reshape.310
  446.5 1.0 reshape.308
  447.6 0.9 fusion.55
  449.1 1.5 convert_element_type.106
  452.7 1.1 copy.94
  453.8 1.0 slice.154
  455.4 0.8 convert_element_type.111
  456.8 0.8 copy.109
  457.6 1.0 copy.110
  (122 shorter events, 13.8 us)
Async XLA Ops:
  0.6 73.3 %copy-start.30 = (s32[1,4]{1,0:T(1,128)S(1)}, s32[1,4]{1,0:T(1,128)}, u32[]{:S(2)}) copy-start(s32[1,4]{1,0:T(1,128)} %param.17) | copy-start | bytes 52
  69.7 5.9 %copy-start = (bf16[4,128,2048]{2,1,0:T(8,128)(2,1)S(1)}, bf16[4,128,2048]{2,1,0:T(8,128)(2,1)}, u32[]{:S(2)}) copy-start(bf16[4,128,2048]{2,1,0:T(8,128)(2,1)} %get-tuple-element.44) | copy-start | bytes 6291460
  71.0 9.0 %copy-start.8 = (f32[16,8,8,128]{3,1,2,0:T(8,128)}, f32[16,8,8,128]{3,1,2,0:T(8,128)S(1)}, u32[]{:S(2)}) copy-start(f32[16,8,8,128]{3,1,2,0:T(8,128)S(1)} %copy.104) | copy-start | bytes 1572868
  73.8 6.1 %copy-start.22 = (s32[4,128]{1,0:T(4,128)}, s32[4,128]{1,0:T(4,128)S(1)}, u32[]{:S(2)}) copy-start(s32[4,128]{1,0:T(4,128)S(1)} %add_add_fusion) | copy-start | bytes 6148
  73.9 6.0 %copy-start.17 = (s32[4,384]{1,0:T(4,128)}, s32[4,384]{1,0:T(4,128)S(1)}, u32[]{:S(2)}) copy-start(s32[4,384]{1,0:T(4,128)S(1)} %get-tuple-element.75) | copy-start | bytes 18436
  73.9 6.0 %copy-start.26 = (pred[4,384]{1,0:T(4,128)(4,1)}, pred[4,384]{1,0:T(4,128)(4,1)S(1)}, u32[]{:S(2)}) copy-start(pred[4,384]{1,0:T(4,128)(4,1)S(1)} %get-tuple-element.74) | copy-start | bytes 4612
  74.3 1.1 copy-start.19
  74.4 5.5 %copy-start.24 = (s32[512]{0:T(512)}, s32[512]{0:T(512)S(1)}, u32[]{:S(2)}) copy-start(s32[512]{0:T(512)S(1)} %convert_reduce_fusion.3) | copy-start | bytes 6148
  87.1 2.7 copy-start.2
  87.1 2.7 copy-start.16
  89.8 68.8 %copy-start.3 = (bf16[512,1536]{1,0:T(8,128)(2,1)S(1)}, bf16[512,1536]{1,0:T(8,128)(2,1)}, u32[]{:S(2)}) copy-start(bf16[512,1536]{1,0:T(8,128)(2,1)} %copy-done.2) | copy-start | bytes 4718596
  162.4 2.5 copy-start.10
  172.6 2.8 copy-start.4
  175.4 3.9 copy-start.6
  179.4 54.6 %copy-start.5 = (bf16[1,128,2048]{2,1,0:T(8,128)(2,1)S(1)}, bf16[1,128,2048]{2,1,0:T(8,128)(2,1)}, u32[]{:S(2)}) copy-start(bf16[1,128,2048]{2,1,0:T(8,128)(2,1)} %param.15) | copy-start | bytes 1572868
  179.4 54.6 %copy-start.21 = (f32[2048]{0:T(1024)S(1)}, f32[2048]{0:T(1024)}, u32[]{:S(2)}) copy-start(f32[2048]{0:T(1024)} %add.177) | copy-start | bytes 24580
  232.2 3.3 copy-start.15
  232.2 3.4 copy-start.11
  235.5 3.9 copy-start.1
  239.4 104.1 %copy-start.18 = (s32[4,384]{1,0:T(4,128)S(1)}, s32[4,384]{1,0:T(4,128)}, u32[]{:S(2)}) copy-start(s32[4,384]{1,0:T(4,128)} %copy-done.17) | copy-start | bytes 18436
  239.4 104.1 %copy-start.20 = (s32[4,384]{1,0:T(4,128)S(1)}, s32[4,384]{1,0:T(4,128)}, u32[]{:S(2)}) copy-start(s32[4,384]{1,0:T(4,128)} %copy-done.19) | copy-start | bytes 18436
  239.4 104.1 %copy-start.23 = (s32[4,128]{1,0:T(4,128)S(1)}, s32[4,128]{1,0:T(4,128)}, u32[]{:S(2)}) copy-start(s32[4,128]{1,0:T(4,128)} %copy-done.22) | copy-start | bytes 6148
  239.4 104.1 %copy-start.25 = (s32[512]{0:T(512)S(1)}, s32[512]{0:T(512)}, u32[]{:S(2)}) copy-start(s32[512]{0:T(512)} %copy-done.24) | copy-start | bytes 6148
  239.4 104.1 %copy-start.27 = (pred[4,384]{1,0:T(4,128)(4,1)S(1)}, pred[4,384]{1,0:T(4,128)(4,1)}, u32[]{:S(2)}) copy-start(pred[4,384]{1,0:T(4,128)(4,1)} %copy-done.26) | copy-start | bytes 4612
  239.4 105.3 %copy-start.28 = (f32[512]{0:T(512)S(1)}, f32[512]{0:T(512)}, u32[]{:S(2)}) copy-start(f32[512]{0:T(512)} %get-tuple-element.113) | copy-start | bytes 6148
  239.4 105.3 %copy-start.29 = (f32[512]{0:T(512)S(1)}, f32[512]{0:T(512)}, u32[]{:S(2)}) copy-start(f32[512]{0:T(512)} %get-tuple-element.115) | copy-start | bytes 6148
  343.5 5.1 %copy-start.7 = (bf16[4,4,128,128]{3,2,1,0:T(8,128)(2,1)S(1)}, bf16[4,4,128,128]{3,2,1,0:T(8,128)(2,1)}, u32[]{:S(2)}) copy-start(bf16[4,4,128,128]{3,2,1,0:T(8,128)(2,1)} %copy-done.6) | copy-start | bytes 1572868
  442.7 9.6 %copy-start.14 = (bf16[4,16,2048]{2,1,0:T(8,128)(2,1)S(1)}, bf16[4,16,2048]{2,1,0:T(8,128)(2,1)}, u32[]{:S(2)}) copy-start(bf16[4,16,2048]{2,1,0:T(8,128)(2,1)} %get-tuple-element.70) | copy-start | bytes 786436
  442.7 12.7 %copy-start.13 = (bf16[64,2048]{1,0:T(8,128)(2,1)S(1)}, bf16[64,2048]{1,0:T(8,128)(2,1)}, u32[]{:S(2)}) copy-start(bf16[64,2048]{1,0:T(8,128)(2,1)} %get-tuple-element.71) | copy-start | bytes 786436
  444.9 11.8 %copy-start.12 = (bf16[128,2048]{1,0:T(8,128)(2,1)S(1)}, bf16[128,2048]{1,0:T(8,128)(2,1)}, u32[]{:S(2)}) copy-start(bf16[128,2048]{1,0:T(8,128)(2,1)} %get-tuple-element.65) | copy-start | bytes 1572868
  446.5 11.0 %copy-start.9 = (f32[128,2048]{1,0:T(8,128)S(1)}, f32[128,2048]{1,0:T(8,128)}, u32[]{:S(2)}) copy-start(f32[128,2048]{1,0:T(8,128)} %get-tuple-element.66) | copy-start | bytes 3145732

commit v4 on v3

--- a/solution.py
+++ b/solution.py
@@ -18,7 +18,7 @@
 SIZE = {"y": 4, "core": 2, "z": 4, "x": 4}
 BF = jnp.bfloat16
 F32 = jnp.float32
-SEMS = 96
+SEMS = 160
 
 
 def coords():
@@ -67,9 +67,10 @@
 
     def drain(self):
         self.arrived(self.open)
-        for copy, remote, _ in self.open:
-            if remote:
+        for copy, remote_copy, _ in self.open:
+            if remote_copy:
                 copy.wait_send()
+        self.open = []
 
 
 def greet(devices):
@@ -79,32 +80,16 @@
     pl.semaphore_wait(barrier, len(devices))
 
 
-def exchange(name, collective_id, body, peers, ins, outs):
-    def kernel(*refs):
-        in_refs = refs[: len(ins)]
-        out_refs = refs[len(ins) : len(ins) + len(outs)]
-        comm = Comm(*refs[len(ins) + len(outs) :])
-        greet(peers())
-        body(comm, in_refs, out_refs)
-        comm.drain()
-
-    return pl.pallas_call(
-        kernel,
-        out_shape=tuple(jax.ShapeDtypeStruct(s, d) for s, d in outs),
-        in_specs=[pl.BlockSpec(memory_space=pl.ANY)] * len(ins),
-        out_specs=tuple(pl.BlockSpec(memory_space=pl.ANY) for _ in outs),
-        scratch_shapes=[pltpu.SemaphoreType.DMA((SEMS,)), pltpu.SemaphoreType.DMA((SEMS,))],
-        compiler_params=pltpu.CompilerParams(collective_id=collective_id, has_side_effects=True),
-        name=name,
-    )(*ins)
-
-
 def ring(axis):
     return [peer(**{axis: k}) for k in (1, 3, 2)]
 
 
 def near():
     return [peer(core=1)]
+
+
+def everyone():
+    return ring("x") + ring("y") + ring("z") + near()
 
 
 def scattered():
@@ -117,158 +102,90 @@
     return (me["x"], me["core"], lax.rem(me["y"] + 3, 4), me["z"])
 
 
-def spread_x(comm, src, dst):
-    x = lax.axis_index("x")
-    sent = [comm.push(src, dst.at[x], to) for to in ring("x")]
-    return sent + [comm.local(src, dst.at[x])]
-
-
-def split_x(comm, src, dst):
-    x = lax.axis_index("x")
-    return [
-        comm.push(src.at[lax.rem(x + k, 4)], dst.at[k - 1], peer(x=k)) for k in (1, 3, 2)
-    ]
-
-
-def halves(rows, cols):
+class Relay:
+    def __init__(self, comm, axis, full, half):
+        self.comm, self.axis, self.full, self.half = comm, axis, full, half
+        self.me = lax.axis_index(axis)
+
+    def to(self, k):
+        return peer(**{self.axis: k})
+
+    def start(self, src=None):
+        own = self.full(self.me)
+        src = own if src is None else src
+        self.sent = [self.comm.push(src, own, self.to(1)), self.comm.push(src, own, self.to(3))]
+
+    def near(self):
+        self.comm.arrived(self.sent)
+        before, after = lax.rem(self.me + 3, 4), lax.rem(self.me + 1, 4)
+        up, down = self.half(before, 0), self.half(after, 1)
+        self.passed = [self.comm.push(up, up, self.to(1)), self.comm.push(down, down, self.to(3))]
+
+    def far(self):
+        self.comm.arrived(self.passed)
+
+
+class Gather:
+    def __init__(self, comm, w, by_core, cut):
+        self.comm, self.w, self.by_core, self.cut = comm, w, by_core, cut
+        me = coords()
+        self.y, self.core, self.z = me["y"], me["core"], me["z"]
+
+    def slot(self, y, z, cut):
+        place = (self.core, y, z) if self.by_core else (y, self.core, z)
+        return self.w.at[place + self.cut[cut]]
+
+    def row(self, y):
+        return lax.rem(y + 3, 4) if self.by_core else y
+
+    def first(self):
+        a = self.slot(self.row(self.y), self.z, 0)
+        b = self.slot(self.row(self.y), self.z, 1)
+        self.one = [self.comm.push(a, a, to) for to in ring("z")]
+        self.one += [self.comm.push(b, b, to) for to in ring("y")]
+
+    def second(self, src_a=None, src_b=None):
+        every = slice(None)
+        self.a = Relay(
+            self.comm,
+            "y",
+            lambda o: self.slot(self.row(o), every, 0),
+            lambda o, h: self.slot(self.row(o), pl.ds(2 * h, 2), 0),
+        )
+        self.b = Relay(
+            self.comm,
+            "z",
+            lambda o: self.slot(every, o, 1),
+            lambda o, h: self.slot(pl.ds(2 * h, 2), o, 1),
+        )
+        self.a.start(src_a)
+        self.b.start(src_b)
+
+    def across(self, k):
+        a, b = self.a.full(lax.rem(self.y + k, 4)), self.b.full(lax.rem(self.z + k, 4))
+        return [self.comm.push(a, a, peer(core=1)), self.comm.push(b, b, peer(core=1))]
+
+    def near(self):
+        self.a.near()
+        self.b.near()
+        self.two = self.across(0) + self.across(1) + self.across(3)
+
+    def far(self):
+        self.a.far()
+        self.b.far()
+        self.two += self.across(2)
+
+    def done(self):
+        self.comm.arrived(self.two)
+
+
+def by_rows(rows):
+    return [(slice(0, rows // 2),), (slice(rows // 2, rows),)]
+
+
+def by_columns(columns):
     every = slice(None)
-    if rows >= 32:
-        return [(slice(0, rows // 2), every), (slice(rows // 2, rows), every)]
-    return [(every, slice(0, cols // 2)), (every, slice(cols // 2, cols))]
-
-
-class Gather:
-    def __init__(self, comm, w, by_core):
-        self.comm, self.w, self.by_core = comm, w, by_core
-        self.cut = halves(*w.shape[3:])
-
-    def at(self, y, core, z, half):
-        slot = (core, y, z) if self.by_core else (y, core, z)
-        return self.w.at[slot + self.cut[half]]
-
-    def place(self):
-        me = coords()
-        y = lax.rem(me["y"] + 3, 4) if self.by_core else me["y"]
-        return y, me["core"], me["z"]
-
-    def first(self):
-        y, c, z = self.place()
-        a, b = self.at(y, c, z, 0), self.at(y, c, z, 1)
-        self.a = [self.comm.push(a, a, to) for to in ring("z")]
-        self.b = [self.comm.push(b, b, to) for to in ring("y")]
-
-    def second(self):
-        y, c, z = self.place()
-        every = slice(None)
-        self.comm.arrived(self.a)
-        a = self.at(y, c, every, 0)
-        self.a2 = [self.comm.push(a, a, to) for to in ring("y")]
-        self.comm.arrived(self.b)
-        b = self.at(every, c, z, 1)
-        self.b2 = [self.comm.push(b, b, to) for to in ring("z")]
-
-    def third(self):
-        _, c, _ = self.place()
-        every = slice(None)
-        self.comm.arrived(self.a2)
-        a = self.at(every, c, every, 0)
-        self.comm.push(a, a, peer(core=1))
-        self.comm.arrived(self.b2)
-        b = self.at(every, c, every, 1)
-        self.comm.push(b, b, peer(core=1))
-
-
-def gather_peers():
-    return ring("x") + ring("y") + ring("z") + near()
-
-
-def into_slot(comm, src, w):
-    me = coords()
-    slot = w.at[me["y"], me["core"], me["z"], pl.ds(me["x"] * 16, 16)]
-    sent = [
-        comm.push(src.at[lax.rem(me["x"] + k, 4)], slot, peer(x=k)) for k in (1, 3, 2)
-    ]
-    return sent + [comm.local(src.at[me["x"]], slot)]
-
-
-def into_scattered(comm, src, w):
-    me = coords()
-    return [comm.push(src, w.at[me["core"], me["z"], me["x"]], scattered())]
-
-
-def swap_cores(comm, g, dst, by_core):
-    other = 1 - lax.axis_index("core")
-    src = g.at[other] if by_core else g.at[:, other]
-    return [comm.push(src, dst, peer(core=1))]
-
-
-def reduce_first(comm, s, dst_a, dst_b, by_core):
-    y, z = lax.axis_index("y"), lax.axis_index("z")
-    cut = halves(*s.shape[2:])
-    for k in (1, 3, 2):
-        to = lax.rem(z + k, 4)
-        comm.push(s.at[(slice(None), to) + cut[0]], dst_a.at[k - 1], peer(z=k))
-    for k in (1, 3, 2):
-        to = lax.rem(y + k + (3 if by_core else 0), 4)
-        comm.push(s.at[(to, slice(None)) + cut[1]], dst_b.at[k - 1], peer(y=k))
-
-
-def reduce_second(comm, sa, sb, dst_a, dst_b, by_core):
-    y, z = lax.axis_index("y"), lax.axis_index("z")
-    for k in (1, 3, 2):
-        to = lax.rem(y + k + (3 if by_core else 0), 4)
-        comm.push(sa.at[to], dst_a.at[k - 1], peer(y=k))
-    for k in (1, 3, 2):
-        comm.push(sb.at[lax.rem(z + k, 4)], dst_b.at[k - 1], peer(z=k))
-
-
-def pick(array, index, axis=0):
-    return lax.dynamic_index_in_dim(array, index, axis, keepdims=False)
-
-
-def after_cores(g, received, by_core):
-    own = pick(g, lax.axis_index("core"), 0 if by_core else 1)
-    return (own.astype(F32) + received.astype(F32)).astype(BF)
-
-
-def slot_y(by_core):
-    y = lax.axis_index("y")
-    return lax.rem(y + 3, 4) if by_core else y
-
-
-def after_first(s, ra, rb, by_core):
-    every = slice(None)
-    cut = halves(*s.shape[2:])
-    own_a = pick(s[(every, every) + cut[0]], lax.axis_index("z"), 1).astype(F32)
-    own_b = pick(s[(every, every) + cut[1]], slot_y(by_core), 0).astype(F32)
-    return (
-        (own_a + ra.astype(F32).sum(0)).astype(BF),
-        (own_b + rb.astype(F32).sum(0)).astype(BF),
-    )
-
-
-def summed(own, received):
-    return (own.astype(F32) + received.astype(F32).sum(0)).astype(BF)
-
-
-def after_second(sa, sb, ra, rb, by_core):
-    own_a = pick(sa, slot_y(by_core)).astype(F32)
-    own_b = pick(sb, lax.axis_index("z")).astype(F32)
-    return jnp.concatenate(
-        [own_a + ra.astype(F32).sum(0), own_b + rb.astype(F32).sum(0)],
-        axis=0 if sa.shape[1] == 32 else 1,
-    ).astype(BF)
-
-
-def layer_norm(values, gain, shift):
-    center = jnp.mean(values, axis=-1, keepdims=True)
-    centred = values - center
-    spread = jnp.mean(centred * centred, axis=-1, keepdims=True)
-    return centred * lax.rsqrt(spread + EPSILON) * gain + shift
-
-
-def doc_number(positions, doc_ends):
-    return jnp.sum((doc_ends[None, :] <= positions[:, None]).astype(jnp.int32), axis=1)
+    return [(every, slice(0, columns // 2)), (every, slice(columns // 2, columns))]
 
 
 def dot(a, b, dims):
@@ -278,6 +195,325 @@
 NN = ((1,), (0,))
 NT = ((1,), (1,))
 TN = ((0,), (0,))
+
+
+def mask_of(lengths, first, blk, reach):
+    q = first + lax.broadcasted_iota(jnp.int32, (blk, reach), 0)
+    k = first - W + lax.broadcasted_iota(jnp.int32, (blk, reach), 1)
+    q_doc, k_doc = jnp.zeros((blk, reach), jnp.int32), jnp.zeros((blk, reach), jnp.int32)
+    end = 0
+    for i in range(lengths.shape[1]):
+        end = end + lengths[0, i]
+        q_doc = q_doc + jnp.where(q >= end, 1, 0)
+        k_doc = k_doc + jnp.where(k >= end, 1, 0)
+    seen = (q_doc == k_doc) & (k <= q) & (q - k < W) & (k >= 0)
+    return jnp.where(seen, 0.0, NEG_FILL).astype(F32)
+
+
+SIZES = (16, 16, 32, 16, 16, 16, 64, 16)
+
+
+def whole_vector(table, index, offset, count):
+    size = SIZES[index]
+    shift = size.bit_length() - 1
+    row = lax.broadcasted_iota(jnp.int32, (128, 1024), 0)
+    tile = lax.broadcasted_iota(jnp.int32, (128, 1024), 1)
+    chosen = jnp.where(tile == row * 8 + index, 1.0, 0.0).astype(BF)
+    share = dot(chosen, table, NN).astype(BF)
+    row = lax.broadcasted_iota(jnp.int32, (128, count), 0)
+    column = lax.broadcasted_iota(jnp.int32, (128, count), 1) + offset
+    spread = jnp.where((column & (size - 1)) == row, 1.0, 0.0).astype(BF)
+    values = jnp.where((column >> shift) == row, dot(share, spread, NN), 0.0)
+    return jnp.sum(values, axis=0, keepdims=True)
+
+
+def forward_body(
+    lengths,
+    tok_in,
+    small_in,
+    dy_hbm,
+    wqkv_hbm,
+    wout_hbm,
+    wup_hbm,
+    wdn_hbm,
+    a2_o,
+    res_o,
+    vec_o,
+    dyg_h,
+    wq_h,
+    wo_h,
+    a1_h,
+    q_h,
+    kv_h,
+    mixed_h,
+    ua_h,
+    ub_h,
+    wd_h,
+    wq,
+    wo,
+    tokg,
+    a1,
+    q,
+    kv,
+    mixed,
+    part,
+    got,
+    own,
+    tmp,
+    smalls,
+    uslot,
+    rs_send,
+    rs_recv,
+    send_sem,
+    recv_sem,
+):
+    comm = Comm(send_sem, recv_sem)
+    me = coords()
+    x, y, z, core = me["x"], me["y"], me["z"], me["core"]
+    blk, width = tok_in.shape
+    span = 4 * blk
+    partw = q.shape[1]
+    hidden = uslot.shape[1]
+    heads = partw // HEAD
+    reach = W + blk
+    scale = 1.0 / math.sqrt(HEAD)
+    mine16 = pl.ds(x * 16, 16)
+
+    greet(everyone() + [scattered(), collected()])
+
+    s_q = []
+    for k in (1, 3, 2):
+        for g in range(3):
+            src = wqkv_hbm.at[:, pl.ds(g * width + lax.rem(x + k, 4) * partw, partw)]
+            dst = wq.at[y, core, z, mine16, pl.ds(g * partw, partw)]
+            s_q.append(comm.push(src, dst, peer(x=k)))
+    for g in range(3):
+        src = wqkv_hbm.at[:, pl.ds(g * width + x * partw, partw)]
+        s_q.append(comm.local(src, wq.at[y, core, z, mine16, pl.ds(g * partw, partw)]))
+    spot = smalls.at[y, core, pl.ds((z * 4 + x) * 8, 8)]
+    s_small = [comm.push(small_in, spot, to) for to in ring("x")] + [comm.local(small_in, spot)]
+    s_o = [comm.push(wout_hbm, wo.at[core, z, x], scattered())]
+    tokens = Relay(
+        comm, "x", lambda o: tokg.at[o], lambda o, h: tokg.at[o, pl.ds(h * blk // 2, blk // 2)]
+    )
+    tokens.start(tok_in)
+    tokg[x] = tok_in[...]
+    s_u = []
+    for k in (1, 3, 2):
+        src = wup_hbm.at[:, pl.ds(lax.rem(x + k, 4) * hidden, hidden)]
+        s_u.append(comm.push(src, uslot.at[mine16], peer(x=k)))
+    s_u.append(comm.local(wup_hbm.at[:, pl.ds(x * hidden, hidden)], uslot.at[mine16]))
+    s_d = [comm.push(wdn_hbm, wd_h.at[core, z, x], scattered())]
+
+    qkv_g = Gather(comm, wq, False, by_rows(64))
+    out_g = Gather(comm, wo, True, by_columns(width))
+    down_g = Gather(comm, wd_h, True, by_rows(64))
+
+    comm.arrived(s_small)
+    block = smalls.at[y, core, pl.ds(z * 32, 32)]
+    s_small = [comm.push(block, block, to) for to in ring("z")]
+    comm.arrived(s_q)
+    qkv_g.first()
+    comm.arrived(s_o)
+    out_g.first()
+    comm.arrived(s_small)
+    block = smalls.at[y, core]
+    s_small = [comm.push(block, block, to) for to in ring("y")]
+    comm.arrived(qkv_g.one)
+    qkv_g.second()
+    comm.arrived(s_small)
+    s_small = []
+    for other_y in range(4):
+        block = smalls.at[other_y, core]
+        s_small.append(comm.push(block, block, peer(core=1)))
+    comm.arrived(out_g.one)
+    out_g.second()
+    tokens.near()
+
+    comm.arrived(s_small)
+    table = smalls[...].reshape(1024, 128).astype(BF)
+    vec_o[0:1, :] = whole_vector(table, 0, 0, width)
+    vec_o[1:2, :] = whole_vector(table, 1, 0, width)
+    gain, shift = vec_o[0:1, :], vec_o[1:2, :]
+
+    def norm_block(o):
+        @pl.loop(0, blk // 16)
+        def _(i):
+            rows = pl.ds(pl.multiple_of(i * 16, 16), 16)
+            v = tokg[o, rows, :].astype(F32)
+            centred = v - jnp.mean(v, axis=-1, keepdims=True)
+            s = lax.rsqrt(jnp.mean(centred * centred, axis=-1, keepdims=True) + EPSILON)
+            at = pl.ds(pl.multiple_of(o * blk + i * 16, 16), 16)
+            a1[at, :] = (centred * s * gain + shift).astype(BF)
+
+    norm_block(x)
+    norm_block(lax.rem(x + 1, 4))
+    qkv_g.near()
+    norm_block(lax.rem(x + 3, 4))
+    tokens.far()
+    cotangent = Relay(
+        comm, "x", lambda o: dyg_h.at[o], lambda o, h: dyg_h.at[o, pl.ds(h * blk // 2, blk // 2)]
+    )
+    cotangent.start(dy_hbm)
+    comm.local(dy_hbm, dyg_h.at[x])
+    norm_block(lax.rem(x + 2, 4))
+    comm.local(a1, a1_h)
+    qkv_g.far()
+    out_g.near()
+    comm.arrived(s_d)
+    down_g.first()
+    comm.arrived(s_u)
+    low, high = uslot.at[0:32], uslot.at[32:64]
+    for to in ring("z"):
+        comm.push(low, ua_h.at[z], to)
+    for to in ring("y"):
+        comm.push(high, ub_h.at[y], to)
+    comm.local(low, ua_h.at[z])
+    comm.local(high, ub_h.at[y])
+
+    vec_o[2:3, :] = jnp.zeros((1, width), F32)
+    vec_o[2:3, 0:partw] = whole_vector(table, 2, x * partw, partw)
+    vec_o[2:3, 2 * partw : 3 * partw] = whole_vector(table, 2, width + x * partw, partw)
+    for i in (3, 4, 5, 7):
+        vec_o[i : i + 1, :] = whole_vector(table, i, 0, width)
+    vec_o[6:7, :] = whole_vector(table, 6, x * hidden, hidden)
+
+    out_g.far()
+    qkv_g.done()
+
+    def project(cols, at):
+        r = dot(a1[...], wq[:, :, :, :, cols].reshape(width, at), NN)
+        return (r + vec_o[2:3, cols]).astype(BF)
+
+    kv[W:, 0:partw] = project(slice(partw, 2 * partw), partw)
+    kv[W:, partw:] = project(slice(2 * partw, 3 * partw), partw)
+    s_edge = [comm.push(kv.at[pl.ds(span, W)], kv.at[pl.ds(0, W)], peer(z=1))]
+    q[...] = project(slice(0, partw), partw)
+    comm.local(wq, wq_h)
+    comm.local(q, q_h)
+    comm.arrived(down_g.one)
+    down_g.second()
+    cotangent.near()
+
+    def attend(b):
+        rows = pl.ds(pl.multiple_of(b * blk, blk), blk)
+        window = pl.ds(pl.multiple_of(b * blk, blk), reach)
+        mask = mask_of(lengths, z * span + b * blk, blk, reach)
+        for h in range(heads):
+            cols, vcols = pl.ds(h * HEAD, HEAD), pl.ds(partw + h * HEAD, HEAD)
+            s = dot(q[rows, cols], kv[window, cols], NT) * scale + mask
+            e = jnp.exp(s - jnp.max(s, axis=-1, keepdims=True))
+            p = (e * (1.0 / jnp.sum(e, axis=-1, keepdims=True))).astype(BF)
+            mixed[rows, cols] = dot(p, kv[window, vcols], NN).astype(BF)
+
+    pl.loop(2, 4)(attend)
+    comm.arrived(s_edge)
+    pl.loop(0, 2)(attend)
+    comm.local(kv, kv_h)
+    comm.local(mixed, mixed_h)
+    down_g.near()
+    cotangent.far()
+    out_g.done()
+    comm.local(wo, wo_h)
+
+    def sends(j):
+        cols = pl.ds(pl.multiple_of(j * 512, 512), 512)
+        return [
+            remote(
+                part.at[lax.rem(x + k, 4), :, cols],
+                got.at[k - 1, :, cols],
+                (rs_send, rs_recv),
+                3 * j + k - 1,
+                peer(x=k),
+            )
+            for k in (2, 1, 3)
+        ]
+
+    @pl.loop(0, 4)
+    def _(j):
+        cols = pl.ds(pl.multiple_of(j * 512, 512), 512)
+        d = dot(mixed[...], wo[:, :, :, :, cols].reshape(partw, 512), NN)
+        part[:, :, cols] = d.astype(BF).reshape(4, blk, 512)
+        tmp[...] = d.reshape(4, blk, 512)
+        own[:, cols] = tmp[x]
+        for copy in sends(j):
+            copy.start()
+
+    down_g.far()
+
+    @pl.loop(0, 4)
+    def _(j):
+        for copy in sends(j):
+            copy.wait_recv()
+
+    b_out, gain2, shift2 = vec_o[3:4, :], vec_o[4:5, :], vec_o[5:6, :]
+
+    @pl.loop(0, blk // 16)
+    def _(i):
+        rows = pl.ds(pl.multiple_of(i * 16, 16), 16)
+        v = tok_in[rows, :].astype(F32) + own[rows, :] + b_out
+        for g in range(3):
+            v = v + got[g, rows, :].astype(F32)
+        res_o[rows, :] = v
+        centred = v - jnp.mean(v, axis=-1, keepdims=True)
+        s = lax.rsqrt(jnp.mean(centred * centred, axis=-1, keepdims=True) + EPSILON)
+        a2_o[rows, :] = (centred * s * gain2 + shift2).astype(BF)
+
+    @pl.loop(0, 4)
+    def _(j):
+        for copy in sends(j):
+            copy.wait_send()
+
+    comm.drain()
+
+
+def forward(collective_id, lengths, tok, small, dy, w_qkv, w_out, w_up, w_down):
+    blk, width = tok.shape
+    span, partw, hidden = 4 * blk, width // 4, w_up.shape[1] // 4
+    vmem = pl.BlockSpec(memory_space=pltpu.VMEM)
+    hbm = pl.BlockSpec(memory_space=pl.ANY)
+    outs = [
+        ((blk, width), BF, vmem),
+        ((blk, width), F32, vmem),
+        ((8, width), F32, vmem),
+        ((4, blk, width), BF, hbm),
+        ((4, 2, 4, 64, 3 * partw), BF, hbm),
+        ((2, 4, 4, 16, width), BF, hbm),
+        ((span, width), BF, hbm),
+        ((span, partw), BF, hbm),
+        ((span + W, 2 * partw), BF, hbm),
+        ((span, partw), BF, hbm),
+        ((4, 32, hidden), BF, hbm),
+        ((4, 32, hidden), BF, hbm),
+        ((2, 4, 4, 64, width), BF, hbm),
+    ]
+    scratch = [
+        ((4, 2, 4, 64, 3 * partw), BF),
+        ((2, 4, 4, 16, width), BF),
+        ((4, blk, width), BF),
+        ((span, width), BF),
+        ((span, partw), BF),
+        ((span + W, 2 * partw), BF),
+        ((span, partw), BF),
+        ((4, blk, width), BF),
+        ((3, blk, width), BF),
+        ((blk, width), F32),
+        ((4, blk, 512), F32),
+        ((4, 2, 128, 128), F32),
+        ((64, hidden), BF),
+    ]
+    return pl.pallas_call(
+        forward_body,
+        out_shape=tuple(jax.ShapeDtypeStruct(s, d) for s, d, _ in outs),
+        in_specs=[pl.BlockSpec(memory_space=pltpu.SMEM)] + [vmem] * 2 + [hbm] * 5,
+        out_specs=tuple(o[2] for o in outs),
+        scratch_shapes=[pltpu.VMEM(s, d) for s, d in scratch]
+        + [pltpu.SemaphoreType.DMA((n,)) for n in (12, 12, SEMS, SEMS)],
+        compiler_params=pltpu.CompilerParams(
+            collective_id=collective_id, has_side_effects=True, vmem_limit_bytes=62 << 20
+        ),
+        name="forward",
+    )(lengths, tok, small, dy, w_qkv, w_out, w_up, w_down)
 
 
 ORDER = (0, 1, 3, 2)
@@ -299,10 +535,10 @@
     a2_in,
     res_in,
     dy_in,
-    gain_in,
-    bias_in,
+    vec_in,
     dyg_hbm,
-    wup_hbm,
+    ua_hbm,
+    ub_hbm,
     wdn_hbm,
     dattn_hbm,
     dhid_out,
@@ -333,8 +569,11 @@
     local_sem,
     send_sem,
     recv_sem,
+    comm_send,
+    comm_recv,
 ):
     sems = (send_sem, recv_sem)
+    comm = Comm(comm_send, comm_recv)
     me = coords()
     x, y, z, core = me["x"], me["y"], me["z"], me["core"]
     other = 1 - core
@@ -352,16 +591,19 @@
             )
         )
         load_dy[-1].start()
-    load_up = pltpu.make_async_copy(wup_hbm, wup, local_sem.at[5])
-    load_up.start()
-
-    greet(ring("x") + ring("y") + ring("z") + near())
-
-    spread = [
-        remote(a2_in, a2g.at[p], sems, p, peer(x=ORDER[p])) for p in (1, 2, 3)
+    low, high = slice(0, 32), slice(32, 64)
+    load_up = [
+        pltpu.make_async_copy(ua_hbm, wup.at[y, core, :, low], local_sem.at[5]),
+        pltpu.make_async_copy(ub_hbm, wup.at[:, core, z, high], local_sem.at[7]),
     ]
-    for copy in spread:
+    for copy in load_up:
         copy.start()
+
+    greet(everyone())
+
+    spread = [comm.push(a2_in, a2g.at[1], peer(x=1)), comm.push(a2_in, a2g.at[2], peer(x=3))]
+    up_g = Gather(comm, wup, False, by_rows(64))
+    up_g.second(ua_hbm, ub_hbm)
     a2g[0] = a2_in[...]
 
     load_down.wait()
@@ -374,15 +616,24 @@
         cols = pl.ds(pl.multiple_of(j * 512, 512), 512)
         dact[:, cols] = dot(dyg[...].reshape(span, width), tile, NT)
 
-    load_up.wait()
-    for copy in spread:
-        copy.wait_recv()
+    comm.arrived(spread)
+    top, bottom = pl.ds(0, blk // 2), pl.ds(blk // 2, blk // 2)
+    passed = [
+        comm.push(a2g.at[1, top], a2g.at[3, top], peer(x=1)),
+        comm.push(a2g.at[2, bottom], a2g.at[3, bottom], peer(x=3)),
+    ]
+    for copy in load_up:
+        copy.wait()
+    up_g.near()
+    comm.arrived(passed)
+    up_g.far()
+    up_g.done()
 
     @pl.loop(0, hidden // 256)
     def _(j):
         cols = pl.ds(pl.multiple_of(j * 256, 256), 256)
         u = dot(a2g[...].reshape(span, width), wup[:, :, :, :, cols].reshape(width, 256), NN)
-        u = u + bias_in[:, cols]
+        u = u + vec_in[6:7, cols]
         phi = 0.5 + 0.5 * lax.erf(u * math.sqrt(0.5))
         act[:, cols] = (u * phi).astype(BF)
         slope = phi + u * (jnp.exp(-0.5 * u * u) * (1.0 / math.sqrt(2.0 * math.pi)))
@@ -441,6 +692,8 @@
         wdn[other, t] = grad_down(other, t).astype(BF).reshape(4, 64, width)
         swap_down(t).start()
 
+    comm.drain()
+
     @pl.loop(0, 4)
     def _(t):
         wup[t, other] = grad_up(t, other).astype(BF).reshape(4, 64, hidden)
@@ -458,7 +711,6 @@
         first.append(remote(src, dst, sems, index, to))
         first[-1].start()
 
-    low, high = slice(0, 32), slice(32, 64)
     for k in (1, 3, 2):
         zz, yy = lax.rem(z + k, 4), lax.rem(y + k + 3, 4)
         stage(wdn.at[core, :, zz, low], dn_a_got.at[k - 1], 24 + k, peer(z=k))
@@ -482,7 +734,7 @@
 
     small_out[0:3, :] = jnp.zeros((3, width), F32)
     small_out[4:8, :] = jnp.zeros((4, width), F32)
-    gain = gain_in[...]
+    gain = vec_in[4:5, :]
 
     @pl.loop(0, blk // 16)
     def _(i):
@@ -510,11 +762,10 @@
         small_out[2:3, :] += jnp.sum(low_hid.astype(F32), axis=0, keepdims=True)
         small_out[4:5, :] += jnp.sum(dy_own, axis=0, keepdims=True)
 
-    attn = [
-        remote(datt, dattn_hbm.at[x], sems, 40 + k, peer(x=k)) for k in (1, 3, 2)
-    ]
-    for copy in attn:
-        copy.start()
+    attn = Relay(
+        comm, "x", lambda o: dattn_hbm.at[o], lambda o, h: dattn_hbm.at[o, pl.ds(h * blk // 2, blk // 2)]
+    )
+    attn.start(datt)
     kept = [keep_out, pltpu.make_async_copy(datt, dattn_hbm.at[x], local_sem.at[7])]
     zy = lax.rem(y + 3, 4)
     kept.append(pltpu.make_async_copy(wdn.at[core, :, z, low], dn_a_own, local_sem.at[8]))
@@ -524,9 +775,10 @@
     for copy in kept[1:]:
         copy.start()
 
-    for copy in first + attn:
+    attn.near()
+    for copy in first:
         copy.wait_recv()
-    for copy in spread + first + attn:
+    for copy in first:
         copy.wait_send()
 
     @pl.loop(0, 4)
@@ -538,11 +790,12 @@
 
     for copy in kept:
         copy.wait()
-
-
-def feed_forward(collective_id, a2, residual, dy, gain, bias, dy_g, wup, wdn):
+    comm.drain()
+
+
+def feed_forward(collective_id, a2, residual, dy, vectors, dy_g, up_a, up_b, wdn):
     blk, width = a2.shape
-    hidden = wup.shape[-1]
+    hidden = up_a.shape[-1]
     span = 4 * blk
     vmem = pl.BlockSpec(memory_space=pltpu.VMEM)
     hbm = pl.BlockSpec(memory_space=pl.ANY)
@@ -572,19 +825,21 @@
     return pl.pallas_call(
         feed_forward_body,
         out_shape=tuple(jax.ShapeDtypeStruct(s, d) for s, d, _ in outs),
-        in_specs=[vmem] * 5 + [hbm] * 3,
+        in_specs=[vmem] * 4 + [hbm] * 4,
         out_specs=tuple(o[2] for o in outs),
         scratch_shapes=[pltpu.VMEM(s, d) for s, d in scratch]
         + [
             pltpu.SemaphoreType.DMA((12,)),
-            pltpu.SemaphoreType.DMA((44,)),
-            pltpu.SemaphoreType.DMA((44,)),
+            pltpu.SemaphoreType.DMA((40,)),
+            pltpu.SemaphoreType.DMA((40,)),
+            pltpu.SemaphoreType.DMA((40,)),
+            pltpu.SemaphoreType.DMA((40,)),
         ],
         compiler_params=pltpu.CompilerParams(
             collective_id=collective_id, has_side_effects=True, vmem_limit_bytes=62 << 20
         ),
         name="feed_forward",
-    )(a2, residual, dy, gain.reshape(1, width), bias.reshape(1, hidden), dy_g, wup, wdn)
+    )(a2, residual, dy, vectors, dy_g, up_a, up_b, wdn)
 
 
 def norm_backward(d, v, gain):
@@ -599,14 +854,13 @@
 
 
 def attention_backward_body(
-    gain_in,
-    bdown_in,
+    lengths,
+    vec_in,
     ffsmall_in,
     dattn_hbm,
     wout_hbm,
-    proj_hbm,
-    edge_hbm,
-    bias_hbm,
+    q_hbm,
+    kv_hbm,
     a1_hbm,
     mixed_hbm,
     wqkv_hbm,
@@ -631,9 +885,8 @@
     small_o,
     dattn,
     wout,
-    proj,
+    q_all,
     kv,
-    bias,
     a1,
     mixed,
     wqkv,
@@ -704,12 +957,7 @@
         return copy
 
     l_dattn, l_wout = load(dattn_hbm, dattn), load(wout_hbm, wout)
-    l_attn = [
-        load(proj_hbm, proj),
-        load(edge_hbm, kv.at[pl.ds(0, W)]),
-        load(proj_hbm.at[:, pl.ds(partw, 2 * partw)], kv.at[pl.ds(W, span)]),
-        load(bias_hbm, bias),
-    ]
+    l_attn = [load(q_hbm, q_all), load(kv_hbm, kv)]
     l_ff = [load(s, fo.at[i]) for i, s in enumerate((ffo0, ffo1, ffo2, ffo3))]
     l_ff += [load(s, fg.at[i]) for i, s in enumerate((ffg0, ffg1, ffg2, ffg3))]
     l_wqkv, l_a1, l_mixed = load(wqkv_hbm, wqkv), load(a1_hbm, a1), load(mixed_hbm, mixed)
@@ -734,11 +982,12 @@
     def block(b):
         rows = pl.ds(pl.multiple_of(b * blk, blk), blk)
         window = pl.ds(pl.multiple_of(b * blk, blk), reach)
+        mask = mask_of(lengths, z * span + b * blk, blk, reach)
         for h in range(heads):
             cols = pl.ds(h * HEAD, HEAD)
             vcols = pl.ds(partw + h * HEAD, HEAD)
-            q, k, v = proj[rows, cols], kv[window, cols], kv[window, vcols]
-            s = dot(q, k, NT) * scale + bias[b]
+            q, k, v = q_all[rows, cols], kv[window, cols], kv[window, vcols]
+            s = dot(q, k, NT) * scale + mask
             e = jnp.exp(s - jnp.max(s, axis=-1, keepdims=True))
             p = e * (1.0 / jnp.sum(e, axis=-1, keepdims=True))
             do = dmix[rows, cols]
@@ -869,7 +1118,7 @@
     @pl.loop(0, blk // 16)
     def _(i):
         rows = pl.ds(pl.multiple_of(i * 16, 16), 16)
-        total = res[rows, :] + bdown_in[...] + outown[rows, :].astype(F32)
+        total = res[rows, :] + vec_in[7:8, :] + outown[rows, :].astype(F32)
         for g in range(3):
             total = total + outgot[g, rows, :].astype(F32)
         out_o[rows, :] = total.astype(BF)
@@ -884,7 +1133,7 @@
         for copy in sends(j):
             copy.wait_recv()
 
-    gain = gain_in[...]
+    gain = vec_in[0:1, :]
 
     @pl.loop(0, blk // 16)
     def _(i):
@@ -977,14 +1226,13 @@
 
 def attention_backward(
     collective_id,
-    gain,
-    b_down,
+    lengths,
+    vectors,
     ff_small,
     d_attn,
     wout,
-    projected,
-    edge,
-    bias,
+    q,
+    kv,
     a1,
     mixed,
     wqkv,
@@ -1013,9 +1261,8 @@
     scratch = [
         ((4, blk, width), BF),
         ((2, 4, 4, 16, width), BF),
-        ((span, 3 * partw), BF),
+        ((span, partw), BF),
         ((span + W, 2 * partw), BF),
-        (bias.shape, F32),
         ((span, width), BF),
         ((span, partw), BF),
         ((4, 2, 4, 64, 3 * partw), BF),
@@ -1059,7 +1306,7 @@
     return pl.pallas_call(
         attention_backward_body,
         out_shape=tuple(jax.ShapeDtypeStruct(s, d) for s, d, _ in outs),
-        in_specs=[vmem] * 3 + [hbm] * 20,
+        in_specs=[pl.BlockSpec(memory_space=pltpu.SMEM)] + [vmem] * 2 + [hbm] * 19,
         out_specs=tuple(o[2] for o in outs),
         scratch_shapes=[pltpu.VMEM(s, d) for s, d in scratch]
         + [
@@ -1072,14 +1319,13 @@
         ),
         name="attention_backward",
     )(
-        gain.reshape(1, width),
-        b_down.reshape(1, width),
+        lengths,
+        vectors,
         ff_small,
         d_attn,
         wout,
-        projected,
-        edge,
-        bias,
+        q,
+        kv,
         a1,
         mixed,
         wqkv,
@@ -1110,160 +1356,30 @@
     b_down,
 ):
     blk, width = tokens.shape[1:]
-    span = 4 * blk
     part = width // 4
     hidden = w_up.shape[1] // 4
-    heads = HEADS // 4
-    x_at, z_at = lax.axis_index("x"), lax.axis_index("z")
-    scale = 1.0 / math.sqrt(HEAD)
-
     tok = tokens.reshape(blk, width)
     dy = grad_out.reshape(blk, width)
-    small = jnp.concatenate([ln1_gain, ln1_bias, b_qv, b_out, ln2_gain, ln2_bias, b_up, b_down])
-    small = jnp.pad(small.astype(F32), (0, 1024 - small.shape[0])).reshape(8, 128)
-    qkv_parts = w_qkv.reshape(16, 3, 4, part).transpose(2, 0, 1, 3).reshape(4, 16, 3 * part)
-    up_parts = w_up.reshape(16, 4, hidden).transpose(1, 0, 2)
-
-    def first_body(comm, ins, outs):
-        tok_r, dy_r, small_r, qkv_r, out_r = ins
-        tok_g, small_g, dy_g, wq, wo = outs
-        me = coords()
-        slot = into_slot(comm, qkv_r, wq)
-        spot = into_scattered(comm, out_r, wo)
-        at = (me["y"], me["core"], me["z"])
-        s0 = [comm.push(small_r, small_g.at[at + (me["x"],)], to) for to in ring("x")]
-        s0.append(comm.local(small_r, small_g.at[at + (me["x"],)]))
-        spread_x(comm, tok_r, tok_g)
-        q, o = Gather(comm, wq, False), Gather(comm, wo, True)
-        comm.arrived(slot)
-        q.first()
-        comm.arrived(s0)
-        mine = small_g.at[at]
-        s1 = [comm.push(mine, mine, to) for to in ring("z")]
-        comm.arrived(spot)
-        o.first()
-        spread_x(comm, dy_r, dy_g)
-        comm.arrived(s1)
-        mine = small_g.at[me["y"], me["core"]]
-        s2 = [comm.push(mine, mine, to) for to in ring("y")]
-        q.second()
-        o.second()
-        comm.arrived(s2)
-        mine = small_g.at[:, me["core"]]
-        comm.push(mine, mine, peer(core=1))
-        q.third()
-        o.third()
-
-    tok_g, small_g, dy_g, wqkv_g, wout_g = exchange(
-        "gather_attn",
-        0,
-        first_body,
-        lambda: gather_peers() + [scattered(), collected()],
-        [tok, dy, small, qkv_parts, w_out],
-        [
-            ((4, blk, width), BF),
-            ((4, 2, 4, 4, 8, 128), F32),
-            ((4, blk, width), BF),
-            ((4, 2, 4, 64, 3 * part), BF),
-            ((2, 4, 4, 16, width), BF),
-        ],
-    )
-    small_g = small_g.reshape(128, 1024)
-    vectors, start = [], 0
-    for size in (16, 16, 32, 16, 16, 16, 64, 16):
-        vectors.append(small_g[:, start : start + size].reshape(128 * size))
-        start += size
-    gain1, shift1, bias_qv, bias_out, gain2, shift2, bias_up, bias_down = vectors
-    weight_qkv = wqkv_g.reshape(width, 3 * part)
-    weight_out = wout_g.reshape(part, width)
-
-    inputs = tok_g.reshape(span, width).astype(F32)
-    normed1 = layer_norm(inputs, gain1, shift1).astype(BF)
-    bias_q = lax.dynamic_slice_in_dim(bias_qv, x_at * part, part)
-    bias_v = lax.dynamic_slice_in_dim(bias_qv, width + x_at * part, part)
-    bias_full = jnp.concatenate([bias_q, jnp.zeros((part,), F32), bias_v])
-    projected = (dot(normed1, weight_qkv, NN) + bias_full).astype(BF)
-
-    def second_body(comm, ins, outs):
-        p_r, up_r, down_r = ins
-        edge, wu, wd = outs
-        comm.push(p_r.at[pl.ds(span - W, W), pl.ds(part, 2 * part)], edge, peer(z=1))
-        slot = into_slot(comm, up_r, wu)
-        spot = into_scattered(comm, down_r, wd)
-        u = Gather(comm, wu, False)
-        comm.arrived(slot)
-        u.first()
-        comm.arrived(spot)
-        u.second()
-        u.third()
-
-    edge_kv, wup_g, wdown_s = exchange(
-        "edge_and_up",
-        1,
-        second_body,
-        lambda: gather_peers() + [scattered(), collected()],
-        [projected, up_parts, w_down],
-        [
-            ((W, 2 * part), BF),
-            ((4, 2, 4, 64, hidden), BF),
-            ((2, 4, 4, 64, width), BF),
-        ],
-    )
-
-    row_ends = jnp.cumsum(lengths.reshape(-1))
-    q_pos = z_at * span + jnp.arange(span, dtype=jnp.int32)
-    k_pos = z_at * span - W + jnp.arange(span + W, dtype=jnp.int32)
-    q_doc, k_doc = doc_number(q_pos, row_ends), doc_number(k_pos, row_ends)
-    reach = W + blk
-
-    def windows(array):
-        return jnp.stack([array[b * blk : b * blk + reach] for b in range(4)])
-
-    qp, qd = q_pos.reshape(4, blk, 1), q_doc.reshape(4, blk, 1)
-    kp, kd = windows(k_pos)[:, None, :], windows(k_doc)[:, None, :]
-    visible = (qd == kd) & (kp <= qp) & (qp - kp < W) & (kp >= 0)
-
-    keys = jnp.concatenate([edge_kv[:, :part], projected[:, part : 2 * part]])
-    values = jnp.concatenate([edge_kv[:, part:], projected[:, 2 * part :]])
-    q_heads = projected[:, :part].reshape(4, blk, heads, HEAD)
-    k_heads = windows(keys).reshape(4, reach, heads, HEAD)
-    v_heads = windows(values).reshape(4, reach, heads, HEAD)
-    scores = jnp.einsum("bqhd,bkhd->bhqk", q_heads, k_heads, preferred_element_type=F32) * scale
-    masked = jnp.where(visible[:, None], scores, NEG_FILL)
-    peak = jnp.max(masked, axis=-1, keepdims=True)
-    log_total = peak + jnp.log(jnp.sum(jnp.exp(masked - peak), axis=-1, keepdims=True))
-    probs = jnp.exp(masked - log_total)
-    probs_low = probs.astype(BF)
-    mixed = jnp.einsum("bhqk,bkhd->bqhd", probs_low, v_heads, preferred_element_type=F32)
-    mixed = mixed.reshape(span, part).astype(BF)
-    attn_part = dot(mixed, weight_out, NN).reshape(4, blk, width)
-
-    def third_body(comm, ins, outs):
-        part_r, wd_in = ins
-        got, wd = outs
-        me = coords()
-        split_x(comm, part_r, got)
-        slot = (me["core"], lax.rem(me["y"] + 3, 4), me["z"])
-        comm.arrived([comm.local(wd_in.at[slot], wd.at[slot])])
-        d = Gather(comm, wd, True)
-        d.first()
-        d.second()
-        d.third()
-
-    attn_got, wdown_g = exchange(
-        "sum_attn_and_down",
-        2,
-        third_body,
-        gather_peers,
-        [attn_part.astype(BF), wdown_s],
-        [((3, blk, width), BF), ((2, 4, 4, 64, width), BF)],
-    )
-
-    own_tok = tok.astype(F32)
-    residual = own_tok + pick(attn_part, x_at) + attn_got.astype(F32).sum(0) + bias_out
-    normed2 = layer_norm(residual, gain2, shift2).astype(BF)
-
-    bias_up_own = lax.dynamic_slice_in_dim(bias_up, x_at * hidden, hidden)
+    small = jnp.zeros((1024,), F32)
+    vectors = (ln1_gain, ln1_bias, b_qv, b_out, ln2_gain, ln2_bias, b_up, b_down)
+    for i, vector in enumerate(vectors):
+        size = vector.shape[0]
+        small = small + jnp.pad(vector.astype(F32), (i * 128, 1024 - i * 128 - size))
+    (
+        a2,
+        residual,
+        vectors,
+        dy_g,
+        wqkv_g,
+        wout_g,
+        a1,
+        query,
+        kv,
+        mixed,
+        up_a,
+        up_b,
+        wdown_g,
+    ) = forward(0, lengths, tok, small.reshape(8, 128), dy, w_qkv, w_out, w_up, w_down)
     (
         d_attn_g,
         d_hidden,
@@ -1272,24 +1388,22 @@
         up_b_own,
         down_a_own,
         down_b_own,
-        up_a,
-        up_b,
-        down_a,
-        down_b,
+        up_a_got,
+        up_b_got,
+        down_a_got,
+        down_b_got,
         ff_small,
-    ) = feed_forward(3, normed2, residual, dy, gain2, bias_up_own, dy_g, wup_g, wdown_g)
-    bias = jnp.where(visible, 0.0, NEG_FILL).astype(F32)
+    ) = feed_forward(1, a2, residual, dy, vectors, dy_g, up_a, up_b, wdown_g)
     out, grad_tokens, qkv_x, g_out_own, up_x, g_down_own, small_x = attention_backward(
-        4,
-        gain1,
-        bias_down,
+        2,
+        lengths,
+        vectors,
         ff_small,
         d_attn_g,
         wout_g,
-        projected,
-        edge_kv,
-        bias,
-        normed1,
+        query,
+        kv,
+        a1,
         mixed,
         wqkv_g,
         tok,
@@ -1297,7 +1411,7 @@
         residual,
         out_part,
         (up_a_own, up_b_own, down_a_own, down_b_own),
-        (up_a, up_b, down_a, down_b),
+        (up_a_got, up_b_got, down_a_got, down_b_got),
     )
 
     def columns(parts, groups):

time: 459 us -> 342 us (0.75)
  Pallas kernels: 378 us -> 326 us
  local copies, waits for them, and re-layouts: 41 us -> 9.09 us
  other arithmetic: 22.7 us -> 5.46 us
  matrix products: 16 us -> 0 us
    pallas_call x3 -> x1, Pallas kernels: 181 us -> 127 us  [forward(): pl.pallas_call(forward_body, out_shape=tuple((jax.ShapeDtypeStruct(s, d)...]
    dot_general x4 -> x0, matrix products: 16 us -> none  [the longest x2 10.7 us: dot(): return lax.dot_general(a, b, (dims, ((), ())), preferred_element_type=F32)]
    another operation x23 -> x0, local copies, waits for them, and re-layouts: 11.6 us -> none  [the longest x20 9.56 us: windows(): return jnp.stack([array[b * blk:b * blk + reach] for b in range(4)])]
    convert_element_type x3 -> x0, other arithmetic: 6.96 us -> none  [the longest x2 5.91 us: local(): normed1 = layer_norm(inputs, gain1, shift1).astype(BF)]
    reduce_sum x8 -> x0, other arithmetic: 5.88 us -> none  [the longest x2 1.85 us: layer_norm(): center = jnp.mean(values, axis=-1, keepdims=True)]
    concatenate x1 -> x0, local copies, waits for them, and re-layouts: 5.44 us -> none  [local(): jnp.concatenate([ln1_gain, ln1_bias, b_qv, b_out, ln2_gain, ln2_bias, b_u...]
where the time goes in v4:
time: 342 us
  Pallas kernels  326 us (95%)
  local copies, waits for them, and re-layouts  9.09 us (3%)
  other arithmetic  5.46 us (2%)
    pallas_call x1, Pallas kernels, forward(): pl.pallas_call(forward_body, out_shape=tuple((jax.ShapeDtypeStruct(s, d)...  127 us
    pallas_call x1, Pallas kernels, feed_forward(): pl.pallas_call(feed_forward_body, out_shape=tuple((jax.ShapeDtypeStruct(s...  107 us
    pallas_call x1, Pallas kernels, attention_backward(): pl.pallas_call(attention_backward_body, out_shape=tuple((jax.ShapeDtypeSt...  93.1 us

profile of v4, /device:TPU:1, one launch (start us, length us, event | category | flops | bytes accessed | tf_op | source)
XLA Modules:
  0.0 341.5 jit_solution(4592342273742258325)
XLA Ops:
  0.6 1.4 add_bitcast_fusion.small_in
  2.0 126.6 %forward.1 = (bf16[128,2048]{1,0:T(8,128)(2,1)}, f32[128,2048]{1,0:T(8,128)}, f32[8,2048]{1,0:T(8,128)}, bf16[4,128,2048]{2,1,0:T(8,128)(2,1)}, bf16[4,2,4,64,15...) custom-call(s32[1,4]{1,0:T(1,128)} %lengths.3, ...), custom_call_target="tpu_custom_call" | custom-call | tf_op jit(solution)/shard_map/forward/pallas_call | solution.py:505
  128.6 106.5 %feed_forward.1 = (bf16[4,128,2048]{2,1,0:T(8,128)(2,1)}, f32[128,2048]{1,0:T(8,128)}, bf16[4,128,2048]{2,1,0:T(8,128)(2,1)}, bf16[4,32,2048]{2,1,0:T(8,128)(2,1...) custom-call(bf16[128,2048]{1,0:T(8,128)(2,1)} %get-tuple-element.47., ...), custom_call_target="tpu_custom_call" | custom-call | tf_op jit(solution)/shard_map/feed_forward/pallas_call | solution.py:825
  235.2 93.1 %attention_backward.1 = (bf16[128,2048]{1,0:T(8,128)(2,1)}, f32[128,2048]{1,0:T(8,128)}, bf16[4,16,1536]{2,1,0:T(8,128)(2,1)}, bf16[16,2048]{1,0:T(8,128)(2,1)},...) custom-call(s32[1,4]{1,0:T(1,128)} %lengths.3, ...), custom_call_target="tpu_custom_call" | custom-call | tf_op jit(solution)/shard_map/attention_backward/pallas_call | solution.py:1306
  328.2 0.0 copy-start.3
  328.2 1.0 reduce_sum.9
  329.3 0.6 fusion.4
  329.9 0.6 fusion.2
  330.5 0.9 fusion.7
  331.4 0.6 fusion.6
  332.0 0.6 fusion
  332.6 1.0 convert_bitcast_fusion
  333.5 0.0 copy-start.2
  333.6 0.3 copy.32
  333.9 0.0 copy-start.4
  333.9 0.0 copy-start.1
  333.9 1.1 copy.33
  335.0 0.0 copy-done.3
  335.0 0.0 copy-start
  335.0 0.3 reshape.68
  335.4 0.3 copy.31
  335.6 1.0 reshape.66
  336.7 0.0 copy-done.2
  336.7 0.8 convert_element_type.63
  337.5 0.0 copy-done.4
  337.5 0.7 convert_element_type.58
  338.2 1.0 slice.34
  339.2 0.6 dynamic_slice.47
  339.7 0.0 copy-done.1
  339.7 0.8 copy.36
  340.5 0.0 copy-done
  340.5 1.0 copy.37
  (1 shorter events, 0.0 us)
Async XLA Ops:
  328.2 6.8 %copy-start.3 = (bf16[4,16,1536]{2,1,0:T(8,128)(2,1)S(1)}, bf16[4,16,1536]{2,1,0:T(8,128)(2,1)}, u32[]{:S(2)}) copy-start(bf16[4,16,1536]{2,1,0:T(8,128)(2,1)} %get-tuple-element.74) | copy-start | bytes 589828
  333.5 3.1 copy-start.2
  333.9 3.6 %copy-start.4 = (bf16[16,2048]{1,0:T(8,128)(2,1)S(1)}, bf16[16,2048]{1,0:T(8,128)(2,1)}, u32[]{:S(2)}) copy-start(bf16[16,2048]{1,0:T(8,128)(2,1)} %get-tuple-element.75) | copy-start | bytes 196612
  333.9 5.8 %copy-start.1 = (bf16[128,2048]{1,0:T(8,128)(2,1)S(1)}, bf16[128,2048]{1,0:T(8,128)(2,1)}, u32[]{:S(2)}) copy-start(bf16[128,2048]{1,0:T(8,128)(2,1)} %get-tuple-element.71) | copy-start | bytes 1572868
  335.0 5.5 %copy-start = (f32[128,2048]{1,0:T(8,128)S(1)}, f32[128,2048]{1,0:T(8,128)}, u32[]{:S(2)}) copy-start(f32[128,2048]{1,0:T(8,128)} %get-tuple-element.72) | copy-start | bytes 3145732

commit v5 on v4

v5 whole, which is shorter than its diff:
```python
import functools
import math

import jax
import jax.numpy as jnp
from jax import lax
from jax.experimental import pallas as pl
from jax.experimental.pallas import tpu as pltpu
from jax.sharding import Mesh, PartitionSpec as P

HEADS = 16
HEAD = 128
W = 256
EPSILON = 1e-05
NEG_FILL = -1e30

AXES = ("y", "core", "z", "x")
SIZE = {"y": 4, "core": 2, "z": 4, "x": 4}
BF = jnp.bfloat16
F32 = jnp.float32
SEMS = 180


def coords():
    return {a: lax.axis_index(a) for a in AXES}


def peer(**delta):
    me = coords()
    return tuple(lax.rem(me[a] + delta.get(a, 0) % SIZE[a], SIZE[a]) for a in AXES)


class Comm:
    def __init__(self, send_sem, recv_sem, base=0, room=SEMS):
        self.send_sem, self.recv_sem = send_sem, recv_sem
        self.count, self.last, self.open = base, base + room, []

    def push(self, src, dst, to):
        copy = pltpu.make_async_remote_copy(
            src_ref=src,
            dst_ref=dst,
            send_sem=self.send_sem.at[self.count],
            recv_sem=self.recv_sem.at[self.count],
            device_id=to,
            device_id_type=pl.DeviceIdType.MESH,
        )
        assert self.count < self.last
        self.count += 1
        copy.start()
        self.open.append([copy, True, True])
        return self.open[-1]

    def local(self, src, dst):
        copy = pltpu.make_async_copy(src, dst, self.send_sem.at[self.count])
        self.count += 1
        copy.start()
        self.open.append([copy, False, True])
        return self.open[-1]

    def arrived(self, entries):
        for entry in entries:
            if entry[2]:
                if entry[1]:
                    entry[0].wait_recv()
                else:
                    entry[0].wait()
                entry[2] = False

    def drain(self):
        self.arrived(self.open)
        for copy, remote_copy, _ in self.open:
            if remote_copy:
                copy.wait_send()
        self.open = []


def greet(devices):
    barrier = pltpu.get_barrier_semaphore()
    for device in devices:
        pl.semaphore_signal(barrier, inc=1, device_id=device, device_id_type=pl.DeviceIdType.MESH)
    pl.semaphore_wait(barrier, len(devices))


def ring(axis):
    return [peer(**{axis: k}) for k in (1, 3, 2)]


def near():
    return [peer(core=1)]


def plane():
    return [peer(y=i // 4, z=i % 4) for i in range(1, 16)]


def everyone():
    return ring("x") + ring("y") + ring("z") + near()


def scattered():
    me = coords()
    return (lax.rem(me["z"] + 1, 4), me["core"], me["x"], me["y"])


def collected():
    me = coords()
    return (me["x"], me["core"], lax.rem(me["y"] + 3, 4), me["z"])


class Relay:
    def __init__(self, comm, axis, full, half):
        self.comm, self.axis, self.full, self.half = comm, axis, full, half
        self.me = lax.axis_index(axis)

    def to(self, k):
        return peer(**{self.axis: k})

    def start(self, src=None):
        own = self.full(self.me)
        src = own if src is None else src
        self.sent = [self.comm.push(src, own, self.to(1)), self.comm.push(src, own, self.to(3))]

    def near(self):
        self.comm.arrived(self.sent)
        before, after = lax.rem(self.me + 3, 4), lax.rem(self.me + 1, 4)
        up, down = self.half(before, 0), self.half(after, 1)
        self.passed = [self.comm.push(up, up, self.to(1)), self.comm.push(down, down, self.to(3))]

    def far(self):
        self.comm.arrived(self.passed)


class Gather:
    def __init__(self, comm, w, by_core, cut, shift=0):
        self.comm, self.w, self.by_core, self.cut = comm, w, by_core, cut
        self.shift = shift
        me = coords()
        self.y, self.core, self.z = me["y"], me["core"], me["z"]

    def slot(self, y, z, cut):
        place = (self.core, y, z) if self.by_core else (y, self.core, z)
        return self.w.at[place + self.cut[cut]]

    def row(self, y):
        return lax.rem(y + self.shift, 4)

    def first(self):
        self.first_a()
        self.first_b()
        self.one = self.one_a + self.one_b

    def first_a(self):
        a = self.slot(self.row(self.y), self.z, 0)
        self.one_a = [self.comm.push(a, a, to) for to in ring("z")]

    def first_b(self):
        b = self.slot(self.row(self.y), self.z, 1)
        self.one_b = [self.comm.push(b, b, to) for to in ring("y")]

    def second(self):
        self.second_a()
        self.second_b()

    def second_a(self):
        every = slice(None)
        self.a = Relay(
            self.comm,
            "y",
            lambda o: self.slot(self.row(o), every, 0),
            lambda o, h: self.slot(self.row(o), pl.ds(2 * h, 2), 0),
        )
        self.a.start()

    def second_b(self):
        every = slice(None)
        self.b = Relay(
            self.comm,
            "z",
            lambda o: self.slot(every, o, 1),
            lambda o, h: self.slot(pl.ds(2 * h, 2), o, 1),
        )
        self.b.start()

    def across(self, relay, k):
        block = relay.full(lax.rem(relay.me + k, 4))
        self.two.append(self.comm.push(block, block, peer(core=1)))

    def near_a(self):
        self.two = []
        self.a.near()
        for k in (0, 1, 3):
            self.across(self.a, k)

    def near_b(self):
        self.b.near()
        for k in (0, 1, 3):
            self.across(self.b, k)

    def near(self):
        self.near_a()
        self.near_b()

    def far_a(self):
        self.a.far()
        self.across(self.a, 2)

    def far_b(self):
        self.b.far()
        self.across(self.b, 2)

    def far(self):
        self.far_a()
        self.far_b()

    def done(self):
        self.comm.arrived(self.two)


def by_rows(rows):
    return [(slice(0, rows // 2),), (slice(rows // 2, rows),)]


def by_columns(columns):
    every = slice(None)
    return [(every, slice(0, columns // 2)), (every, slice(columns // 2, columns))]


def dot(a, b, dims):
    return lax.dot_general(a, b, (dims, ((), ())), preferred_element_type=F32)


NN = ((1,), (0,))
NT = ((1,), (1,))
TN = ((0,), (0,))


def mask_of(lengths, first, blk, reach):
    q = first + lax.broadcasted_iota(jnp.int32, (blk, reach), 0)
    k = first - W + lax.broadcasted_iota(jnp.int32, (blk, reach), 1)
    q_doc, k_doc = jnp.zeros((blk, reach), jnp.int32), jnp.zeros((blk, reach), jnp.int32)
    end = 0
    for i in range(lengths.shape[1]):
        end = end + lengths[0, i]
        q_doc = q_doc + jnp.where(q >= end, 1, 0)
        k_doc = k_doc + jnp.where(k >= end, 1, 0)
    seen = (q_doc == k_doc) & (k <= q) & (q - k < W) & (k >= 0)
    return jnp.where(seen, 0.0, NEG_FILL).astype(F32)


def shuffle():
    row = lax.broadcasted_iota(jnp.int32, (512, 512), 0)
    column = lax.broadcasted_iota(jnp.int32, (512, 512), 1)
    source = 64 * ((column >> 4) & 7) + 16 * (column >> 7) + (column & 15)
    return jnp.where(source == row, 1.0, 0.0).astype(BF)


def whole_vector(table, index, offset, count, size, lane):
    shift = size.bit_length() - 1
    row = lax.broadcasted_iota(jnp.int32, (128, 1024), 0)
    tile = lax.broadcasted_iota(jnp.int32, (128, 1024), 1)
    chosen = jnp.where(tile == row * 8 + index, 1.0, 0.0).astype(BF)
    share = dot(chosen, table, NN).astype(BF)
    row = lax.broadcasted_iota(jnp.int32, (128, count), 0)
    column = lax.broadcasted_iota(jnp.int32, (128, count), 1) + offset
    spread = jnp.where((column & (size - 1)) + lane == row, 1.0, 0.0).astype(BF)
    values = jnp.where((column >> shift) == row, dot(share, spread, NN), 0.0)
    return jnp.sum(values, axis=0, keepdims=True)


ORDER = (0, 1, 3, 2)


def remote(src, dst, sems, index, to):
    send, recv = sems
    return pltpu.make_async_remote_copy(
        src_ref=src,
        dst_ref=dst,
        send_sem=send.at[index],
        recv_sem=recv.at[index],
        device_id=to,
        device_id_type=pl.DeviceIdType.MESH,
    )


def forward_body(
    lengths,
    tok_in,
    small_in,
    wup_in,
    dy_in,
    wdn_in,
    wqkv_hbm,
    wout_hbm,
    vec_o,
    res_o,
    dhid_out,
    small_out,
    wq_h,
    wo_h,
    a1_h,
    q_h,
    kv_h,
    mixed_h,
    dattn_hbm,
    outp_hbm,
    up_a_own,
    up_b_own,
    dn_a_own,
    dn_b_own,
    up_a_got,
    up_b_got,
    dn_a_got,
    dn_b_got,
    wup,
    wdn,
    cc,
    wo,
    tokg,
    act,
    dup,
    dact,
    q,
    kv,
    mixed,
    dyg,
    part,
    got,
    own,
    outp,
    dattn,
    smalls,
    stack,
    uparts,
    local_sem,
    free_sem,
    rs_send,
    rs_recv,
    ff_send,
    ff_recv,
    send_sem,
    recv_sem,
):
    groups, taken = [], [0]

    def group(room):
        comm = Comm(send_sem, recv_sem, taken[0], room)
        taken[0] += room
        groups.append(comm)
        return comm

    c_q, c_o, c_u, c_d = group(36), group(26), group(26), group(26)
    c_small, c_tok, comm = group(28), group(4), group(32)
    sems = (ff_send, ff_recv)
    me = coords()
    x, y, z, core = me["x"], me["y"], me["z"], me["core"]
    other = 1 - core
    blk, width = tok_in.shape
    span = 4 * blk
    partw = q.shape[1]
    hidden = act.shape[1]
    heads = partw // HEAD
    reach = W + blk
    scale = 1.0 / math.sqrt(HEAD)
    mine16 = pl.ds(x * 16, 16)
    low, high = slice(0, 32), slice(32, 64)
    a1, up_c, dn_c, a2g = act, cc.at[0], cc.at[1], tokg
    wide = slice(0, 3 * partw)

    greet(ring("x") + plane() + near() + [scattered(), collected()])

    s_q = []
    for k in (1, 3, 2):
        for g in range(3):
            src = wqkv_hbm.at[:, pl.ds(g * width + lax.rem(x + k, 4) * partw, partw)]
            dst = cc.at[core, y, z, mine16, pl.ds(g * partw, partw)]
            s_q.append(c_q.push(src, dst, peer(x=k)))
    for g in range(3):
        src = wqkv_hbm.at[:, pl.ds(g * width + x * partw, partw)]
        s_q.append(c_q.local(src, cc.at[core, y, z, mine16, pl.ds(g * partw, partw)]))
    spot = smalls.at[y, core, pl.ds((z * 4 + x) * 8, 8)]
    s_small = [c_small.push(small_in, spot, to) for to in ring("x")]
    s_small.append(c_small.local(small_in, spot))
    s_o = [c_o.push(wout_hbm, wo.at[core, z, x], scattered())]
    tokens = Relay(
        c_tok, "x", lambda o: tokg.at[o], lambda o, h: tokg.at[o, pl.ds(h * blk // 2, blk // 2)]
    )
    tokens.start(tok_in)
    tokg[x] = tok_in[...]

    qkv_g = Gather(c_q, cc, True, [cut + (wide,) for cut in by_rows(64)])
    out_g = Gather(c_o, wo, True, by_columns(width), 3)
    down_g = Gather(c_d, wdn, False, by_rows(64))
    up_g = Gather(c_u, wup, False, by_rows(64))

    c_q.arrived(s_q)
    qkv_g.first()
    c_small.arrived(s_small)
    block = smalls.at[y, core, pl.ds(z * 32, 32)]
    s_small = [c_small.push(block, block, to) for to in plane()]

    slabs = 4 * hidden // 512
    for i in range(slabs):
        stack[16 * i : 16 * i + 16, :] = wup_in[:, 512 * i : 512 * i + 512]
    mixed_up = dot(stack[...], shuffle(), NN).astype(BF)
    for i in range(slabs):
        for to in range(4):
            uparts[to, :, 128 * i : 128 * i + 128] = mixed_up[
                16 * i : 16 * i + 16, 128 * to : 128 * to + 128
            ]

    c_q.arrived(qkv_g.one)
    qkv_g.second()
    c_o.arrived(s_o)
    out_g.first()
    c_small.arrived(s_small)
    s_small = []
    for other_y in range(4):
        block = smalls.at[other_y, core]
        s_small.append(c_small.push(block, block, peer(core=1)))
    tokens.near()
    s_u, s_d = [], []
    for k in (1, 3, 2):
        to = lax.rem(x + k, 4)
        s_d.append(
            c_d.push(wdn_in.at[pl.ds(to * 16, 16)], wdn.at[y, core, z, mine16], peer(x=k))
        )
        s_u.append(c_u.push(uparts.at[to], wup.at[y, core, z, mine16], peer(x=k)))
    s_d.append(c_d.local(wdn_in.at[mine16], wdn.at[y, core, z, mine16]))
    s_u.append(c_u.local(uparts.at[x], wup.at[y, core, z, mine16]))

    c_small.arrived(s_small)
    table = smalls[...].reshape(1024, 128).astype(BF)
    vec_o[0:1, :] = whole_vector(table, 0, 0, width, 16, 0)
    vec_o[1:2, :] = whole_vector(table, 1, 0, width, 16, 0)
    gain, shift = vec_o[0:1, :], vec_o[1:2, :]

    def norm_block(o):
        @pl.loop(0, blk // 16)
        def _(i):
            rows = pl.ds(pl.multiple_of(i * 16, 16), 16)
            v = tokg[o, rows, :].astype(F32)
            centred = v - jnp.mean(v, axis=-1, keepdims=True)
            s = lax.rsqrt(jnp.mean(centred * centred, axis=-1, keepdims=True) + EPSILON)
            at = pl.ds(pl.multiple_of(o * blk + i * 16, 16), 16)
            a1[at, :] = (centred * s * gain + shift).astype(BF)

    norm_block(x)
    qkv_g.near()
    c_o.arrived(out_g.one)
    out_g.second()
    norm_block(lax.rem(x + 1, 4))
    norm_block(lax.rem(x + 3, 4))
    qkv_g.far()
    out_g.near()
    c_d.arrived(s_d)
    down_g.first()
    c_u.arrived(s_u)
    up_g.first()
    tokens.far()
    s_dy = [comm.push(dy_in, dyg.at[p], peer(x=ORDER[p])) for p in (1, 2, 3)]
    dyg[0] = dy_in[...]
    norm_block(lax.rem(x + 2, 4))
    keep_a1 = [comm.local(a1, a1_h)]
    vec_o[2:3, :] = jnp.zeros((1, width), F32)
    vec_o[2:3, 0:partw] = whole_vector(table, 2, x * partw, partw, 32, 0)
    vec_o[2:3, 2 * partw : 3 * partw] = whole_vector(table, 2, width + x * partw, partw, 32, 0)
    qkv_g.done()

    def project(first):
        cols = slice(first, first + partw)
        total = vec_o[2:3, cols]
        rows = [
            jnp.concatenate([cc[0, j, :, :, cols], cc[1, j, :, :, cols]]).reshape(512, partw)
            for j in range(4)
        ]
        w = jnp.concatenate(rows)
        return (dot(a1[...], w, NN) + total).astype(BF)

    kv[W:, 0:partw] = project(partw)
    kv[W:, partw:] = project(2 * partw)
    s_edge = [comm.push(kv.at[pl.ds(span, W)], kv.at[pl.ds(0, W)], peer(z=1))]
    q[...] = project(0)
    keep_q = [c_q.local(cc.at[:, :, :, :, wide], wq_h)]
    comm.local(q, q_h)

    def attend(b):
        rows = pl.ds(pl.multiple_of(b * blk, blk), blk)
        window = pl.ds(pl.multiple_of(b * blk, blk), reach)
        mask = mask_of(lengths, z * span + b * blk, blk, reach)
        for h in range(heads):
            cols, vcols = pl.ds(h * HEAD, HEAD), pl.ds(partw + h * HEAD, HEAD)
            s = dot(q[rows, cols], kv[window, cols], NT) * scale + mask
            e = jnp.exp(s - jnp.max(s, axis=-1, keepdims=True))
            p = (e * (1.0 / jnp.sum(e, axis=-1, keepdims=True))).astype(BF)
            mixed[rows, cols] = dot(p, kv[window, vcols], NN).astype(BF)

    pl.loop(2, 4)(attend)
    out_g.far()
    c_d.arrived(down_g.one)
    down_g.second_a()
    c_u.arrived(up_g.one)
    up_g.second_a()
    for i in (3, 4, 5, 7):
        vec_o[i : i + 1, :] = whole_vector(table, i, 0, width, 16, 0)
    vec_o[6:7, :] = whole_vector(table, 6, 0, hidden, 16, x * 16)
    comm.arrived(s_edge)
    down_g.second_b()
    up_g.second_b()
    pl.loop(0, 2)(attend)
    comm.local(kv, kv_h)
    comm.local(mixed, mixed_h)
    out_g.done()
    c_o.local(wo, wo_h)
    c_tok.drain()

    def sends_attn(j):
        cols = pl.ds(pl.multiple_of(j * 512, 512), 512)
        return [
            remote(
                part.at[lax.rem(x + k, 4), :, cols],
                got.at[k - 1, :, cols],
                (rs_send, rs_recv),
                3 * j + k - 1,
                peer(x=k),
            )
            for k in (2, 1, 3)
        ]

    @pl.loop(0, 4)
    def _(j):
        cols = pl.ds(pl.multiple_of(j * 512, 512), 512)
        d = dot(mixed[...], wo[:, :, :, :, cols].reshape(partw, 512), NN)
        part[:, :, cols] = d.astype(BF).reshape(4, blk, 512)
        dact[:, 0:512] = d
        own[:, cols] = dact[pl.ds(pl.multiple_of(x * blk, blk), blk), 0:512]
        for copy in sends_attn(j):
            copy.start()

    c_q.drain()
    pl.semaphore_signal(
        free_sem, inc=1, device_id=peer(core=1), device_id_type=pl.DeviceIdType.MESH
    )

    down_g.near_a()
    up_g.near_a()
    down_g.near_b()
    down_g.far_a()
    up_g.near_b()
    up_g.far_a()

    @pl.loop(0, 4)
    def _(j):
        for copy in sends_attn(j):
            copy.wait_recv()

    b_out, gain2, shift2 = vec_o[3:4, :], vec_o[4:5, :], vec_o[5:6, :]

    @pl.loop(0, blk // 16)
    def _(i):
        rows = pl.ds(pl.multiple_of(i * 16, 16), 16)
        v = tok_in[rows, :].astype(F32) + own[rows, :] + b_out
        for g in range(3):
            v = v + got[g, rows, :].astype(F32)
        res_o[rows, :] = v
        centred = v - jnp.mean(v, axis=-1, keepdims=True)
        s = lax.rsqrt(jnp.mean(centred * centred, axis=-1, keepdims=True) + EPSILON)
        a2g[0, rows, :] = (centred * s * gain2 + shift2).astype(BF)

    spread = [comm.push(a2g.at[0], a2g.at[p], peer(x=ORDER[p])) for p in (1, 2)]
    down_g.far_b()
    up_g.far_b()

    @pl.loop(0, 4)
    def _(j):
        for copy in sends_attn(j):
            copy.wait_send()

    comm.arrived(keep_a1 + s_dy)
    down_g.done()

    @pl.loop(0, 4)
    def _(j):
        tile = wdn[j].reshape(512, width)
        cols = pl.ds(pl.multiple_of(j * 512, 512), 512)
        dact[:, cols] = dot(dyg[...].reshape(span, width), tile, NT)

    comm.arrived(spread)
    top, bottom = pl.ds(0, blk // 2), pl.ds(blk // 2, blk // 2)
    passed = [
        comm.push(a2g.at[1, top], a2g.at[3, top], peer(x=1)),
        comm.push(a2g.at[2, bottom], a2g.at[3, bottom], peer(x=3)),
    ]
    up_g.done()
    comm.arrived(passed)

    @pl.loop(0, hidden // 256)
    def _(j):
        cols = pl.ds(pl.multiple_of(j * 256, 256), 256)
        u = dot(a2g[...].reshape(span, width), wup[:, :, :, :, cols].reshape(width, 256), NN)
        u = u + vec_o[6:7, cols]
        phi = 0.5 + 0.5 * lax.erf(u * math.sqrt(0.5))
        act[:, cols] = (u * phi).astype(BF)
        slope = phi + u * (jnp.exp(-0.5 * u * u) * (1.0 / math.sqrt(2.0 * math.pi)))
        d_up = (dact[:, cols] * slope).astype(BF)
        dup[:, cols] = d_up
        small_out[3:4, cols] = jnp.sum(d_up.astype(F32), axis=0, keepdims=True)

    def sends(j):
        cols = pl.ds(pl.multiple_of(j * 512, 512), 512)
        return [
            remote(
                part.at[p - 1, :, cols],
                got.at[p - 1, :, cols],
                sems,
                4 + 3 * j + p - 1,
                peer(x=-ORDER[p]),
            )
            for p in (3, 1, 2)
        ]

    @pl.loop(0, 4)
    def _(j):
        cols = pl.ds(pl.multiple_of(j * 512, 512), 512)
        d = dot(dup[...], wup[j].reshape(512, hidden), NT)
        own[:, cols] = d[:blk]
        for p in (1, 2, 3):
            part[p - 1, :, cols] = d[p * blk : (p + 1) * blk].astype(BF)
        for copy in sends(j):
            copy.start()

    def grad_down(t, c):
        cols = pl.ds(pl.multiple_of(t * 512 + c * 256, 256), 256)
        return dot(act[:, cols], dyg[...].reshape(span, width), TN)

    def grad_up(t, c):
        cols = pl.ds(pl.multiple_of(t * 512 + c * 256, 256), 256)
        return dot(a2g[:, :, cols].reshape(span, 256), dup[...], TN)

    def swap_down(t):
        return remote(wdn.at[t, other], dn_c.at[t], sems, 16 + t, peer(core=1))

    def swap_up(t):
        return remote(wup.at[t, other], up_c.at[t], sems, 20 + t, peer(core=1))

    c_u.drain()
    pl.semaphore_wait(free_sem, 1)

    @pl.loop(0, 4)
    def _(t):
        wup[t, other] = grad_up(t, other).astype(BF).reshape(4, 64, hidden)
        swap_up(t).start()

    first = []

    def stage(src, dst, index, to):
        first.append(remote(src, dst, sems, index, to))
        first[-1].start()

    @pl.loop(0, 4)
    def _(t):
        swap_up(t).wait_recv()
        total = grad_up(t, core) + up_c[t].reshape(256, hidden).astype(F32)
        wup[t, core] = total.astype(BF).reshape(4, 64, hidden)

    for k in (1, 3, 2):
        zz, yy = lax.rem(z + k, 4), lax.rem(y + k, 4)
        stage(wup.at[:, core, zz, low], up_a_got.at[k - 1], 32 + k, peer(z=k))
        stage(wup.at[yy, core, :, high], up_b_got.at[k - 1], 36 + k, peer(y=k))

    @pl.loop(0, 4)
    def _(j):
        cols = pl.ds(pl.multiple_of(j * 512, 512), 512)
        o = dot(act[...], wdn[:, :, :, :, cols].reshape(hidden, 512), NN)
        outp[:, :, cols] = o.astype(BF).reshape(4, blk, 512)

    keep_out = pltpu.make_async_copy(outp, outp_hbm, local_sem.at[0])
    keep_out.start()

    c_d.drain()

    @pl.loop(0, 4)
    def _(t):
        wdn[t, other] = grad_down(t, other).astype(BF).reshape(4, 64, width)
        swap_down(t).start()

    @pl.loop(0, 4)
    def _(t):
        swap_down(t).wait_recv()
        total = grad_down(t, core) + dn_c[t].reshape(256, width).astype(F32)
        wdn[t, core] = total.astype(BF).reshape(4, 64, width)

    for k in (1, 3, 2):
        zz, yy = lax.rem(z + k, 4), lax.rem(y + k, 4)
        stage(wdn.at[:, core, zz, low], dn_a_got.at[k - 1], 24 + k, peer(z=k))
        stage(wdn.at[yy, core, :, high], dn_b_got.at[k - 1], 28 + k, peer(y=k))

    @pl.loop(0, 4)
    def _(j):
        for copy in sends(j):
            copy.wait_recv()

    small_out[0:3, :] = jnp.zeros((3, width), F32)
    small_out[4:8, :] = jnp.zeros((4, width), F32)
    gain = vec_o[4:5, :]

    @pl.loop(0, blk // 16)
    def _(i):
        rows = pl.ds(pl.multiple_of(i * 16, 16), 16)
        d = own[rows, :]
        for p in range(3):
            d = d + got[p, rows, :].astype(F32)
        v = res_o[rows, :]
        centred = v - jnp.mean(v, axis=-1, keepdims=True)
        s = lax.rsqrt(jnp.mean(centred * centred, axis=-1, keepdims=True) + EPSILON)
        n = centred * s
        dn = d * gain
        d_res = s * (
            dn
            - jnp.mean(dn, axis=-1, keepdims=True)
            - n * jnp.mean(dn * n, axis=-1, keepdims=True)
        )
        dy_own = dy_in[rows, :].astype(F32)
        hid = dy_own + d_res
        low_hid = hid.astype(BF)
        dhid_out[rows, :] = hid
        dattn[x, rows, :] = low_hid
        small_out[0:1, :] += jnp.sum(d * n, axis=0, keepdims=True)
        small_out[1:2, :] += jnp.sum(d, axis=0, keepdims=True)
        small_out[2:3, :] += jnp.sum(low_hid.astype(F32), axis=0, keepdims=True)
        small_out[4:5, :] += jnp.sum(dy_own, axis=0, keepdims=True)

    attn = Relay(
        comm, "x", lambda o: dattn.at[o], lambda o, h: dattn.at[o, pl.ds(h * blk // 2, blk // 2)]
    )
    attn.start()
    kept = [keep_out]
    kept.append(pltpu.make_async_copy(wdn.at[:, core, z, low], dn_a_own, local_sem.at[2]))
    kept.append(pltpu.make_async_copy(wdn.at[y, core, :, high], dn_b_own, local_sem.at[3]))
    kept.append(pltpu.make_async_copy(wup.at[:, core, z, low], up_a_own, local_sem.at[4]))
    kept.append(pltpu.make_async_copy(wup.at[y, core, :, high], up_b_own, local_sem.at[5]))
    for copy in kept[1:]:
        copy.start()
    attn.near()
    attn.far()
    kept.append(pltpu.make_async_copy(dattn, dattn_hbm, local_sem.at[1]))
    kept[-1].start()

    for copy in first:
        copy.wait_recv()
    for copy in first:
        copy.wait_send()

    @pl.loop(0, 4)
    def _(j):
        for copy in sends(j):
            copy.wait_send()
        swap_down(j).wait_send()
        swap_up(j).wait_send()

    for copy in kept:
        copy.wait()
    for done in groups:
        done.drain()


def forward(collective_id, lengths, tok, small, w_up, dy, w_down, w_qkv, w_out):
    blk, width = tok.shape
    span, partw, hidden = 4 * blk, width // 4, w_up.shape[1] // 4
    vmem = pl.BlockSpec(memory_space=pltpu.VMEM)
    hbm = pl.BlockSpec(memory_space=pl.ANY)
    quarter = (4, 32, width)
    outs = [
        ((8, width), F32, vmem),
        ((blk, width), F32, vmem),
        ((blk, width), F32, vmem),
        ((8, width), F32, vmem),
        ((2, 4, 4, 64, 3 * partw), BF, hbm),
        ((2, 4, 4, 16, width), BF, hbm),
        ((span, width), BF, hbm),
        ((span, partw), BF, hbm),
        ((span + W, 2 * partw), BF, hbm),
        ((span, partw), BF, hbm),
        ((4, blk, width), BF, hbm),
        ((4, blk, width), BF, hbm),
    ]
    outs += [(quarter, BF, hbm)] * 4 + [((3,) + quarter, BF, hbm)] * 4
    scratch = [
        ((4, 2, 4, 64, hidden), BF),
        ((4, 2, 4, 64, width), BF),
        ((2, 4, 4, 64, width), BF),
        ((2, 4, 4, 16, width), BF),
        ((4, blk, width), BF),
        ((span, hidden), BF),
        ((span, hidden), BF),
        ((span, hidden), F32),
        ((span, partw), BF),
        ((span + W, 2 * partw), BF),
        ((span, partw), BF),
        ((4, blk, width), BF),
        ((4, blk, width), BF),
        ((3, blk, width), BF),
        ((blk, width), F32),
        ((4, blk, width), BF),
        ((4, blk, width), BF),
        ((4, 2, 128, 128), F32),
        ((hidden // 8, 512), BF),
        ((4, 16, hidden), BF),
    ]
    return pl.pallas_call(
        forward_body,
        out_shape=tuple(jax.ShapeDtypeStruct(s, d) for s, d, _ in outs),
        in_specs=[pl.BlockSpec(memory_space=pltpu.SMEM)] + [vmem] * 5 + [hbm] * 2,
        out_specs=tuple(o[2] for o in outs),
        scratch_shapes=[pltpu.VMEM(s, d) for s, d in scratch]
        + [pltpu.SemaphoreType.DMA((8,)), pltpu.SemaphoreType.REGULAR]
        + [pltpu.SemaphoreType.DMA((n,)) for n in (12, 12, 40, 40, SEMS, SEMS)],
        compiler_params=pltpu.CompilerParams(
            collective_id=collective_id, has_side_effects=True, vmem_limit_bytes=63 << 20
        ),
        name="forward",
    )(lengths, tok, small, w_up, dy, w_down, w_qkv, w_out)


def norm_backward(d, v, gain):
    centred = v - jnp.mean(v, axis=-1, keepdims=True)
    s = lax.rsqrt(jnp.mean(centred * centred, axis=-1, keepdims=True) + EPSILON)
    n = centred * s
    dn = d * gain
    d_v = s * (
        dn - jnp.mean(dn, axis=-1, keepdims=True) - n * jnp.mean(dn * n, axis=-1, keepdims=True)
    )
    return d_v, n


def attention_backward_body(
    lengths,
    vec_in,
    ffsmall_in,
    dattn_hbm,
    wout_hbm,
    q_hbm,
    kv_hbm,
    a1_hbm,
    mixed_hbm,
    wqkv_hbm,
    tok_hbm,
    dhid_hbm,
    res_hbm,
    outp_hbm,
    ffo0,
    ffo1,
    ffo2,
    ffo3,
    ffg0,
    ffg1,
    ffg2,
    ffg3,
    out_o,
    gtok_o,
    gqkv_o,
    gout_o,
    gup_o,
    gdn_o,
    small_o,
    late_o,
    dattn,
    wout,
    q_all,
    kv,
    a1,
    mixed,
    wqkv,
    tok,
    dhid,
    res,
    outown,
    outgot,
    fo,
    fg,
    fs,
    fg2,
    fup,
    fdn,
    dmix,
    dkv,
    dqkv,
    dedge,
    dedge_got,
    part,
    got,
    qkv_c,
    out_c,
    qa,
    qb,
    oa,
    ob,
    qs,
    os_,
    qa2,
    qb2,
    oa2,
    ob2,
    fq,
    fout,
    sm,
    smc,
    smz,
    smy,
    late,
    late_c,
    late_p,
    late_sum,
    gux,
    stack,
    gq,
    local_sem,
    send_sem,
    recv_sem,
):
    sems = (send_sem, recv_sem)
    me = coords()
    x, y, z, core = me["x"], me["y"], me["z"], me["core"]
    other = 1 - core
    zy = lax.rem(y + 3, 4)
    blk, width = tok.shape
    span = 4 * blk
    partw = mixed.shape[1]
    heads = partw // HEAD
    scale = 1.0 / math.sqrt(HEAD)
    reach = W + blk
    used = [0]
    pending = []

    def load(src, dst):
        copy = pltpu.make_async_copy(src, dst, local_sem.at[used[0]])
        used[0] += 1
        copy.start()
        return copy

    def push(src, dst, index, to):
        copy = remote(src, dst, sems, index, to)
        copy.start()
        pending.append(copy)
        return copy

    l_dattn, l_wout = load(dattn_hbm, dattn), load(wout_hbm, wout)
    l_attn = [load(q_hbm, q_all), load(kv_hbm, kv)]
    low, high = slice(0, 32), slice(32, 64)
    l_ff = [load(s, fo.at[i]) for i, s in enumerate((ffo0, ffo1, ffo2, ffo3))]
    l_ff += [load(s, fg.at[i]) for i, s in enumerate((ffg0, ffg1, ffg2, ffg3))]
    l_wqkv, l_a1, l_mixed = load(wqkv_hbm, wqkv), load(a1_hbm, a1), load(mixed_hbm, mixed)
    l_end = [load(outp_hbm.at[0], outown), load(res_hbm, res)]
    l_end += [load(tok_hbm, tok), load(dhid_hbm, dhid)]

    greet(ring("x") + plane() + near() + [scattered(), collected()])

    p_out = [
        push(outp_hbm.at[p], outgot.at[p - 1], p, peer(x=-ORDER[p])) for p in (1, 2, 3)
    ]

    dkv[...] = jnp.zeros(dkv.shape, F32)
    l_dattn.wait()
    l_wout.wait()
    dmix[...] = dot(
        dattn[...].reshape(span, width), wout[...].reshape(partw, width), NT
    ).astype(BF)
    for copy in l_attn:
        copy.wait()

    def block(b):
        rows = pl.ds(pl.multiple_of(b * blk, blk), blk)
        window = pl.ds(pl.multiple_of(b * blk, blk), reach)
        mask = mask_of(lengths, z * span + b * blk, blk, reach)
        for h in range(heads):
            cols = pl.ds(h * HEAD, HEAD)
            vcols = pl.ds(partw + h * HEAD, HEAD)
            q, k, v = q_all[rows, cols], kv[window, cols], kv[window, vcols]
            s = dot(q, k, NT) * scale + mask
            e = jnp.exp(s - jnp.max(s, axis=-1, keepdims=True))
            p = e * (1.0 / jnp.sum(e, axis=-1, keepdims=True))
            do = dmix[rows, cols]
            dp = dot(do, v, NT)
            ds = (p * (dp - jnp.sum(dp * p, axis=-1, keepdims=True))).astype(BF)
            dqkv[rows, cols] = (dot(ds, k, NN) * scale).astype(BF)
            dkv[window, cols] += dot(ds, q, TN) * scale
            dkv[window, vcols] += dot(p.astype(BF), do, TN)

    pl.loop(0, 2)(block)
    dedge[...] = dkv[0:W, :].astype(BF)
    p_edge = push(dedge, dedge_got, 4, peer(z=3))

    def ff_sum(i):
        for c in range(4):
            total = fo[i, c].astype(F32)
            for g in range(3):
                total = total + fg[i, g, c].astype(F32)
            fs[i, c] = total.astype(BF)

    p_ff = []

    def ff_second(i):
        axis, here = ("y", y) if i % 2 == 0 else ("z", z)
        for k in (1, 3, 2):
            src = fs.at[i, lax.rem(here + k, 4)]
            p_ff.append(push(src, fg2.at[i, k - 1], 4 + 3 * i + k, peer(**{axis: k})))

    for copy in l_ff:
        copy.wait()
    for i in range(4):
        ff_sum(i)
    ff_second(0)
    ff_second(2)
    pl.loop(2, 4)(block)

    p_edge.wait_recv()
    ff_second(1)
    ff_second(3)
    dqkv[0 : span - W, partw:] = dkv[W:span, :].astype(BF)
    dqkv[span - W :, partw:] = (dkv[span:, :] + dedge_got[...].astype(F32)).astype(BF)
    sm[0, 0:5, :] = ffsmall_in[0:5, :]
    sm[0, 5:8, :] = jnp.zeros((3, width), F32)
    sm[0, 7:8, 0 : 3 * partw] = jnp.sum(dqkv[...].astype(F32), axis=0, keepdims=True)
    p_sc = push(sm.at[0], smc, 53, peer(core=1))

    def sends(j):
        cols = pl.ds(pl.multiple_of(j * 512, 512), 512)
        return [
            remote(
                part.at[lax.rem(x + k, 4), :, cols],
                got.at[k - 1, :, cols],
                sems,
                20 + 3 * j + k - 1,
                peer(x=k),
            )
            for k in (2, 1, 3)
        ]

    def grad_qkv(t, c):
        cols = pl.ds(pl.multiple_of(t * 512 + c * 256, 256), 256)
        return dot(a1[:, cols], dqkv[...], TN)

    def grad_out(c):
        cols = pl.ds(pl.multiple_of(c * 256, 256), 256)
        return dot(mixed[:, cols], dattn[...].reshape(span, width), TN)

    def swap(t):
        return remote(gq.at[t, 1], qkv_c.at[t], sems, 32 + t, peer(core=1))

    l_a1.wait()

    @pl.loop(0, 4)
    def _(t):
        gq[t, 1] = grad_qkv(t, other).astype(BF).reshape(4, 64, 3 * partw)
        swap(t).start()

    l_mixed.wait()
    wout[other] = grad_out(other).astype(BF).reshape(4, 4, 16, width)
    p_oc = push(wout.at[other], out_c, 36, peer(core=1))

    @pl.loop(0, 4)
    def _(t):
        swap(t).wait_recv()
        total = grad_qkv(t, core) + qkv_c[t].reshape(256, 3 * partw).astype(F32)
        gq[t, 0] = total.astype(BF).reshape(4, 64, 3 * partw)

    left, right = slice(0, width // 2), slice(width // 2, width)
    p_q1, p_o1 = [], []
    for k in (1, 3, 2):
        tz, ty = lax.rem(z + k, 4), lax.rem(y + k, 4)
        p_q1.append(push(gq.at[:, 0, tz, low], qa.at[k - 1], 36 + k, peer(z=k)))
        p_q1.append(push(gq.at[ty, 0, :, high], qb.at[k - 1], 39 + k, peer(y=k)))

    l_wqkv.wait()

    @pl.loop(0, 4)
    def _(j):
        cols = pl.ds(pl.multiple_of(j * 512, 512), 512)
        d = dot(dqkv[...], wqkv[:, j].reshape(512, 3 * partw), NT)
        part[:, :, cols] = d.astype(BF).reshape(4, blk, 512)
        for copy in sends(j):
            copy.start()

    p_sc.wait_recv()
    sm[1] = sm[0] + smc[...]
    p_sz = [push(sm.at[1], smz.at[k - 1], 59 + k, peer(z=k)) for k in (1, 3, 2)]
    p_oc.wait_recv()
    wout[core] = (
        grad_out(core) + out_c[...].reshape(256, width).astype(F32)
    ).astype(BF).reshape(4, 4, 16, width)
    for k in (1, 3, 2):
        tz, tyc = lax.rem(z + k, 4), lax.rem(y + k + 3, 4)
        p_o1.append(push(wout.at[core, :, tz, :, left], oa.at[k - 1], 42 + k, peer(z=k)))
        p_o1.append(push(wout.at[core, tyc, :, :, right], ob.at[k - 1], 45 + k, peer(y=k)))

    for copy in l_end:
        copy.wait()
    for copy in p_out:
        copy.wait_recv()

    @pl.loop(0, blk // 16)
    def _(i):
        rows = pl.ds(pl.multiple_of(i * 16, 16), 16)
        total = res[rows, :] + vec_in[7:8, :] + outown[rows, :].astype(F32)
        for g in range(3):
            total = total + outgot[g, rows, :].astype(F32)
        out_o[rows, :] = total.astype(BF)

    for copy in p_q1:
        copy.wait_recv()
    for c in range(4):
        ta, tb = gq[c, 0, z, low].astype(F32), gq[y, 0, c, high].astype(F32)
        for g in range(3):
            ta, tb = ta + qa[g, c].astype(F32), tb + qb[g, c].astype(F32)
        qs[0, c], qs[1, c] = ta.astype(BF), tb.astype(BF)
    p_q2 = []
    for k in (1, 3, 2):
        tz, ty = lax.rem(z + k, 4), lax.rem(y + k, 4)
        p_q2.append(push(qs.at[0, ty], qa2.at[k - 1], 53 + k, peer(y=k)))
        p_q2.append(push(qs.at[1, tz], qb2.at[k - 1], 56 + k, peer(z=k)))

    for copy in p_sz:
        copy.wait_recv()
    sm[2] = sm[1] + smz[0] + smz[1] + smz[2]
    p_sy = [push(sm.at[2], smy.at[k - 1], 68 + k, peer(y=k)) for k in (1, 3, 2)]
    for copy in p_o1:
        copy.wait_recv()
    for c in range(4):
        ta, tb = wout[core, c, z, :, left].astype(F32), wout[core, zy, c, :, right].astype(F32)
        for g in range(3):
            ta, tb = ta + oa[g, c].astype(F32), tb + ob[g, c].astype(F32)
        os_[0, c], os_[1, c] = ta.astype(BF), tb.astype(BF)
    p_o2 = []
    for k in (1, 3, 2):
        tz, tyc = lax.rem(z + k, 4), lax.rem(y + k + 3, 4)
        p_o2.append(push(os_.at[0, tyc], oa2.at[k - 1], 62 + k, peer(y=k)))
        p_o2.append(push(os_.at[1, tz], ob2.at[k - 1], 65 + k, peer(z=k)))

    late_sum[...] = jnp.zeros(late_sum.shape, F32)

    @pl.loop(0, 4)
    def _(j):
        for copy in sends(j):
            copy.wait_recv()

    gain = vec_in[0:1, :]

    @pl.loop(0, blk // 16)
    def _(i):
        rows = pl.ds(pl.multiple_of(i * 16, 16), 16)
        d = part[x, rows, :].astype(F32)
        for g in range(3):
            d = d + got[g, rows, :].astype(F32)
        d_in, n = norm_backward(d, tok[rows, :].astype(F32), gain)
        gtok_o[rows, :] = dhid[rows, :] + d_in
        late_sum[0:1, :] += jnp.sum(d * n, axis=0, keepdims=True)
        late_sum[1:2, :] += jnp.sum(d, axis=0, keepdims=True)

    for i in range(8):
        at = (i % 4) * (width // 4)
        late[0, i : i + 1, :] = late_sum[i // 4 : i // 4 + 1, at : at + width // 4]
    p_lc = push(late.at[0], late_c, 52, peer(core=1))
    p_lc.wait_recv()
    late[1] = late[0] + late_c[...]
    p_lz = [push(late.at[1], late_p.at[i], 98 + i, to) for i, to in enumerate(plane())]

    for copy in p_sy:
        copy.wait_recv()
    sm[3] = sm[2] + smy[0] + smy[1] + smy[2]
    p_x = [push(sm.at[3], small_o.at[x], 71 + k, peer(x=k)) for k in (1, 3, 2)]
    kept = [load(sm.at[3], small_o.at[x])]


    for copy in p_ff:
        copy.wait_recv()
    at = (y, z, y, z)
    for i in range(4):
        total = fs[i, at[i]].astype(F32)
        for g in range(3):
            total = total + fg2[i, g].astype(F32)
        into, half = (fup, fdn)[i // 2], i % 2
        into[2 * half : 2 * half + 2] = total.astype(BF).reshape(2, 16, width)
    p_u = []
    for k in (1, 3, 2):
        p_u.append(push(fup.at[lax.rem(x + k, 4)], gux.at[x], 48 + k, peer(x=k)))
        p_x.append(push(fdn.at[lax.rem(x + k, 4)], gdn_o.at[x], 76 + k, peer(x=k)))
    gux[x] = fup[x]
    kept.append(load(fdn.at[x], gdn_o.at[x]))

    for copy in p_q2:
        copy.wait_recv()
    ta, tb = qs[0, y].astype(F32), qs[1, z].astype(F32)
    for g in range(3):
        ta, tb = ta + qa2[g].astype(F32), tb + qb2[g].astype(F32)
    fq[0:2] = ta.astype(BF).reshape(2, 16, 3 * partw)
    fq[2:4] = tb.astype(BF).reshape(2, 16, 3 * partw)
    for g in range(3):
        block_cols, own_cols = pl.ds(g * partw, partw), pl.ds(g * width + x * partw, partw)
        for k in (1, 3, 2):
            src = fq.at[lax.rem(x + k, 4), :, block_cols]
            p_x.append(push(src, gqkv_o.at[:, own_cols], 83 + 3 * g + k - 1, peer(x=k)))
        kept.append(load(fq.at[x, :, block_cols], gqkv_o.at[:, own_cols]))

    for copy in p_o2:
        copy.wait_recv()
    ta, tb = os_[0, zy].astype(F32), os_[1, z].astype(F32)
    for g in range(3):
        ta, tb = ta + oa2[g].astype(F32), tb + ob2[g].astype(F32)
    fout[:, left], fout[:, right] = ta.astype(BF), tb.astype(BF)
    p_x.append(push(fout, gout_o, 75, collected()))

    for copy in p_lz:
        copy.wait_recv()
    total = late[1]
    for i in range(15):
        total = total + late_p[i]
    late[2] = total
    p_x += [push(late.at[2], late_o.at[x], 79 + k, peer(x=k)) for k in (1, 3, 2)]
    kept.append(load(late.at[2], late_o.at[x]))

    for copy in p_u:
        copy.wait_recv()
    slabs = width // 128
    for i in range(slabs):
        for c in range(4):
            stack[16 * i : 16 * i + 16, 128 * c : 128 * c + 128] = gux[
                c, :, 128 * i : 128 * i + 128
            ]
    spread_up = dot(stack[...], shuffle(), NT)
    for i in range(slabs):
        gup_o[:, 512 * i : 512 * i + 512] = spread_up[16 * i : 16 * i + 16, :]

    for copy in p_x:
        copy.wait_recv()
    for copy in pending:
        copy.wait_send()

    @pl.loop(0, 4)
    def _(j):
        for copy in sends(j):
            copy.wait_send()
        swap(j).wait_send()

    for copy in kept:
        copy.wait()


def attention_backward(
    collective_id,
    lengths,
    vectors,
    ff_small,
    d_attn,
    wout,
    q,
    kv,
    a1,
    mixed,
    wqkv,
    tok,
    d_hidden,
    residual,
    out_part,
    ff_own,
    ff_got,
):
    blk, width = tok.shape
    span, partw = mixed.shape
    hidden = ff_own[0].shape[-1]
    vmem = pl.BlockSpec(memory_space=pltpu.VMEM)
    hbm = pl.BlockSpec(memory_space=pl.ANY)
    outs = [
        ((blk, width), BF, vmem),
        ((blk, width), F32, vmem),
        ((16, 3 * width), BF, hbm),
        ((16, width), BF, hbm),
        ((16, 4 * hidden), F32, vmem),
        ((4, 16, width), BF, hbm),
        ((4, 8, width), F32, hbm),
        ((4, 8, width // 4), F32, hbm),
    ]
    half = width // 2
    scratch = [
        ((4, blk, width), BF),
        ((2, 4, 4, 16, width), BF),
        ((span, partw), BF),
        ((span + W, 2 * partw), BF),
        ((span, width), BF),
        ((span, partw), BF),
        ((2, 4, 4, 64, 3 * partw), BF),
        ((blk, width), BF),
        ((blk, width), F32),
        ((blk, width), F32),
        ((blk, width), BF),
        ((3, blk, width), BF),
        ((4, 4, 32, width), BF),
        ((4, 3, 4, 32, width), BF),
        ((4, 4, 32, width), BF),
        ((4, 3, 32, width), BF),
        ((4, 16, hidden), BF),
        ((4, 16, width), BF),
        ((span, partw), BF),
        ((span + W, 2 * partw), F32),
        ((span, 3 * partw), BF),
        ((W, 2 * partw), BF),
        ((W, 2 * partw), BF),
        ((4, blk, width), BF),
        ((3, blk, width), BF),
        ((4, 4, 64, 3 * partw), BF),
        ((4, 4, 16, width), BF),
        ((3, 4, 32, 3 * partw), BF),
        ((3, 4, 32, 3 * partw), BF),
        ((3, 4, 16, half), BF),
        ((3, 4, 16, half), BF),
        ((2, 4, 32, 3 * partw), BF),
        ((2, 4, 16, half), BF),
        ((3, 32, 3 * partw), BF),
        ((3, 32, 3 * partw), BF),
        ((3, 16, half), BF),
        ((3, 16, half), BF),
        ((4, 16, 3 * partw), BF),
        ((16, width), BF),
        ((4, 8, width), F32),
        ((8, width), F32),
        ((3, 8, width), F32),
        ((3, 8, width), F32),
        ((3, 8, width // 4), F32),
        ((8, width // 4), F32),
        ((15, 8, width // 4), F32),
        ((2, width), F32),
        ((4, 16, hidden), BF),
        ((hidden // 8, 512), BF),
        ((4, 2, 4, 64, 3 * partw), BF),
    ]
    return pl.pallas_call(
        attention_backward_body,
        out_shape=tuple(jax.ShapeDtypeStruct(s, d) for s, d, _ in outs),
        in_specs=[pl.BlockSpec(memory_space=pltpu.SMEM)] + [vmem] * 2 + [hbm] * 19,
        out_specs=tuple(o[2] for o in outs),
        scratch_shapes=[pltpu.VMEM(s, d) for s, d in scratch]
        + [
            pltpu.SemaphoreType.DMA((32,)),
            pltpu.SemaphoreType.DMA((114,)),
            pltpu.SemaphoreType.DMA((114,)),
        ],
        compiler_params=pltpu.CompilerParams(
            collective_id=collective_id, has_side_effects=True, vmem_limit_bytes=62 << 20
        ),
        name="attention_backward",
    )(
        lengths,
        vectors,
        ff_small,
        d_attn,
        wout,
        q,
        kv,
        a1,
        mixed,
        wqkv,
        tok,
        d_hidden,
        residual,
        out_part,
        *ff_own,
        *ff_got,
    )


def results_body(
    out,
    gtok,
    gqkv,
    gout,
    gup,
    gdn,
    small,
    late,
    out_o,
    gtok_o,
    gain1_o,
    shift1_o,
    gqkv_o,
    bqv_o,
    gout_o,
    bout_o,
    gain2_o,
    shift2_o,
    gup_o,
    bup_o,
    gdn_o,
    bdown_o,
    sums,
):
    me = coords()
    device = ((me["y"] * 2 + me["core"]) * 4 + me["z"]) * 4 + me["x"]
    out_o[...] = out[...]
    gtok_o[...] = gtok[...]
    gqkv_o[...] = gqkv[...].astype(F32)
    gout_o[...] = gout[...].astype(F32)
    gup_o[...] = gup[...]
    gdn_o[...] = gdn[...].reshape(gdn_o.shape).astype(F32)

    tile = pl.ds(pl.multiple_of(device // 8 * 128, 128), 128)
    turn = lax.rem(128 - 16 * lax.rem(device, 8), 128)
    shares = [pltpu.roll(small[i, :, tile], turn, 1) for i in range(4)]
    total = shares[0] + shares[1] + shares[2] + shares[3]
    gain2_o[...] = total[0:1, 0:16]
    shift2_o[...] = total[1:2, 0:16]
    bout_o[...] = total[2:3, 0:16]
    bdown_o[...] = total[4:5, 0:16]
    for i in range(4):
        bup_o[:, 16 * i : 16 * i + 16] = shares[i][3:4, 0:16]

    sums[...] = late[0] + late[1] + late[2] + late[3]
    place = lax.rem(device, 32)
    tile = pl.ds(pl.multiple_of(place // 8 * 128, 128), 128)
    turned = pltpu.roll(sums[:, tile], turn, 1)
    row = lax.broadcasted_iota(jnp.int32, turned.shape, 0)

    def only(i):
        return jnp.sum(jnp.where(row == i, turned, 0.0), axis=0, keepdims=True)[:, 0:16]

    gain1_o[...] = only(device // 32)
    shift1_o[...] = only(4 + device // 32)

    half, place = device // 64, lax.rem(device, 16)
    tile = pl.ds(pl.multiple_of(half * 1024 + place // 4 * 128, 128), 128)
    turn = lax.rem(128 - 32 * lax.rem(device, 4), 128)
    bqv_o[...] = pltpu.roll(small[lax.rem(device, 64) // 16, :, tile], turn, 1)[7:8, 0:32]


def results(*arrays):
    out, gtok, gqkv, gout, gup, gdn = arrays[:6]
    vmem = pl.BlockSpec(memory_space=pltpu.VMEM)
    rows, vector = gdn.shape[0] * gdn.shape[1], lambda n: ((1, n), F32)
    outs = [
        (out.shape, BF),
        (gtok.shape, F32),
        vector(16),
        vector(16),
        (gqkv.shape, F32),
        vector(32),
        (gout.shape, F32),
        vector(16),
        vector(16),
        vector(16),
        (gup.shape, F32),
        vector(64),
        ((rows, gdn.shape[2]), F32),
        vector(16),
    ]
    return pl.pallas_call(
        results_body,
        out_shape=tuple(jax.ShapeDtypeStruct(s, d) for s, d in outs),
        in_specs=[vmem] * 8,
        out_specs=(vmem,) * 14,
        scratch_shapes=[pltpu.VMEM(arrays[7].shape[1:], F32)],
        compiler_params=pltpu.CompilerParams(vmem_limit_bytes=40 << 20),
        name="results",
    )(*arrays)


def local(
    tokens,
    grad_out,
    lengths,
    ln1_gain,
    ln1_bias,
    w_qkv,
    b_qv,
    w_out,
    b_out,
    ln2_gain,
    ln2_bias,
    w_up,
    b_up,
    w_down,
    b_down,
):
    blk, width = tokens.shape[1:]
    part = width // 4
    hidden = w_up.shape[1] // 4
    tok = tokens.reshape(blk, width)
    dy = grad_out.reshape(blk, width)
    small = jnp.zeros((1024,), F32)
    vectors = (ln1_gain, ln1_bias, b_qv, b_out, ln2_gain, ln2_bias, b_up, b_down)
    for i, vector in enumerate(vectors):
        size = vector.shape[0]
        small = small + jnp.pad(vector.astype(F32), (i * 128, 1024 - i * 128 - size))
    (
        vectors,
        residual,
        d_hidden,
        ff_small,
        wqkv_g,
        wout_g,
        a1,
        query,
        kv,
        mixed,
        d_attn_g,
        out_part,
        up_a_own,
        up_b_own,
        down_a_own,
        down_b_own,
        up_a_got,
        up_b_got,
        down_a_got,
        down_b_got,
    ) = forward(0, lengths, tok, small.reshape(8, 128), w_up, dy, w_down, w_qkv, w_out)
    last = attention_backward(
        1,
        lengths,
        vectors,
        ff_small,
        d_attn_g,
        wout_g,
        query,
        kv,
        a1,
        mixed,
        wqkv_g,
        tok,
        d_hidden,
        residual,
        out_part,
        (up_a_own, up_b_own, down_a_own, down_b_own),
        (up_a_got, up_b_got, down_a_got, down_b_got),
    )

    final = list(results(*last))
    final[0] = final[0].reshape(1, blk, width)
    final[1] = final[1].reshape(1, blk, width)
    for i in (2, 3, 5, 7, 8, 9, 11, 13):
        final[i] = final[i].reshape(-1)
    return tuple(final)


def solution(mesh):
    fine = Mesh(mesh.devices.reshape(4, 2, 4, 4), AXES)
    rows, seq = ("y", "core"), ("z", "x")
    every = rows + seq
    token = P(rows, seq, None)
    vec, mat = P(every), P(every, None)
    in_specs = (token, token, P(rows, None), vec, vec, mat, vec, mat, vec, vec, vec, mat, vec, mat, vec)
    out_specs = (token, token, vec, vec, mat, vec, mat, vec, vec, vec, mat, vec, mat, vec)
    return jax.shard_map(local, mesh=fine, in_specs=in_specs, out_specs=out_specs, check_vma=False)
```

time: 342 us -> 288 us (0.84)
  Pallas kernels: 326 us -> 278 us
  other arithmetic: 5.46 us -> 1.38 us
    pallas_call x1, Pallas kernels: 107 us -> 1.8 us  [results(): pl.pallas_call(results_body, out_shape=tuple((jax.ShapeDtypeStruct(s, d)...]
    pallas_call x1, Pallas kernels: 127 us -> 186 us  [forward(): pl.pallas_call(forward_body, out_shape=tuple((jax.ShapeDtypeStruct(s, d)...]
    unnamed x13 -> x16, local copies, waits for them, and re-layouts: 2.88 us -> 7.8 us
where the time goes in v5:
time: 288 us
  Pallas kernels  278 us (97%)
  local copies, waits for them, and re-layouts  7.8 us (3%)
    pallas_call x1, Pallas kernels, forward(): pl.pallas_call(forward_body, out_shape=tuple((jax.ShapeDtypeStruct(s, d)...  186 us
    pallas_call x1, Pallas kernels, attention_backward(): pl.pallas_call(attention_backward_body, out_shape=tuple((jax.ShapeDtypeSt...  89.9 us
    unnamed x16, local copies, waits for them, and re-layouts  7.8 us

profile of v5, /device:TPU:1, one launch (start us, length us, event | category | flops | bytes accessed | tf_op | source)
XLA Modules:
  0.0 287.6 jit_solution(12674890376516563299)
XLA Ops:
  0.6 1.4 add_bitcast_fusion.small_in
  2.0 186.1 %forward.1 = (f32[8,2048]{1,0:T(8,128)}, f32[128,2048]{1,0:T(8,128)}, f32[128,2048]{1,0:T(8,128)}, f32[8,2048]{1,0:T(8,128)}, bf16[2,4,4,64,1536]{4,3,2,1,0:T(8,...) custom-call(s32[1,4]{1,0:T(1,128)} %lengths.3, ...), custom_call_target="tpu_custom_call" | custom-call | tf_op jit(solution)/shard_map/forward/pallas_call | solution.py:809
  188.1 89.9 %attention_backward.1 = (bf16[128,2048]{1,0:T(8,128)(2,1)}, f32[128,2048]{1,0:T(8,128)}, bf16[16,6144]{1,0:T(8,128)(2,1)}, bf16[16,2048]{1,0:T(8,128)(2,1)}, f32...) custom-call(s32[1,4]{1,0:T(1,128)} %lengths.3, ...), custom_call_target="tpu_custom_call" | custom-call | tf_op jit(solution)/shard_map/attention_backward/pallas_call | solution.py:1334
  278.0 0.0 copy-start
  278.0 1.2 copy-done
  279.2 0.0 copy-start.1
  279.2 1.0 copy-done.1
  280.3 0.0 copy-start.2
  280.3 1.0 copy-done.2
  281.3 0.0 copy-start.3
  281.3 0.9 copy-done.3
  282.2 0.0 copy-start.4
  282.3 0.9 copy-done.4
  283.2 0.0 copy-start.5
  283.2 0.9 copy-done.5
  284.1 0.0 copy-start.6
  284.1 0.8 copy-done.6
  285.0 0.0 copy-start.7
  285.0 0.8 copy-done.7
  285.8 1.8 results.1
Async XLA Ops:
  278.0 1.2 copy-start
  279.2 1.0 copy-start.1
  280.3 1.0 copy-start.2
  281.3 0.9 copy-start.3
  282.2 0.9 copy-start.4
  283.2 0.9 copy-start.5
  284.1 0.8 copy-start.6
  285.0 0.8 copy-start.7

commit v6 on v5

--- a/solution.py
+++ b/solution.py
@@ -18,7 +18,7 @@
 SIZE = {"y": 4, "core": 2, "z": 4, "x": 4}
 BF = jnp.bfloat16
 F32 = jnp.float32
-SEMS = 180
+SEMS = 212
 
 
 def coords():
@@ -128,6 +128,38 @@
 
     def far(self):
         self.comm.arrived(self.passed)
+
+
+class RingSum:
+    def __init__(self, comm, axis, ref, tmp, got):
+        self.comm, self.axis, self.ref, self.tmp, self.got = comm, axis, ref, tmp, got
+        self.me = lax.axis_index(axis)
+
+    def at(self, k):
+        return lax.rem(self.me + k, 4)
+
+    def push(self, src, dst, k):
+        return self.comm.push(src, dst, peer(**{self.axis: k}))
+
+    def start(self):
+        self.up = self.push(self.ref(self.at(2), 0), self.tmp.at[0], 1)
+        self.down = self.push(self.ref(self.at(2), 1), self.tmp.at[1], 3)
+        self.end = [
+            self.push(self.ref(self.at(1), 1), self.got.at[0, pl.ds(2, 2)], 1),
+            self.push(self.ref(self.at(3), 0), self.got.at[1, pl.ds(0, 2)], 3),
+        ]
+
+    def middle(self):
+        for arrived, k, h, back in ((self.up, 1, 0, 0), (self.down, 3, 1, 2)):
+            self.comm.arrived([arrived])
+            block = self.ref(self.at(k), h)
+            for c in range(2):
+                total = block[c].astype(F32) + self.tmp[h, c].astype(F32)
+                block[c] = total.astype(BF)
+            self.end.append(self.push(block, self.got.at[h, pl.ds(back, 2)], k))
+
+    def finish(self):
+        self.comm.arrived(self.end)
 
 
 class Gather:
@@ -331,6 +363,7 @@
     smalls,
     stack,
     uparts,
+    ring_tmp,
     local_sem,
     free_sem,
     rs_send,
@@ -427,6 +460,8 @@
         s_u.append(c_u.push(uparts.at[to], wup.at[y, core, z, mine16], peer(x=k)))
     s_d.append(c_d.local(wdn_in.at[mine16], wdn.at[y, core, z, mine16]))
     s_u.append(c_u.local(uparts.at[x], wup.at[y, core, z, mine16]))
+    s_dy = [comm.push(dy_in, dyg.at[p], peer(x=ORDER[p])) for p in (1, 2, 3)]
+    dyg[0] = dy_in[...]
 
     c_small.arrived(s_small)
     table = smalls[...].reshape(1024, 128).astype(BF)
@@ -451,15 +486,13 @@
     norm_block(lax.rem(x + 1, 4))
     norm_block(lax.rem(x + 3, 4))
     qkv_g.far()
+    tokens.far()
+    norm_block(lax.rem(x + 2, 4))
     out_g.near()
     c_d.arrived(s_d)
     down_g.first()
     c_u.arrived(s_u)
-    up_g.first()
-    tokens.far()
-    s_dy = [comm.push(dy_in, dyg.at[p], peer(x=ORDER[p])) for p in (1, 2, 3)]
-    dyg[0] = dy_in[...]
-    norm_block(lax.rem(x + 2, 4))
+    up_g.first_b()
     keep_a1 = [comm.local(a1, a1_h)]
     vec_o[2:3, :] = jnp.zeros((1, width), F32)
     vec_o[2:3, 0:partw] = whole_vector(table, 2, x * partw, partw, 32, 0)
@@ -493,25 +526,6 @@
             e = jnp.exp(s - jnp.max(s, axis=-1, keepdims=True))
             p = (e * (1.0 / jnp.sum(e, axis=-1, keepdims=True))).astype(BF)
             mixed[rows, cols] = dot(p, kv[window, vcols], NN).astype(BF)
-
-    pl.loop(2, 4)(attend)
-    out_g.far()
-    c_d.arrived(down_g.one)
-    down_g.second_a()
-    c_u.arrived(up_g.one)
-    up_g.second_a()
-    for i in (3, 4, 5, 7):
-        vec_o[i : i + 1, :] = whole_vector(table, i, 0, width, 16, 0)
-    vec_o[6:7, :] = whole_vector(table, 6, 0, hidden, 16, x * 16)
-    comm.arrived(s_edge)
-    down_g.second_b()
-    up_g.second_b()
-    pl.loop(0, 2)(attend)
-    comm.local(kv, kv_h)
-    comm.local(mixed, mixed_h)
-    out_g.done()
-    c_o.local(wo, wo_h)
-    c_tok.drain()
 
     def sends_attn(j):
         cols = pl.ds(pl.multiple_of(j * 512, 512), 512)
@@ -526,27 +540,56 @@
             for k in (2, 1, 3)
         ]
 
-    @pl.loop(0, 4)
-    def _(j):
-        cols = pl.ds(pl.multiple_of(j * 512, 512), 512)
-        d = dot(mixed[...], wo[:, :, :, :, cols].reshape(partw, 512), NN)
-        part[:, :, cols] = d.astype(BF).reshape(4, blk, 512)
-        dact[:, 0:512] = d
-        own[:, cols] = dact[pl.ds(pl.multiple_of(x * blk, blk), blk), 0:512]
-        for copy in sends_attn(j):
-            copy.start()
-
+    def project_out(o):
+        rows = slice(o * blk, (o + 2) * blk)
+
+        @pl.loop(0, 4)
+        def _(j):
+            cols = pl.ds(pl.multiple_of(j * 512, 512), 512)
+            d = dot(mixed[rows, :], wo[:, :, :, :, cols].reshape(partw, 512), NN)
+            part[o : o + 2, :, cols] = d.astype(BF).reshape(2, blk, 512)
+            dact[rows, cols] = d
+            for to in (o, o + 1):
+                k = lax.rem(to - x + 4, 4)
+
+                @pl.when(k != 0)
+                def _():
+                    remote(
+                        part.at[to, :, cols],
+                        got.at[k - 1, :, cols],
+                        (rs_send, rs_recv),
+                        3 * j + k - 1,
+                        (y, core, z, to),
+                    ).start()
+
+    pl.loop(2, 4)(attend)
+    out_g.far()
+    c_d.arrived(down_g.one)
+    down_g.second_a()
+    for i in (3, 4, 5, 7):
+        vec_o[i : i + 1, :] = whole_vector(table, i, 0, width, 16, 0)
+    vec_o[6:7, :] = whole_vector(table, 6, 0, hidden, 16, x * 16)
+    out_g.done()
+    c_tok.drain()
+    project_out(2)
+    comm.arrived(s_edge)
+    up_g.first_a()
+    down_g.second_b()
+    pl.loop(0, 2)(attend)
+    project_out(0)
+    down_g.near_a()
+    c_u.arrived(up_g.one_a + up_g.one_b)
+    up_g.second_a()
+    comm.local(kv, kv_h)
+    comm.local(mixed, mixed_h)
+    c_o.local(wo, wo_h)
     c_q.drain()
     pl.semaphore_signal(
         free_sem, inc=1, device_id=peer(core=1), device_id_type=pl.DeviceIdType.MESH
     )
-
-    down_g.near_a()
-    up_g.near_a()
     down_g.near_b()
+    up_g.second_b()
     down_g.far_a()
-    up_g.near_b()
-    up_g.far_a()
 
     @pl.loop(0, 4)
     def _(j):
@@ -558,7 +601,8 @@
     @pl.loop(0, blk // 16)
     def _(i):
         rows = pl.ds(pl.multiple_of(i * 16, 16), 16)
-        v = tok_in[rows, :].astype(F32) + own[rows, :] + b_out
+        own_rows = pl.ds(pl.multiple_of(x * blk + i * 16, 16), 16)
+        v = tok_in[rows, :].astype(F32) + dact[own_rows, :] + b_out
         for g in range(3):
             v = v + got[g, rows, :].astype(F32)
         res_o[rows, :] = v
@@ -568,7 +612,8 @@
 
     spread = [comm.push(a2g.at[0], a2g.at[p], peer(x=ORDER[p])) for p in (1, 2)]
     down_g.far_b()
-    up_g.far_b()
+    up_g.near_a()
+    up_g.near_b()
 
     @pl.loop(0, 4)
     def _(j):
@@ -590,6 +635,8 @@
         comm.push(a2g.at[1, top], a2g.at[3, top], peer(x=1)),
         comm.push(a2g.at[2, bottom], a2g.at[3, bottom], peer(x=3)),
     ]
+    up_g.far_a()
+    up_g.far_b()
     up_g.done()
     comm.arrived(passed)
 
@@ -650,11 +697,16 @@
         wup[t, other] = grad_up(t, other).astype(BF).reshape(4, 64, hidden)
         swap_up(t).start()
 
-    first = []
-
-    def stage(src, dst, index, to):
-        first.append(remote(src, dst, sems, index, to))
-        first[-1].start()
+    c_ring = group(32)
+
+    def ring_sums(w, tmp_a, tmp_b, got_a, got_b):
+        return (
+            RingSum(c_ring, "z", lambda o, h: w.at[pl.ds(2 * h, 2), core, o, low], tmp_a, got_a),
+            RingSum(c_ring, "y", lambda o, h: w.at[o, core, pl.ds(2 * h, 2), high], tmp_b, got_b),
+        )
+
+    up_sums = ring_sums(wup, ring_tmp.at[0], ring_tmp.at[1], up_a_got, up_b_got)
+    down_sums = ring_sums(wdn, ring_tmp.at[2], ring_tmp.at[3], dn_a_got, dn_b_got)
 
     @pl.loop(0, 4)
     def _(t):
@@ -662,10 +714,8 @@
         total = grad_up(t, core) + up_c[t].reshape(256, hidden).astype(F32)
         wup[t, core] = total.astype(BF).reshape(4, 64, hidden)
 
-    for k in (1, 3, 2):
-        zz, yy = lax.rem(z + k, 4), lax.rem(y + k, 4)
-        stage(wup.at[:, core, zz, low], up_a_got.at[k - 1], 32 + k, peer(z=k))
-        stage(wup.at[yy, core, :, high], up_b_got.at[k - 1], 36 + k, peer(y=k))
+    for total in up_sums:
+        total.start()
 
     @pl.loop(0, 4)
     def _(j):
@@ -683,16 +733,17 @@
         wdn[t, other] = grad_down(t, other).astype(BF).reshape(4, 64, width)
         swap_down(t).start()
 
+    for total in up_sums:
+        total.middle()
+
     @pl.loop(0, 4)
     def _(t):
         swap_down(t).wait_recv()
         total = grad_down(t, core) + dn_c[t].reshape(256, width).astype(F32)
         wdn[t, core] = total.astype(BF).reshape(4, 64, width)
 
-    for k in (1, 3, 2):
-        zz, yy = lax.rem(z + k, 4), lax.rem(y + k, 4)
-        stage(wdn.at[:, core, zz, low], dn_a_got.at[k - 1], 24 + k, peer(z=k))
-        stage(wdn.at[yy, core, :, high], dn_b_got.at[k - 1], 28 + k, peer(y=k))
+    for total in down_sums:
+        total.start()
 
     @pl.loop(0, 4)
     def _(j):
@@ -740,15 +791,15 @@
     kept.append(pltpu.make_async_copy(wup.at[y, core, :, high], up_b_own, local_sem.at[5]))
     for copy in kept[1:]:
         copy.start()
+    for total in down_sums:
+        total.middle()
     attn.near()
     attn.far()
     kept.append(pltpu.make_async_copy(dattn, dattn_hbm, local_sem.at[1]))
     kept[-1].start()
 
-    for copy in first:
-        copy.wait_recv()
-    for copy in first:
-        copy.wait_send()
+    for total in up_sums + down_sums:
+        total.finish()
 
     @pl.loop(0, 4)
     def _(j):
@@ -783,7 +834,7 @@
         ((4, blk, width), BF, hbm),
         ((4, blk, width), BF, hbm),
     ]
-    outs += [(quarter, BF, hbm)] * 4 + [((3,) + quarter, BF, hbm)] * 4
+    outs += [(quarter, BF, hbm)] * 4 + [((2,) + quarter, BF, hbm)] * 4
     scratch = [
         ((4, 2, 4, 64, hidden), BF),
         ((4, 2, 4, 64, width), BF),
@@ -805,6 +856,7 @@
         ((4, 2, 128, 128), F32),
         ((hidden // 8, 512), BF),
         ((4, 16, hidden), BF),
+        ((4, 2, 2, 32, width), BF),
     ]
     return pl.pallas_call(
         forward_body,
@@ -913,11 +965,17 @@
     gux,
     stack,
     gq,
+    part_tmp,
+    q_tmp,
+    o_tmp,
     local_sem,
     send_sem,
     recv_sem,
+    comm_send,
+    comm_recv,
 ):
     sems = (send_sem, recv_sem)
+    comm = Comm(comm_send, comm_recv, 0, 32)
     me = coords()
     x, y, z, core = me["x"], me["y"], me["z"], me["core"]
     other = 1 - core
@@ -958,6 +1016,25 @@
         push(outp_hbm.at[p], outgot.at[p - 1], p, peer(x=-ORDER[p])) for p in (1, 2, 3)
     ]
 
+    def ff_sum(i):
+        for c in range(4):
+            total = fo[i, c].astype(F32) + fg[i, 0, c].astype(F32) + fg[i, 1, c].astype(F32)
+            fs[i, c] = total.astype(BF)
+
+    p_ff = []
+
+    def ff_second(i):
+        axis, here = ("y", y) if i % 2 == 0 else ("z", z)
+        for k in (1, 3, 2):
+            src = fs.at[i, lax.rem(here + k, 4)]
+            p_ff.append(push(src, fg2.at[i, k - 1], 4 + 3 * i + k, peer(**{axis: k})))
+
+    for copy in l_ff:
+        copy.wait()
+    for i in range(4):
+        ff_sum(i)
+    ff_second(0)
+    ff_second(2)
     dkv[...] = jnp.zeros(dkv.shape, F32)
     l_dattn.wait()
     l_wout.wait()
@@ -989,27 +1066,6 @@
     dedge[...] = dkv[0:W, :].astype(BF)
     p_edge = push(dedge, dedge_got, 4, peer(z=3))
 
-    def ff_sum(i):
-        for c in range(4):
-            total = fo[i, c].astype(F32)
-            for g in range(3):
-                total = total + fg[i, g, c].astype(F32)
-            fs[i, c] = total.astype(BF)
-
-    p_ff = []
-
-    def ff_second(i):
-        axis, here = ("y", y) if i % 2 == 0 else ("z", z)
-        for k in (1, 3, 2):
-            src = fs.at[i, lax.rem(here + k, 4)]
-            p_ff.append(push(src, fg2.at[i, k - 1], 4 + 3 * i + k, peer(**{axis: k})))
-
-    for copy in l_ff:
-        copy.wait()
-    for i in range(4):
-        ff_sum(i)
-    ff_second(0)
-    ff_second(2)
     pl.loop(2, 4)(block)
 
     p_edge.wait_recv()
@@ -1022,18 +1078,24 @@
     sm[0, 7:8, 0 : 3 * partw] = jnp.sum(dqkv[...].astype(F32), axis=0, keepdims=True)
     p_sc = push(sm.at[0], smc, 53, peer(core=1))
 
-    def sends(j):
-        cols = pl.ds(pl.multiple_of(j * 512, 512), 512)
-        return [
-            remote(
-                part.at[lax.rem(x + k, 4), :, cols],
-                got.at[k - 1, :, cols],
-                sems,
-                20 + 3 * j + k - 1,
-                peer(x=k),
-            )
-            for k in (2, 1, 3)
-        ]
+    ring_d = RingSum(comm, "x", lambda o, h: part.at[o, pl.ds(2 * h, 2)], part_tmp, got)
+    qkv_sums = (
+        RingSum(comm, "z", lambda o, h: gq.at[pl.ds(2 * h, 2), 0, o, low], q_tmp.at[0], qa),
+        RingSum(comm, "y", lambda o, h: gq.at[o, 0, pl.ds(2 * h, 2), high], q_tmp.at[1], qb),
+    )
+    left, right = slice(0, width // 2), slice(width // 2, width)
+    out_sums = (
+        RingSum(
+            comm, "z", lambda o, h: wout.at[core, pl.ds(2 * h, 2), o, :, left], o_tmp.at[0], oa
+        ),
+        RingSum(
+            comm,
+            "y",
+            lambda o, h: wout.at[core, lax.rem(o + 3, 4), pl.ds(2 * h, 2), :, right],
+            o_tmp.at[1],
+            ob,
+        ),
+    )
 
     def grad_qkv(t, c):
         cols = pl.ds(pl.multiple_of(t * 512 + c * 256, 256), 256)
@@ -1063,12 +1125,8 @@
         total = grad_qkv(t, core) + qkv_c[t].reshape(256, 3 * partw).astype(F32)
         gq[t, 0] = total.astype(BF).reshape(4, 64, 3 * partw)
 
-    left, right = slice(0, width // 2), slice(width // 2, width)
-    p_q1, p_o1 = [], []
-    for k in (1, 3, 2):
-        tz, ty = lax.rem(z + k, 4), lax.rem(y + k, 4)
-        p_q1.append(push(gq.at[:, 0, tz, low], qa.at[k - 1], 36 + k, peer(z=k)))
-        p_q1.append(push(gq.at[ty, 0, :, high], qb.at[k - 1], 39 + k, peer(y=k)))
+    for total in qkv_sums:
+        total.start()
 
     l_wqkv.wait()
 
@@ -1076,10 +1134,9 @@
     def _(j):
         cols = pl.ds(pl.multiple_of(j * 512, 512), 512)
         d = dot(dqkv[...], wqkv[:, j].reshape(512, 3 * partw), NT)
-        part[:, :, cols] = d.astype(BF).reshape(4, blk, 512)
-        for copy in sends(j):
-            copy.start()
-
+        part[:, :, :, cols] = d.astype(BF).reshape(4, 4, blk // 4, 512)
+
+    ring_d.start()
     p_sc.wait_recv()
     sm[1] = sm[0] + smc[...]
     p_sz = [push(sm.at[1], smz.at[k - 1], 59 + k, peer(z=k)) for k in (1, 3, 2)]
@@ -1087,10 +1144,11 @@
     wout[core] = (
         grad_out(core) + out_c[...].reshape(256, width).astype(F32)
     ).astype(BF).reshape(4, 4, 16, width)
-    for k in (1, 3, 2):
-        tz, tyc = lax.rem(z + k, 4), lax.rem(y + k + 3, 4)
-        p_o1.append(push(wout.at[core, :, tz, :, left], oa.at[k - 1], 42 + k, peer(z=k)))
-        p_o1.append(push(wout.at[core, tyc, :, :, right], ob.at[k - 1], 45 + k, peer(y=k)))
+    for total in out_sums:
+        total.start()
+    for total in qkv_sums:
+        total.middle()
+    ring_d.middle()
 
     for copy in l_end:
         copy.wait()
@@ -1105,11 +1163,13 @@
             total = total + outgot[g, rows, :].astype(F32)
         out_o[rows, :] = total.astype(BF)
 
-    for copy in p_q1:
-        copy.wait_recv()
+    for total in out_sums:
+        total.middle()
+    for total in qkv_sums:
+        total.finish()
     for c in range(4):
         ta, tb = gq[c, 0, z, low].astype(F32), gq[y, 0, c, high].astype(F32)
-        for g in range(3):
+        for g in range(2):
             ta, tb = ta + qa[g, c].astype(F32), tb + qb[g, c].astype(F32)
         qs[0, c], qs[1, c] = ta.astype(BF), tb.astype(BF)
     p_q2 = []
@@ -1118,57 +1178,7 @@
         p_q2.append(push(qs.at[0, ty], qa2.at[k - 1], 53 + k, peer(y=k)))
         p_q2.append(push(qs.at[1, tz], qb2.at[k - 1], 56 + k, peer(z=k)))
 
-    for copy in p_sz:
-        copy.wait_recv()
-    sm[2] = sm[1] + smz[0] + smz[1] + smz[2]
-    p_sy = [push(sm.at[2], smy.at[k - 1], 68 + k, peer(y=k)) for k in (1, 3, 2)]
-    for copy in p_o1:
-        copy.wait_recv()
-    for c in range(4):
-        ta, tb = wout[core, c, z, :, left].astype(F32), wout[core, zy, c, :, right].astype(F32)
-        for g in range(3):
-            ta, tb = ta + oa[g, c].astype(F32), tb + ob[g, c].astype(F32)
-        os_[0, c], os_[1, c] = ta.astype(BF), tb.astype(BF)
-    p_o2 = []
-    for k in (1, 3, 2):
-        tz, tyc = lax.rem(z + k, 4), lax.rem(y + k + 3, 4)
-        p_o2.append(push(os_.at[0, tyc], oa2.at[k - 1], 62 + k, peer(y=k)))
-        p_o2.append(push(os_.at[1, tz], ob2.at[k - 1], 65 + k, peer(z=k)))
-
     late_sum[...] = jnp.zeros(late_sum.shape, F32)
-
-    @pl.loop(0, 4)
-    def _(j):
-        for copy in sends(j):
-            copy.wait_recv()
-
-    gain = vec_in[0:1, :]
-
-    @pl.loop(0, blk // 16)
-    def _(i):
-        rows = pl.ds(pl.multiple_of(i * 16, 16), 16)
-        d = part[x, rows, :].astype(F32)
-        for g in range(3):
-            d = d + got[g, rows, :].astype(F32)
-        d_in, n = norm_backward(d, tok[rows, :].astype(F32), gain)
-        gtok_o[rows, :] = dhid[rows, :] + d_in
-        late_sum[0:1, :] += jnp.sum(d * n, axis=0, keepdims=True)
-        late_sum[1:2, :] += jnp.sum(d, axis=0, keepdims=True)
-
-    for i in range(8):
-        at = (i % 4) * (width // 4)
-        late[0, i : i + 1, :] = late_sum[i // 4 : i // 4 + 1, at : at + width // 4]
-    p_lc = push(late.at[0], late_c, 52, peer(core=1))
-    p_lc.wait_recv()
-    late[1] = late[0] + late_c[...]
-    p_lz = [push(late.at[1], late_p.at[i], 98 + i, to) for i, to in enumerate(plane())]
-
-    for copy in p_sy:
-        copy.wait_recv()
-    sm[3] = sm[2] + smy[0] + smy[1] + smy[2]
-    p_x = [push(sm.at[3], small_o.at[x], 71 + k, peer(x=k)) for k in (1, 3, 2)]
-    kept = [load(sm.at[3], small_o.at[x])]
-
 
     for copy in p_ff:
         copy.wait_recv()
@@ -1179,12 +1189,51 @@
             total = total + fg2[i, g].astype(F32)
         into, half = (fup, fdn)[i // 2], i % 2
         into[2 * half : 2 * half + 2] = total.astype(BF).reshape(2, 16, width)
-    p_u = []
+    ring_d.finish()
+    p_u, p_x, kept = [], [], []
     for k in (1, 3, 2):
         p_u.append(push(fup.at[lax.rem(x + k, 4)], gux.at[x], 48 + k, peer(x=k)))
         p_x.append(push(fdn.at[lax.rem(x + k, 4)], gdn_o.at[x], 76 + k, peer(x=k)))
     gux[x] = fup[x]
     kept.append(load(fdn.at[x], gdn_o.at[x]))
+    gain = vec_in[0:1, :]
+
+    @pl.loop(0, blk // 16)
+    def _(i):
+        rows = pl.ds(pl.multiple_of(i * 16, 16), 16)
+        c, r = i // 2, pl.ds(pl.multiple_of(lax.rem(i, 2) * 16, 16), 16)
+        d = part[x, c, r, :].astype(F32)
+        for g in range(2):
+            d = d + got[g, c, r, :].astype(F32)
+        d_in, n = norm_backward(d, tok[rows, :].astype(F32), gain)
+        gtok_o[rows, :] = dhid[rows, :] + d_in
+        late_sum[0:1, :] += jnp.sum(d * n, axis=0, keepdims=True)
+        late_sum[1:2, :] += jnp.sum(d, axis=0, keepdims=True)
+
+    for i in range(8):
+        at = (i % 4) * (width // 4)
+        late[0, i : i + 1, :] = late_sum[i // 4 : i // 4 + 1, at : at + width // 4]
+    p_lc = push(late.at[0], late_c, 52, peer(core=1))
+    p_lc.wait_recv()
+    late[1] = late[0] + late_c[...]
+    p_lz = [push(late.at[1], late_p.at[i], 98 + i, to) for i, to in enumerate(plane())]
+
+    for copy in p_sz:
+        copy.wait_recv()
+    sm[2] = sm[1] + smz[0] + smz[1] + smz[2]
+    p_sy = [push(sm.at[2], smy.at[k - 1], 68 + k, peer(y=k)) for k in (1, 3, 2)]
+    for total in out_sums:
+        total.finish()
+    for c in range(4):
+        ta, tb = wout[core, c, z, :, left].astype(F32), wout[core, zy, c, :, right].astype(F32)
+        for g in range(2):
+            ta, tb = ta + oa[g, c].astype(F32), tb + ob[g, c].astype(F32)
+        os_[0, c], os_[1, c] = ta.astype(BF), tb.astype(BF)
+    p_o2 = []
+    for k in (1, 3, 2):
+        tz, tyc = lax.rem(z + k, 4), lax.rem(y + k + 3, 4)
+        p_o2.append(push(os_.at[0, tyc], oa2.at[k - 1], 62 + k, peer(y=k)))
+        p_o2.append(push(os_.at[1, tz], ob2.at[k - 1], 65 + k, peer(z=k)))
 
     for copy in p_q2:
         copy.wait_recv()
@@ -1200,6 +1249,13 @@
             p_x.append(push(src, gqkv_o.at[:, own_cols], 83 + 3 * g + k - 1, peer(x=k)))
         kept.append(load(fq.at[x, :, block_cols], gqkv_o.at[:, own_cols]))
 
+    for copy in p_sy:
+        copy.wait_recv()
+    sm[3] = sm[2] + smy[0] + smy[1] + smy[2]
+    p_x += [push(sm.at[3], small_o.at[x], 71 + k, peer(x=k)) for k in (1, 3, 2)]
+    kept.append(load(sm.at[3], small_o.at[x]))
+
+
     for copy in p_o2:
         copy.wait_recv()
     ta, tb = os_[0, zy].astype(F32), os_[1, z].astype(F32)
@@ -1236,9 +1292,9 @@
 
     @pl.loop(0, 4)
     def _(j):
-        for copy in sends(j):
-            copy.wait_send()
         swap(j).wait_send()
+
+    comm.drain()
 
     for copy in kept:
         copy.wait()
@@ -1293,7 +1349,7 @@
         ((blk, width), BF),
         ((3, blk, width), BF),
         ((4, 4, 32, width), BF),
-        ((4, 3, 4, 32, width), BF),
+        ((4, 2, 4, 32, width), BF),
         ((4, 4, 32, width), BF),
         ((4, 3, 32, width), BF),
         ((4, 16, hidden), BF),
@@ -1303,14 +1359,14 @@
         ((span, 3 * partw), BF),
         ((W, 2 * partw), BF),
         ((W, 2 * partw), BF),
-        ((4, blk, width), BF),
-        ((3, blk, width), BF),
+        ((4, 4, blk // 4, width), BF),
+        ((2, 4, blk // 4, width), BF),
         ((4, 4, 64, 3 * partw), BF),
         ((4, 4, 16, width), BF),
-        ((3, 4, 32, 3 * partw), BF),
-        ((3, 4, 32, 3 * partw), BF),
-        ((3, 4, 16, half), BF),
-        ((3, 4, 16, half), BF),
+        ((2, 4, 32, 3 * partw), BF),
+        ((2, 4, 32, 3 * partw), BF),
+        ((2, 4, 16, half), BF),
+        ((2, 4, 16, half), BF),
         ((2, 4, 32, 3 * partw), BF),
         ((2, 4, 16, half), BF),
         ((3, 32, 3 * partw), BF),
@@ -1330,6 +1386,9 @@
         ((4, 16, hidden), BF),
         ((hidden // 8, 512), BF),
         ((4, 2, 4, 64, 3 * partw), BF),
+        ((2, 2, blk // 4, width), BF),
+        ((2, 2, 2, 32, 3 * partw), BF),
+        ((2, 2, 2, 16, half), BF),
     ]
     return pl.pallas_call(
         attention_backward_body,
@@ -1341,6 +1400,8 @@
             pltpu.SemaphoreType.DMA((32,)),
             pltpu.SemaphoreType.DMA((114,)),
             pltpu.SemaphoreType.DMA((114,)),
+            pltpu.SemaphoreType.DMA((32,)),
+            pltpu.SemaphoreType.DMA((32,)),
         ],
         compiler_params=pltpu.CompilerParams(
             collective_id=collective_id, has_side_effects=True, vmem_limit_bytes=62 << 20

time: 288 us -> 270 us (0.938)
  Pallas kernels: 278 us -> 259 us
    pallas_call x1, Pallas kernels: 186 us -> 173 us  [forward(): pl.pallas_call(forward_body, out_shape=tuple((jax.ShapeDtypeStruct(s, d)...]
    pallas_call x1, Pallas kernels: 89.9 us -> 84.3 us  [attention_backward(): pl.pallas_call(attention_backward_body, out_shape=tuple((jax.ShapeDtypeSt...]
where the time goes in v6:
time: 270 us; the launch traced here: 269 us
  Pallas kernels  259 us (96%)
  local copies, waits for them, and re-layouts  7.8 us (3%)
    pallas_call x1, Pallas kernels, forward(): pl.pallas_call(forward_body, out_shape=tuple((jax.ShapeDtypeStruct(s, d)...  173 us
    pallas_call x1, Pallas kernels, attention_backward(): pl.pallas_call(attention_backward_body, out_shape=tuple((jax.ShapeDtypeSt...  84.3 us
    unnamed x16, local copies, waits for them, and re-layouts  7.8 us

profile of v6, /device:TPU:1, one launch (start us, length us, event | category | flops | bytes accessed | tf_op | source)
XLA Modules:
  0.0 268.5 jit_solution(3905550032718368361)
XLA Ops:
  0.6 1.4 add_bitcast_fusion.small_in
  2.0 172.6 %forward.1 = (f32[8,2048]{1,0:T(8,128)}, f32[128,2048]{1,0:T(8,128)}, f32[128,2048]{1,0:T(8,128)}, f32[8,2048]{1,0:T(8,128)}, bf16[2,4,4,64,1536]{4,3,2,1,0:T(8,...) custom-call(s32[1,4]{1,0:T(1,128)} %lengths.3, ...), custom_call_target="tpu_custom_call" | custom-call | tf_op jit(solution)/shard_map/forward/pallas_call | solution.py:861
  174.6 84.3 %attention_backward.1 = (bf16[128,2048]{1,0:T(8,128)(2,1)}, f32[128,2048]{1,0:T(8,128)}, bf16[16,6144]{1,0:T(8,128)(2,1)}, bf16[16,2048]{1,0:T(8,128)(2,1)}, f32...) custom-call(s32[1,4]{1,0:T(1,128)} %lengths.3, ...), custom_call_target="tpu_custom_call" | custom-call | tf_op jit(solution)/shard_map/attention_backward/pallas_call | solution.py:1393
  258.9 0.0 copy-start
  258.9 1.2 copy-done
  260.1 0.0 copy-start.1
  260.1 1.0 copy-done.1
  261.2 0.0 copy-start.2
  261.2 1.0 copy-done.2
  262.2 0.0 copy-start.3
  262.2 0.9 copy-done.3
  263.2 0.0 copy-start.4
  263.2 0.9 copy-done.4
  264.1 0.0 copy-start.5
  264.1 0.9 copy-done.5
  265.0 0.0 copy-start.6
  265.1 0.8 copy-done.6
  265.9 0.0 copy-start.7
  265.9 0.8 copy-done.7
  266.7 1.8 results.1
Async XLA Ops:
  258.9 1.2 copy-start
  260.1 1.0 copy-start.1
  261.2 1.0 copy-start.2
  262.2 0.9 copy-start.3
  263.2 0.9 copy-start.4
  264.1 0.9 copy-start.5
  265.0 0.8 copy-start.6
  265.9 0.8 copy-start.7

commit v7 on v6

--- a/solution.py
+++ b/solution.py
@@ -18,7 +18,7 @@
 SIZE = {"y": 4, "core": 2, "z": 4, "x": 4}
 BF = jnp.bfloat16
 F32 = jnp.float32
-SEMS = 212
+SEMS = 264
 
 
 def coords():
@@ -36,6 +36,11 @@
         self.count, self.last, self.open = base, base + room, []
 
     def push(self, src, dst, to):
+        entry = self.plan(src, dst, to)
+        entry[0].start()
+        return entry
+
+    def plan(self, src, dst, to):
         copy = pltpu.make_async_remote_copy(
             src_ref=src,
             dst_ref=dst,
@@ -46,7 +51,6 @@
         )
         assert self.count < self.last
         self.count += 1
-        copy.start()
         self.open.append([copy, True, True])
         return self.open[-1]
 
@@ -115,16 +119,17 @@
     def to(self, k):
         return peer(**{self.axis: k})
 
-    def start(self, src=None):
-        own = self.full(self.me)
-        src = own if src is None else src
-        self.sent = [self.comm.push(src, own, self.to(1)), self.comm.push(src, own, self.to(3))]
+    def start(self):
+        a, b = self.half(self.me, 0), self.half(self.me, 1)
+        self.sent = [self.comm.push(a, a, self.to(1)), self.comm.push(b, b, self.to(3))]
+        self.rest = [self.comm.push(b, b, self.to(1)), self.comm.push(a, a, self.to(3))]
 
     def near(self):
         self.comm.arrived(self.sent)
         before, after = lax.rem(self.me + 3, 4), lax.rem(self.me + 1, 4)
         up, down = self.half(before, 0), self.half(after, 1)
         self.passed = [self.comm.push(up, up, self.to(1)), self.comm.push(down, down, self.to(3))]
+        self.comm.arrived(self.rest)
 
     def far(self):
         self.comm.arrived(self.passed)
@@ -141,13 +146,31 @@
     def push(self, src, dst, k):
         return self.comm.push(src, dst, peer(**{self.axis: k}))
 
+    def plan(self, src, dst, k):
+        return self.comm.plan(src, dst, peer(**{self.axis: k}))
+
+    def prepare(self):
+        self.up = self.plan(self.ref(self.at(2), 0), self.tmp.at[0], 1)
+        self.down = self.plan(self.ref(self.at(2), 1), self.tmp.at[1], 3)
+        self.end = [
+            self.plan(self.ref(self.at(1), 1), self.got.at[0, pl.ds(2, 2)], 1),
+            self.plan(self.ref(self.at(3), 0), self.got.at[1, pl.ds(0, 2)], 3),
+        ]
+        self.first = {1: [self.end[0]], 2: [self.up, self.down], 3: [self.end[1]]}
+
     def start(self):
-        self.up = self.push(self.ref(self.at(2), 0), self.tmp.at[0], 1)
-        self.down = self.push(self.ref(self.at(2), 1), self.tmp.at[1], 3)
-        self.end = [
-            self.push(self.ref(self.at(1), 1), self.got.at[0, pl.ds(2, 2)], 1),
-            self.push(self.ref(self.at(3), 0), self.got.at[1, pl.ds(0, 2)], 3),
-        ]
+        self.prepare()
+        for k in (2, 1, 3):
+            for entry in self.first[k]:
+                entry[0].start()
+
+    def start_block(self, to):
+        for k in (2, 1, 3):
+
+            @pl.when(self.at(k) == to)
+            def _():
+                for entry in self.first[k]:
+                    entry[0].start()
 
     def middle(self):
         for arrived, k, h, back in ((self.up, 1, 0, 0), (self.down, 3, 1, 2)):
@@ -321,11 +344,11 @@
     wup_in,
     dy_in,
     wdn_in,
-    wqkv_hbm,
-    wout_hbm,
+    wqkv_in,
+    wout_in,
     vec_o,
-    res_o,
-    dhid_out,
+    res_h,
+    dhid_h,
     small_out,
     wq_h,
     wo_h,
@@ -335,12 +358,10 @@
     mixed_h,
     dattn_hbm,
     outp_hbm,
-    up_a_own,
-    up_b_own,
+    up_mine,
+    up_two,
     dn_a_own,
     dn_b_own,
-    up_a_got,
-    up_b_got,
     dn_a_got,
     dn_b_got,
     wup,
@@ -357,17 +378,16 @@
     dyg,
     part,
     got,
-    own,
-    outp,
     dattn,
     smalls,
     stack,
     uparts,
     ring_tmp,
+    up_got,
+    res_o,
+    dhid_out,
     local_sem,
     free_sem,
-    rs_send,
-    rs_recv,
     ff_send,
     ff_recv,
     send_sem,
@@ -381,8 +401,8 @@
         groups.append(comm)
         return comm
 
-    c_q, c_o, c_u, c_d = group(36), group(26), group(26), group(26)
-    c_small, c_tok, comm = group(28), group(4), group(32)
+    c_q, c_o, c_u, c_d = group(40), group(30), group(30), group(30)
+    c_small, c_tok, comm = group(28), group(6), group(40)
     sems = (ff_send, ff_recv)
     me = coords()
     x, y, z, core = me["x"], me["y"], me["z"], me["core"]
@@ -404,21 +424,21 @@
     s_q = []
     for k in (1, 3, 2):
         for g in range(3):
-            src = wqkv_hbm.at[:, pl.ds(g * width + lax.rem(x + k, 4) * partw, partw)]
+            src = wqkv_in.at[:, pl.ds(g * width + lax.rem(x + k, 4) * partw, partw)]
             dst = cc.at[core, y, z, mine16, pl.ds(g * partw, partw)]
             s_q.append(c_q.push(src, dst, peer(x=k)))
     for g in range(3):
-        src = wqkv_hbm.at[:, pl.ds(g * width + x * partw, partw)]
+        src = wqkv_in.at[:, pl.ds(g * width + x * partw, partw)]
         s_q.append(c_q.local(src, cc.at[core, y, z, mine16, pl.ds(g * partw, partw)]))
     spot = smalls.at[y, core, pl.ds((z * 4 + x) * 8, 8)]
     s_small = [c_small.push(small_in, spot, to) for to in ring("x")]
     s_small.append(c_small.local(small_in, spot))
-    s_o = [c_o.push(wout_hbm, wo.at[core, z, x], scattered())]
+    s_o = [c_o.push(wout_in, wo.at[core, z, x], scattered())]
     tokens = Relay(
         c_tok, "x", lambda o: tokg.at[o], lambda o, h: tokg.at[o, pl.ds(h * blk // 2, blk // 2)]
     )
-    tokens.start(tok_in)
     tokg[x] = tok_in[...]
+    tokens.start()
 
     qkv_g = Gather(c_q, cc, True, [cut + (wide,) for cut in by_rows(64)])
     out_g = Gather(c_o, wo, True, by_columns(width), 3)
@@ -527,18 +547,9 @@
             p = (e * (1.0 / jnp.sum(e, axis=-1, keepdims=True))).astype(BF)
             mixed[rows, cols] = dot(p, kv[window, vcols], NN).astype(BF)
 
-    def sends_attn(j):
-        cols = pl.ds(pl.multiple_of(j * 512, 512), 512)
-        return [
-            remote(
-                part.at[lax.rem(x + k, 4), :, cols],
-                got.at[k - 1, :, cols],
-                (rs_send, rs_recv),
-                3 * j + k - 1,
-                peer(x=k),
-            )
-            for k in (2, 1, 3)
-        ]
+    c_sum = group(8)
+    ring_a = RingSum(c_sum, "x", lambda o, h: part.at[o, pl.ds(2 * h, 2)], ring_tmp.at[0], got)
+    ring_a.prepare()
 
     def project_out(o):
         rows = slice(o * blk, (o + 2) * blk)
@@ -547,31 +558,22 @@
         def _(j):
             cols = pl.ds(pl.multiple_of(j * 512, 512), 512)
             d = dot(mixed[rows, :], wo[:, :, :, :, cols].reshape(partw, 512), NN)
-            part[o : o + 2, :, cols] = d.astype(BF).reshape(2, blk, 512)
+            part[o : o + 2, :, :, cols] = d.astype(BF).reshape(2, 4, blk // 4, 512)
             dact[rows, cols] = d
-            for to in (o, o + 1):
-                k = lax.rem(to - x + 4, 4)
-
-                @pl.when(k != 0)
-                def _():
-                    remote(
-                        part.at[to, :, cols],
-                        got.at[k - 1, :, cols],
-                        (rs_send, rs_recv),
-                        3 * j + k - 1,
-                        (y, core, z, to),
-                    ).start()
+
+        for to in (o, o + 1):
+            ring_a.start_block(to)
 
     pl.loop(2, 4)(attend)
     out_g.far()
+    out_g.done()
+    c_tok.drain()
+    project_out(2)
     c_d.arrived(down_g.one)
     down_g.second_a()
     for i in (3, 4, 5, 7):
         vec_o[i : i + 1, :] = whole_vector(table, i, 0, width, 16, 0)
     vec_o[6:7, :] = whole_vector(table, 6, 0, hidden, 16, x * 16)
-    out_g.done()
-    c_tok.drain()
-    project_out(2)
     comm.arrived(s_edge)
     up_g.first_a()
     down_g.second_b()
@@ -589,13 +591,10 @@
     )
     down_g.near_b()
     up_g.second_b()
+    ring_a.middle()
     down_g.far_a()
 
-    @pl.loop(0, 4)
-    def _(j):
-        for copy in sends_attn(j):
-            copy.wait_recv()
-
+    ring_a.finish()
     b_out, gain2, shift2 = vec_o[3:4, :], vec_o[4:5, :], vec_o[5:6, :]
 
     @pl.loop(0, blk // 16)
@@ -603,23 +602,22 @@
         rows = pl.ds(pl.multiple_of(i * 16, 16), 16)
         own_rows = pl.ds(pl.multiple_of(x * blk + i * 16, 16), 16)
         v = tok_in[rows, :].astype(F32) + dact[own_rows, :] + b_out
-        for g in range(3):
-            v = v + got[g, rows, :].astype(F32)
+        c, r = i // 2, pl.ds(pl.multiple_of(lax.rem(i, 2) * 16, 16), 16)
+        for g in range(2):
+            v = v + got[g, c, r, :].astype(F32)
         res_o[rows, :] = v
         centred = v - jnp.mean(v, axis=-1, keepdims=True)
         s = lax.rsqrt(jnp.mean(centred * centred, axis=-1, keepdims=True) + EPSILON)
         a2g[0, rows, :] = (centred * s * gain2 + shift2).astype(BF)
 
-    spread = [comm.push(a2g.at[0], a2g.at[p], peer(x=ORDER[p])) for p in (1, 2)]
+    top, bottom = pl.ds(0, blk // 2), pl.ds(blk // 2, blk // 2)
+    spread = []
+    for p, rows in ((1, top), (2, bottom), (1, bottom), (2, top)):
+        spread.append(comm.push(a2g.at[0, rows], a2g.at[p, rows], peer(x=ORDER[p])))
+    comm.local(res_o, res_h)
     down_g.far_b()
     up_g.near_a()
-    up_g.near_b()
-
-    @pl.loop(0, 4)
-    def _(j):
-        for copy in sends_attn(j):
-            copy.wait_send()
-
+    c_sum.drain()
     comm.arrived(keep_a1 + s_dy)
     down_g.done()
 
@@ -629,16 +627,16 @@
         cols = pl.ds(pl.multiple_of(j * 512, 512), 512)
         dact[:, cols] = dot(dyg[...].reshape(span, width), tile, NT)
 
-    comm.arrived(spread)
-    top, bottom = pl.ds(0, blk // 2), pl.ds(blk // 2, blk // 2)
+    comm.arrived(spread[:2])
     passed = [
         comm.push(a2g.at[1, top], a2g.at[3, top], peer(x=1)),
         comm.push(a2g.at[2, bottom], a2g.at[3, bottom], peer(x=3)),
     ]
+    up_g.near_b()
     up_g.far_a()
     up_g.far_b()
     up_g.done()
-    comm.arrived(passed)
+    comm.arrived(passed + spread)
 
     @pl.loop(0, hidden // 256)
     def _(j):
@@ -652,28 +650,20 @@
         dup[:, cols] = d_up
         small_out[3:4, cols] = jnp.sum(d_up.astype(F32), axis=0, keepdims=True)
 
-    def sends(j):
-        cols = pl.ds(pl.multiple_of(j * 512, 512), 512)
-        return [
-            remote(
-                part.at[p - 1, :, cols],
-                got.at[p - 1, :, cols],
-                sems,
-                4 + 3 * j + p - 1,
-                peer(x=-ORDER[p]),
-            )
-            for p in (3, 1, 2)
-        ]
+    c_ff = group(12)
+    places = [lax.rem(x + 4 - k, 4) for k in ORDER]
+    ring_f = RingSum(c_ff, "x", lambda o, h: part.at[o, pl.ds(2 * h, 2)], ring_tmp.at[1], got)
 
     @pl.loop(0, 4)
     def _(j):
         cols = pl.ds(pl.multiple_of(j * 512, 512), 512)
         d = dot(dup[...], wup[j].reshape(512, hidden), NT)
-        own[:, cols] = d[:blk]
+        dact[0:blk, cols] = d[:blk]
         for p in (1, 2, 3):
-            part[p - 1, :, cols] = d[p * blk : (p + 1) * blk].astype(BF)
-        for copy in sends(j):
-            copy.start()
+            block = d[p * blk : (p + 1) * blk].astype(BF)
+            part[places[p], :, :, cols] = block.reshape(4, blk // 4, 512)
+
+    ring_f.start()
 
     def grad_down(t, c):
         cols = pl.ds(pl.multiple_of(t * 512 + c * 256, 256), 256)
@@ -697,7 +687,7 @@
         wup[t, other] = grad_up(t, other).astype(BF).reshape(4, 64, hidden)
         swap_up(t).start()
 
-    c_ring = group(32)
+    c_ring = group(34)
 
     def ring_sums(w, tmp_a, tmp_b, got_a, got_b):
         return (
@@ -705,8 +695,8 @@
             RingSum(c_ring, "y", lambda o, h: w.at[o, core, pl.ds(2 * h, 2), high], tmp_b, got_b),
         )
 
-    up_sums = ring_sums(wup, ring_tmp.at[0], ring_tmp.at[1], up_a_got, up_b_got)
-    down_sums = ring_sums(wdn, ring_tmp.at[2], ring_tmp.at[3], dn_a_got, dn_b_got)
+    up_sums = ring_sums(wup, ring_tmp.at[2], ring_tmp.at[3], up_got.at[0], up_got.at[1])
+    down_sums = ring_sums(wdn, ring_tmp.at[4], ring_tmp.at[5], dn_a_got, dn_b_got)
 
     @pl.loop(0, 4)
     def _(t):
@@ -721,10 +711,11 @@
     def _(j):
         cols = pl.ds(pl.multiple_of(j * 512, 512), 512)
         o = dot(act[...], wdn[:, :, :, :, cols].reshape(hidden, 512), NN)
-        outp[:, :, cols] = o.astype(BF).reshape(4, blk, 512)
-
-    keep_out = pltpu.make_async_copy(outp, outp_hbm, local_sem.at[0])
+        dup[:, cols] = o.astype(BF)
+
+    keep_out = pltpu.make_async_copy(dup, outp_hbm, local_sem.at[0])
     keep_out.start()
+    ring_f.middle()
 
     c_d.drain()
 
@@ -745,11 +736,7 @@
     for total in down_sums:
         total.start()
 
-    @pl.loop(0, 4)
-    def _(j):
-        for copy in sends(j):
-            copy.wait_recv()
-
+    ring_f.finish()
     small_out[0:3, :] = jnp.zeros((3, width), F32)
     small_out[4:8, :] = jnp.zeros((4, width), F32)
     gain = vec_o[4:5, :]
@@ -757,9 +744,10 @@
     @pl.loop(0, blk // 16)
     def _(i):
         rows = pl.ds(pl.multiple_of(i * 16, 16), 16)
-        d = own[rows, :]
-        for p in range(3):
-            d = d + got[p, rows, :].astype(F32)
+        d = dact[rows, :]
+        c, r = i // 2, pl.ds(pl.multiple_of(lax.rem(i, 2) * 16, 16), 16)
+        for g in range(2):
+            d = d + got[g, c, r, :].astype(F32)
         v = res_o[rows, :]
         centred = v - jnp.mean(v, axis=-1, keepdims=True)
         s = lax.rsqrt(jnp.mean(centred * centred, axis=-1, keepdims=True) + EPSILON)
@@ -784,27 +772,41 @@
         comm, "x", lambda o: dattn.at[o], lambda o, h: dattn.at[o, pl.ds(h * blk // 2, blk // 2)]
     )
     attn.start()
+    comm.local(dattn.at[x], dattn_hbm.at[x])
+    for total in up_sums:
+        total.finish()
+    for c in range(4):
+        a, b = wup[c, core, z, low].astype(F32), wup[y, core, c, high].astype(F32)
+        for g in range(2):
+            a, b = a + up_got[0, g, c].astype(F32), b + up_got[1, g, c].astype(F32)
+        wup[c, core, z, low], wup[y, core, c, high] = a.astype(BF), b.astype(BF)
+    for k in (1, 3, 2):
+        ty, tz = lax.rem(y + k, 4), lax.rem(z + k, 4)
+        c_ring.push(wup.at[ty, core, z, low], up_two.at[0, k - 1], peer(y=k))
+        c_ring.push(wup.at[y, core, tz, high], up_two.at[1, k - 1], peer(z=k))
+    c_ring.local(wup.at[y, core, z, low], up_mine.at[0])
+    c_ring.local(wup.at[y, core, z, high], up_mine.at[1])
+    comm.local(dhid_out, dhid_h)
     kept = [keep_out]
     kept.append(pltpu.make_async_copy(wdn.at[:, core, z, low], dn_a_own, local_sem.at[2]))
     kept.append(pltpu.make_async_copy(wdn.at[y, core, :, high], dn_b_own, local_sem.at[3]))
-    kept.append(pltpu.make_async_copy(wup.at[:, core, z, low], up_a_own, local_sem.at[4]))
-    kept.append(pltpu.make_async_copy(wup.at[y, core, :, high], up_b_own, local_sem.at[5]))
     for copy in kept[1:]:
         copy.start()
     for total in down_sums:
         total.middle()
     attn.near()
+    for k in (1, 3):
+        o = lax.rem(x + k, 4)
+        comm.local(dattn.at[o], dattn_hbm.at[o])
     attn.far()
-    kept.append(pltpu.make_async_copy(dattn, dattn_hbm, local_sem.at[1]))
-    kept[-1].start()
+    o = lax.rem(x + 2, 4)
+    comm.local(dattn.at[o], dattn_hbm.at[o])
 
     for total in up_sums + down_sums:
         total.finish()
 
     @pl.loop(0, 4)
     def _(j):
-        for copy in sends(j):
-            copy.wait_send()
         swap_down(j).wait_send()
         swap_up(j).wait_send()
 
@@ -822,8 +824,8 @@
     quarter = (4, 32, width)
     outs = [
         ((8, width), F32, vmem),
-        ((blk, width), F32, vmem),
-        ((blk, width), F32, vmem),
+        ((blk, width), F32, hbm),
+        ((blk, width), F32, hbm),
         ((8, width), F32, vmem),
         ((2, 4, 4, 64, 3 * partw), BF, hbm),
         ((2, 4, 4, 16, width), BF, hbm),
@@ -832,9 +834,10 @@
         ((span + W, 2 * partw), BF, hbm),
         ((span, partw), BF, hbm),
         ((4, blk, width), BF, hbm),
-        ((4, blk, width), BF, hbm),
+        ((span, width), BF, hbm),
     ]
-    outs += [(quarter, BF, hbm)] * 4 + [((2,) + quarter, BF, hbm)] * 4
+    outs += [((2, 32, width), BF, hbm), ((2, 3, 32, width), BF, hbm)]
+    outs += [(quarter, BF, hbm)] * 2 + [((2,) + quarter, BF, hbm)] * 2
     scratch = [
         ((4, 2, 4, 64, hidden), BF),
         ((4, 2, 4, 64, width), BF),
@@ -848,24 +851,25 @@
         ((span + W, 2 * partw), BF),
         ((span, partw), BF),
         ((4, blk, width), BF),
-        ((4, blk, width), BF),
-        ((3, blk, width), BF),
-        ((blk, width), F32),
-        ((4, blk, width), BF),
+        ((4, 4, blk // 4, width), BF),
+        ((2, 4, blk // 4, width), BF),
         ((4, blk, width), BF),
         ((4, 2, 128, 128), F32),
         ((hidden // 8, 512), BF),
         ((4, 16, hidden), BF),
-        ((4, 2, 2, 32, width), BF),
+        ((6, 2, 2, 32, width), BF),
+        ((2, 2) + quarter, BF),
+        ((blk, width), F32),
+        ((blk, width), F32),
     ]
     return pl.pallas_call(
         forward_body,
         out_shape=tuple(jax.ShapeDtypeStruct(s, d) for s, d, _ in outs),
-        in_specs=[pl.BlockSpec(memory_space=pltpu.SMEM)] + [vmem] * 5 + [hbm] * 2,
+        in_specs=[pl.BlockSpec(memory_space=pltpu.SMEM)] + [vmem] * 7,
         out_specs=tuple(o[2] for o in outs),
         scratch_shapes=[pltpu.VMEM(s, d) for s, d in scratch]
         + [pltpu.SemaphoreType.DMA((8,)), pltpu.SemaphoreType.REGULAR]
-        + [pltpu.SemaphoreType.DMA((n,)) for n in (12, 12, 40, 40, SEMS, SEMS)],
+        + [pltpu.SemaphoreType.DMA((n,)) for n in (40, 40, SEMS, SEMS)],
         compiler_params=pltpu.CompilerParams(
             collective_id=collective_id, has_side_effects=True, vmem_limit_bytes=63 << 20
         ),
@@ -899,16 +903,14 @@
     dhid_hbm,
     res_hbm,
     outp_hbm,
-    ffo0,
-    ffo1,
+    up_mine,
+    up_two,
     ffo2,
     ffo3,
-    ffg0,
-    ffg1,
     ffg2,
     ffg3,
-    out_o,
-    gtok_o,
+    out_h,
+    gtok_h,
     gqkv_o,
     gout_o,
     gup_o,
@@ -931,6 +933,7 @@
     fg,
     fs,
     fg2,
+    fmine,
     fup,
     fdn,
     dmix,
@@ -968,6 +971,8 @@
     part_tmp,
     q_tmp,
     o_tmp,
+    out_o,
+    gtok_o,
     local_sem,
     send_sem,
     recv_sem,
@@ -1004,16 +1009,17 @@
     l_dattn, l_wout = load(dattn_hbm, dattn), load(wout_hbm, wout)
     l_attn = [load(q_hbm, q_all), load(kv_hbm, kv)]
     low, high = slice(0, 32), slice(32, 64)
-    l_ff = [load(s, fo.at[i]) for i, s in enumerate((ffo0, ffo1, ffo2, ffo3))]
-    l_ff += [load(s, fg.at[i]) for i, s in enumerate((ffg0, ffg1, ffg2, ffg3))]
+    l_ff = [load(s, fo.at[i]) for i, s in enumerate((ffo2, ffo3))]
+    l_ff += [load(s, fg.at[i]) for i, s in enumerate((ffg2, ffg3))]
+    l_up = [load(up_two, fg2.at[pl.ds(0, 2)]), load(up_mine, fmine)]
     l_wqkv, l_a1, l_mixed = load(wqkv_hbm, wqkv), load(a1_hbm, a1), load(mixed_hbm, mixed)
-    l_end = [load(outp_hbm.at[0], outown), load(res_hbm, res)]
+    l_end = [load(outp_hbm.at[pl.ds(0, blk)], outown), load(res_hbm, res)]
     l_end += [load(tok_hbm, tok), load(dhid_hbm, dhid)]
 
     greet(ring("x") + plane() + near() + [scattered(), collected()])
 
     p_out = [
-        push(outp_hbm.at[p], outgot.at[p - 1], p, peer(x=-ORDER[p])) for p in (1, 2, 3)
+        push(outp_hbm.at[pl.ds(p * blk, blk)], outgot.at[p - 1], p, peer(x=-ORDER[p])) for p in (1, 2, 3)
     ]
 
     def ff_sum(i):
@@ -1024,17 +1030,17 @@
     p_ff = []
 
     def ff_second(i):
-        axis, here = ("y", y) if i % 2 == 0 else ("z", z)
+        axis, here = ("y", y) if i == 0 else ("z", z)
         for k in (1, 3, 2):
             src = fs.at[i, lax.rem(here + k, 4)]
-            p_ff.append(push(src, fg2.at[i, k - 1], 4 + 3 * i + k, peer(**{axis: k})))
+            p_ff.append(push(src, fg2.at[2 + i, k - 1], 4 + 3 * i + k, peer(**{axis: k})))
 
     for copy in l_ff:
         copy.wait()
-    for i in range(4):
-        ff_sum(i)
+    ff_sum(0)
+    ff_sum(1)
     ff_second(0)
-    ff_second(2)
+
     dkv[...] = jnp.zeros(dkv.shape, F32)
     l_dattn.wait()
     l_wout.wait()
@@ -1065,18 +1071,6 @@
     pl.loop(0, 2)(block)
     dedge[...] = dkv[0:W, :].astype(BF)
     p_edge = push(dedge, dedge_got, 4, peer(z=3))
-
-    pl.loop(2, 4)(block)
-
-    p_edge.wait_recv()
-    ff_second(1)
-    ff_second(3)
-    dqkv[0 : span - W, partw:] = dkv[W:span, :].astype(BF)
-    dqkv[span - W :, partw:] = (dkv[span:, :] + dedge_got[...].astype(F32)).astype(BF)
-    sm[0, 0:5, :] = ffsmall_in[0:5, :]
-    sm[0, 5:8, :] = jnp.zeros((3, width), F32)
-    sm[0, 7:8, 0 : 3 * partw] = jnp.sum(dqkv[...].astype(F32), axis=0, keepdims=True)
-    p_sc = push(sm.at[0], smc, 53, peer(core=1))
 
     ring_d = RingSum(comm, "x", lambda o, h: part.at[o, pl.ds(2 * h, 2)], part_tmp, got)
     qkv_sums = (
@@ -1097,13 +1091,33 @@
         ),
     )
 
+    def grad_out(c):
+        cols = pl.ds(pl.multiple_of(c * 256, 256), 256)
+        return dot(mixed[:, cols], dattn[...].reshape(span, width), TN)
+
+    l_mixed.wait()
+    wout[other] = grad_out(other).astype(BF).reshape(4, 4, 16, width)
+    p_oc = push(wout.at[other], out_c, 36, peer(core=1))
+
+    pl.loop(2, 4)(block)
+    p_oc.wait_recv()
+
+    wout[core] = (
+        grad_out(core) + out_c[...].reshape(256, width).astype(F32)
+    ).astype(BF).reshape(4, 4, 16, width)
+    for total in out_sums:
+        total.start()
+    p_edge.wait_recv()
+    dqkv[0 : span - W, partw:] = dkv[W:span, :].astype(BF)
+    dqkv[span - W :, partw:] = (dkv[span:, :] + dedge_got[...].astype(F32)).astype(BF)
+    sm[0, 0:5, :] = ffsmall_in[0:5, :]
+    sm[0, 5:8, :] = jnp.zeros((3, width), F32)
+    sm[0, 7:8, 0 : 3 * partw] = jnp.sum(dqkv[...].astype(F32), axis=0, keepdims=True)
+    p_sc = push(sm.at[0], smc, 53, peer(core=1))
+
     def grad_qkv(t, c):
         cols = pl.ds(pl.multiple_of(t * 512 + c * 256, 256), 256)
         return dot(a1[:, cols], dqkv[...], TN)
-
-    def grad_out(c):
-        cols = pl.ds(pl.multiple_of(c * 256, 256), 256)
-        return dot(mixed[:, cols], dattn[...].reshape(span, width), TN)
 
     def swap(t):
         return remote(gq.at[t, 1], qkv_c.at[t], sems, 32 + t, peer(core=1))
@@ -1114,10 +1128,6 @@
     def _(t):
         gq[t, 1] = grad_qkv(t, other).astype(BF).reshape(4, 64, 3 * partw)
         swap(t).start()
-
-    l_mixed.wait()
-    wout[other] = grad_out(other).astype(BF).reshape(4, 4, 16, width)
-    p_oc = push(wout.at[other], out_c, 36, peer(core=1))
 
     @pl.loop(0, 4)
     def _(t):
@@ -1127,6 +1137,8 @@
 
     for total in qkv_sums:
         total.start()
+    for total in out_sums:
+        total.middle()
 
     l_wqkv.wait()
 
@@ -1140,15 +1152,14 @@
     p_sc.wait_recv()
     sm[1] = sm[0] + smc[...]
     p_sz = [push(sm.at[1], smz.at[k - 1], 59 + k, peer(z=k)) for k in (1, 3, 2)]
-    p_oc.wait_recv()
-    wout[core] = (
-        grad_out(core) + out_c[...].reshape(256, width).astype(F32)
-    ).astype(BF).reshape(4, 4, 16, width)
-    for total in out_sums:
-        total.start()
     for total in qkv_sums:
         total.middle()
+    ff_second(1)
     ring_d.middle()
+    for copy in p_sz:
+        copy.wait_recv()
+    sm[2] = sm[1] + smz[0] + smz[1] + smz[2]
+    p_sy = [push(sm.at[2], smy.at[k - 1], 68 + k, peer(y=k)) for k in (1, 3, 2)]
 
     for copy in l_end:
         copy.wait()
@@ -1163,8 +1174,21 @@
             total = total + outgot[g, rows, :].astype(F32)
         out_o[rows, :] = total.astype(BF)
 
+    kept = [load(out_o, out_h)]
+
     for total in out_sums:
-        total.middle()
+        total.finish()
+    for c in range(4):
+        ta, tb = wout[core, c, z, :, left].astype(F32), wout[core, zy, c, :, right].astype(F32)
+        for g in range(2):
+            ta, tb = ta + oa[g, c].astype(F32), tb + ob[g, c].astype(F32)
+        os_[0, c], os_[1, c] = ta.astype(BF), tb.astype(BF)
+    p_o2 = []
+    for k in (1, 3, 2):
+        tz, tyc = lax.rem(z + k, 4), lax.rem(y + k + 3, 4)
+        p_o2.append(push(os_.at[0, tyc], oa2.at[k - 1], 62 + k, peer(y=k)))
+        p_o2.append(push(os_.at[1, tz], ob2.at[k - 1], 65 + k, peer(z=k)))
+
     for total in qkv_sums:
         total.finish()
     for c in range(4):
@@ -1180,22 +1204,13 @@
 
     late_sum[...] = jnp.zeros(late_sum.shape, F32)
 
-    for copy in p_ff:
+    p_u, p_x = [], []
+    for copy in p_sy:
         copy.wait_recv()
-    at = (y, z, y, z)
-    for i in range(4):
-        total = fs[i, at[i]].astype(F32)
-        for g in range(3):
-            total = total + fg2[i, g].astype(F32)
-        into, half = (fup, fdn)[i // 2], i % 2
-        into[2 * half : 2 * half + 2] = total.astype(BF).reshape(2, 16, width)
+    sm[3] = sm[2] + smy[0] + smy[1] + smy[2]
+    p_x += [push(sm.at[3], small_o.at[x], 71 + k, peer(x=k)) for k in (1, 3, 2)]
+    kept.append(load(sm.at[3], small_o.at[x]))
     ring_d.finish()
-    p_u, p_x, kept = [], [], []
-    for k in (1, 3, 2):
-        p_u.append(push(fup.at[lax.rem(x + k, 4)], gux.at[x], 48 + k, peer(x=k)))
-        p_x.append(push(fdn.at[lax.rem(x + k, 4)], gdn_o.at[x], 76 + k, peer(x=k)))
-    gux[x] = fup[x]
-    kept.append(load(fdn.at[x], gdn_o.at[x]))
     gain = vec_in[0:1, :]
 
     @pl.loop(0, blk // 16)
@@ -1210,6 +1225,7 @@
         late_sum[0:1, :] += jnp.sum(d * n, axis=0, keepdims=True)
         late_sum[1:2, :] += jnp.sum(d, axis=0, keepdims=True)
 
+    kept.append(load(gtok_o, gtok_h))
     for i in range(8):
         at = (i % 4) * (width // 4)
         late[0, i : i + 1, :] = late_sum[i // 4 : i // 4 + 1, at : at + width // 4]
@@ -1218,22 +1234,28 @@
     late[1] = late[0] + late_c[...]
     p_lz = [push(late.at[1], late_p.at[i], 98 + i, to) for i, to in enumerate(plane())]
 
-    for copy in p_sz:
+    for copy in p_ff:
         copy.wait_recv()
-    sm[2] = sm[1] + smz[0] + smz[1] + smz[2]
-    p_sy = [push(sm.at[2], smy.at[k - 1], 68 + k, peer(y=k)) for k in (1, 3, 2)]
-    for total in out_sums:
-        total.finish()
-    for c in range(4):
-        ta, tb = wout[core, c, z, :, left].astype(F32), wout[core, zy, c, :, right].astype(F32)
-        for g in range(2):
-            ta, tb = ta + oa[g, c].astype(F32), tb + ob[g, c].astype(F32)
-        os_[0, c], os_[1, c] = ta.astype(BF), tb.astype(BF)
-    p_o2 = []
+    for copy in l_up:
+        copy.wait()
+    for i in range(4):
+        total = (fmine[i] if i < 2 else fs[i - 2, (y, z)[i - 2]]).astype(F32)
+        for g in range(3):
+            total = total + fg2[i, g].astype(F32)
+        into, half = (fup, fdn)[i // 2], i % 2
+        into[2 * half : 2 * half + 2] = total.astype(BF).reshape(2, 16, width)
     for k in (1, 3, 2):
-        tz, tyc = lax.rem(z + k, 4), lax.rem(y + k + 3, 4)
-        p_o2.append(push(os_.at[0, tyc], oa2.at[k - 1], 62 + k, peer(y=k)))
-        p_o2.append(push(os_.at[1, tz], ob2.at[k - 1], 65 + k, peer(z=k)))
+        p_u.append(push(fup.at[lax.rem(x + k, 4)], gux.at[x], 48 + k, peer(x=k)))
+        p_x.append(push(fdn.at[lax.rem(x + k, 4)], gdn_o.at[x], 76 + k, peer(x=k)))
+    gux[x] = fup[x]
+    kept.append(load(fdn.at[x], gdn_o.at[x]))
+    for copy in p_o2:
+        copy.wait_recv()
+    ta, tb = os_[0, zy].astype(F32), os_[1, z].astype(F32)
+    for g in range(3):
+        ta, tb = ta + oa2[g].astype(F32), tb + ob2[g].astype(F32)
+    fout[:, left], fout[:, right] = ta.astype(BF), tb.astype(BF)
+    p_x.append(push(fout, gout_o, 75, collected()))
 
     for copy in p_q2:
         copy.wait_recv()
@@ -1248,21 +1270,6 @@
             src = fq.at[lax.rem(x + k, 4), :, block_cols]
             p_x.append(push(src, gqkv_o.at[:, own_cols], 83 + 3 * g + k - 1, peer(x=k)))
         kept.append(load(fq.at[x, :, block_cols], gqkv_o.at[:, own_cols]))
-
-    for copy in p_sy:
-        copy.wait_recv()
-    sm[3] = sm[2] + smy[0] + smy[1] + smy[2]
-    p_x += [push(sm.at[3], small_o.at[x], 71 + k, peer(x=k)) for k in (1, 3, 2)]
-    kept.append(load(sm.at[3], small_o.at[x]))
-
-
-    for copy in p_o2:
-        copy.wait_recv()
-    ta, tb = os_[0, zy].astype(F32), os_[1, z].astype(F32)
-    for g in range(3):
-        ta, tb = ta + oa2[g].astype(F32), tb + ob2[g].astype(F32)
-    fout[:, left], fout[:, right] = ta.astype(BF), tb.astype(BF)
-    p_x.append(push(fout, gout_o, 75, collected()))
 
     for copy in p_lz:
         copy.wait_recv()
@@ -1316,6 +1323,8 @@
     d_hidden,
     residual,
     out_part,
+    up_mine,
+    up_two,
     ff_own,
     ff_got,
 ):
@@ -1325,8 +1334,8 @@
     vmem = pl.BlockSpec(memory_space=pltpu.VMEM)
     hbm = pl.BlockSpec(memory_space=pl.ANY)
     outs = [
-        ((blk, width), BF, vmem),
-        ((blk, width), F32, vmem),
+        ((blk, width), BF, hbm),
+        ((blk, width), F32, hbm),
         ((16, 3 * width), BF, hbm),
         ((16, width), BF, hbm),
         ((16, 4 * hidden), F32, vmem),
@@ -1348,10 +1357,11 @@
         ((blk, width), F32),
         ((blk, width), BF),
         ((3, blk, width), BF),
-        ((4, 4, 32, width), BF),
-        ((4, 2, 4, 32, width), BF),
-        ((4, 4, 32, width), BF),
+        ((2, 4, 32, width), BF),
+        ((2, 2, 4, 32, width), BF),
+        ((2, 4, 32, width), BF),
         ((4, 3, 32, width), BF),
+        ((2, 32, width), BF),
         ((4, 16, hidden), BF),
         ((4, 16, width), BF),
         ((span, partw), BF),
@@ -1389,11 +1399,13 @@
         ((2, 2, blk // 4, width), BF),
         ((2, 2, 2, 32, 3 * partw), BF),
         ((2, 2, 2, 16, half), BF),
+        ((blk, width), BF),
+        ((blk, width), F32),
     ]
     return pl.pallas_call(
         attention_backward_body,
         out_shape=tuple(jax.ShapeDtypeStruct(s, d) for s, d, _ in outs),
-        in_specs=[pl.BlockSpec(memory_space=pltpu.SMEM)] + [vmem] * 2 + [hbm] * 19,
+        in_specs=[pl.BlockSpec(memory_space=pltpu.SMEM)] + [vmem] * 2 + [hbm] * 17,
         out_specs=tuple(o[2] for o in outs),
         scratch_shapes=[pltpu.VMEM(s, d) for s, d in scratch]
         + [
@@ -1422,6 +1434,8 @@
         d_hidden,
         residual,
         out_part,
+        up_mine,
+        up_two,
         *ff_own,
         *ff_got,
     )
@@ -1561,12 +1575,10 @@
         mixed,
         d_attn_g,
         out_part,
-        up_a_own,
-        up_b_own,
+        up_mine,
+        up_two,
         down_a_own,
         down_b_own,
-        up_a_got,
-        up_b_got,
         down_a_got,
         down_b_got,
     ) = forward(0, lengths, tok, small.reshape(8, 128), w_up, dy, w_down, w_qkv, w_out)
@@ -1586,8 +1598,10 @@
         d_hidden,
         residual,
         out_part,
-        (up_a_own, up_b_own, down_a_own, down_b_own),
-        (up_a_got, up_b_got, down_a_got, down_b_got),
+        up_mine,
+        up_two,
+        (down_a_own, down_b_own),
+        (down_a_got, down_b_got),
     )
 
     final = list(results(*last))

time: 270 us -> 265 us (0.981)
  Pallas kernels: 259 us -> 255 us
    pallas_call x1, Pallas kernels: 84.3 us -> 77.7 us  [attention_backward(): pl.pallas_call(attention_backward_body, out_shape=tuple((jax.ShapeDtypeSt...]
    pallas_call x1, Pallas kernels: 173 us -> 175 us  [forward(): pl.pallas_call(forward_body, out_shape=tuple((jax.ShapeDtypeStruct(s, d)...]
where the time goes in v7:
time: 265 us
  Pallas kernels  255 us (96%)
  local copies, waits for them, and re-layouts  7.8 us (3%)
    pallas_call x1, Pallas kernels, forward(): pl.pallas_call(forward_body, out_shape=tuple((jax.ShapeDtypeStruct(s, d)...  175 us
    pallas_call x1, Pallas kernels, attention_backward(): pl.pallas_call(attention_backward_body, out_shape=tuple((jax.ShapeDtypeSt...  77.7 us
    unnamed x16, local copies, waits for them, and re-layouts  7.8 us

profile of v7, /device:TPU:1, one launch (start us, length us, event | category | flops | bytes accessed | tf_op | source)
XLA Modules:
  0.0 264.7 jit_solution(17659636525354728788)
XLA Ops:
  0.6 1.4 add_bitcast_fusion.small_in
  2.0 175.3 %forward.1 = (f32[8,2048]{1,0:T(8,128)}, f32[128,2048]{1,0:T(8,128)}, f32[128,2048]{1,0:T(8,128)}, f32[8,2048]{1,0:T(8,128)}, bf16[2,4,4,64,1536]{4,3,2,1,0:T(8,...) custom-call(s32[1,4]{1,0:T(1,128)} %lengths.3, ...), custom_call_target="tpu_custom_call" | custom-call | tf_op jit(solution)/shard_map/forward/pallas_call | solution.py:865
  177.3 77.7 %attention_backward.1 = (bf16[128,2048]{1,0:T(8,128)(2,1)}, f32[128,2048]{1,0:T(8,128)}, bf16[16,6144]{1,0:T(8,128)(2,1)}, bf16[16,2048]{1,0:T(8,128)(2,1)}, f32...) custom-call(s32[1,4]{1,0:T(1,128)} %lengths.3, ...), custom_call_target="tpu_custom_call" | custom-call | tf_op jit(solution)/shard_map/attention_backward/pallas_call | solution.py:1405
  255.1 0.0 copy-start
  255.1 1.2 copy-done
  256.3 0.0 copy-start.1
  256.3 1.0 copy-done.1
  257.4 0.0 copy-start.2
  257.4 1.0 copy-done.2
  258.4 0.0 copy-start.3
  258.4 0.9 copy-done.3
  259.4 0.0 copy-start.4
  259.4 0.9 copy-done.4
  260.3 0.0 copy-start.5
  260.3 0.9 copy-done.5
  261.2 0.0 copy-start.6
  261.2 0.8 copy-done.6
  262.1 0.0 copy-start.7
  262.1 0.8 copy-done.7
  262.9 1.8 results.1
Async XLA Ops:
  255.1 1.2 copy-start
  256.3 1.0 copy-start.1
  257.4 1.0 copy-start.2
  258.4 0.9 copy-start.3
  259.4 0.9 copy-start.4
  260.3 0.9 copy-start.5
  261.2 0.8 copy-start.6
  262.1 0.8 copy-start.7

commit v8 on v7

--- a/solution.py
+++ b/solution.py
@@ -504,13 +504,13 @@
     c_o.arrived(out_g.one)
     out_g.second()
     norm_block(lax.rem(x + 1, 4))
+    c_d.arrived(s_d)
+    down_g.first()
     norm_block(lax.rem(x + 3, 4))
     qkv_g.far()
     tokens.far()
     norm_block(lax.rem(x + 2, 4))
     out_g.near()
-    c_d.arrived(s_d)
-    down_g.first()
     c_u.arrived(s_u)
     up_g.first_b()
     keep_a1 = [comm.local(a1, a1_h)]

time: 265 us -> 264 us (level)
  no operation moved by 1% of the time
where the time goes in v8:
time: 264 us; the launch traced here: 263 us
  Pallas kernels  253 us (96%)
  local copies, waits for them, and re-layouts  7.8 us (3%)
    pallas_call x1, Pallas kernels, forward(): pl.pallas_call(forward_body, out_shape=tuple((jax.ShapeDtypeStruct(s, d)...  175 us
    pallas_call x1, Pallas kernels, attention_backward(): pl.pallas_call(attention_backward_body, out_shape=tuple((jax.ShapeDtypeSt...  76.5 us
    unnamed x16, local copies, waits for them, and re-layouts  7.8 us

profile of v8, /device:TPU:1, one launch (start us, length us, event | category | flops | bytes accessed | tf_op | source)
XLA Modules:
  0.0 263.1 jit_solution(1848691334386774212)
XLA Ops:
  0.6 1.4 add_bitcast_fusion.small_in
  2.0 174.9 %forward.1 = (f32[8,2048]{1,0:T(8,128)}, f32[128,2048]{1,0:T(8,128)}, f32[128,2048]{1,0:T(8,128)}, f32[8,2048]{1,0:T(8,128)}, bf16[2,4,4,64,1536]{4,3,2,1,0:T(8,...) custom-call(s32[1,4]{1,0:T(1,128)} %lengths.3, ...), custom_call_target="tpu_custom_call" | custom-call | tf_op jit(solution)/shard_map/forward/pallas_call | solution.py:865
  177.0 76.5 %attention_backward.1 = (bf16[128,2048]{1,0:T(8,128)(2,1)}, f32[128,2048]{1,0:T(8,128)}, bf16[16,6144]{1,0:T(8,128)(2,1)}, bf16[16,2048]{1,0:T(8,128)(2,1)}, f32...) custom-call(s32[1,4]{1,0:T(1,128)} %lengths.3, ...), custom_call_target="tpu_custom_call" | custom-call | tf_op jit(solution)/shard_map/attention_backward/pallas_call | solution.py:1405
  253.5 0.0 copy-start
  253.5 1.2 copy-done
  254.7 0.0 copy-start.1
  254.7 1.0 copy-done.1
  255.8 0.0 copy-start.2
  255.8 1.0 copy-done.2
  256.8 0.0 copy-start.3
  256.8 0.9 copy-done.3
  257.7 0.0 copy-start.4
  257.7 0.9 copy-done.4
  258.7 0.0 copy-start.5
  258.7 0.9 copy-done.5
  259.6 0.0 copy-start.6
  259.6 0.8 copy-done.6
  260.5 0.0 copy-start.7
  260.5 0.8 copy-done.7
  261.3 1.8 results.1
Async XLA Ops:
  253.5 1.2 copy-start
  254.7 1.0 copy-start.1
  255.8 1.0 copy-start.2
  256.8 0.9 copy-start.3
  257.7 0.9 copy-start.4
  258.7 0.9 copy-start.5
  259.6 0.8 copy-start.6
  260.5 0.8 copy-start.7

commit v9 on v8

--- a/solution.py
+++ b/solution.py
@@ -1264,12 +1264,9 @@
         ta, tb = ta + qa2[g].astype(F32), tb + qb2[g].astype(F32)
     fq[0:2] = ta.astype(BF).reshape(2, 16, 3 * partw)
     fq[2:4] = tb.astype(BF).reshape(2, 16, 3 * partw)
-    for g in range(3):
-        block_cols, own_cols = pl.ds(g * partw, partw), pl.ds(g * width + x * partw, partw)
-        for k in (1, 3, 2):
-            src = fq.at[lax.rem(x + k, 4), :, block_cols]
-            p_x.append(push(src, gqkv_o.at[:, own_cols], 83 + 3 * g + k - 1, peer(x=k)))
-        kept.append(load(fq.at[x, :, block_cols], gqkv_o.at[:, own_cols]))
+    for k in (1, 3, 2):
+        p_x.append(push(fq.at[lax.rem(x + k, 4)], gqkv_o.at[x], 82 + k, peer(x=k)))
+    kept.append(load(fq.at[x], gqkv_o.at[x]))
 
     for copy in p_lz:
         copy.wait_recv()
@@ -1336,7 +1333,7 @@
     outs = [
         ((blk, width), BF, hbm),
         ((blk, width), F32, hbm),
-        ((16, 3 * width), BF, hbm),
+        ((4, 16, 3 * partw), BF, hbm),
         ((16, width), BF, hbm),
         ((16, 4 * hidden), F32, vmem),
         ((4, 16, width), BF, hbm),
@@ -1470,7 +1467,11 @@
     device = ((me["y"] * 2 + me["core"]) * 4 + me["z"]) * 4 + me["x"]
     out_o[...] = out[...]
     gtok_o[...] = gtok[...]
-    gqkv_o[...] = gqkv[...].astype(F32)
+    cut = gqkv.shape[2] // 3
+    for g in range(3):
+        for c in range(4):
+            at = (4 * g + c) * cut
+            gqkv_o[:, at : at + cut] = gqkv[c, :, g * cut : (g + 1) * cut].astype(F32)
     gout_o[...] = gout[...].astype(F32)
     gup_o[...] = gup[...]
     gdn_o[...] = gdn[...].reshape(gdn_o.shape).astype(F32)
@@ -1513,7 +1514,7 @@
         (gtok.shape, F32),
         vector(16),
         vector(16),
-        (gqkv.shape, F32),
+        ((16, 4 * gqkv.shape[2]), F32),
         vector(32),
         (gout.shape, F32),
         vector(16),

time: 264 us -> 264 us (level)
  no operation moved by 1% of the time
where the time goes in v9:
time: 264 us; the launch traced here: 263 us
  Pallas kernels  253 us (96%)
  local copies, waits for them, and re-layouts  7.8 us (3%)
    pallas_call x1, Pallas kernels, forward(): pl.pallas_call(forward_body, out_shape=tuple((jax.ShapeDtypeStruct(s, d)...  175 us
    pallas_call x1, Pallas kernels, attention_backward(): pl.pallas_call(attention_backward_body, out_shape=tuple((jax.ShapeDtypeSt...  76.5 us
    unnamed x16, local copies, waits for them, and re-layouts  7.8 us

profile of v9, /device:TPU:1, one launch (start us, length us, event | category | flops | bytes accessed | tf_op | source)
XLA Modules:
  0.0 263.1 jit_solution(1395138056140616336)
XLA Ops:
  0.6 1.4 add_bitcast_fusion.small_in
  2.0 174.9 %forward.1 = (f32[8,2048]{1,0:T(8,128)}, f32[128,2048]{1,0:T(8,128)}, f32[128,2048]{1,0:T(8,128)}, f32[8,2048]{1,0:T(8,128)}, bf16[2,4,4,64,1536]{4,3,2,1,0:T(8,...) custom-call(s32[1,4]{1,0:T(1,128)} %lengths.3, ...), custom_call_target="tpu_custom_call" | custom-call | tf_op jit(solution)/shard_map/forward/pallas_call | solution.py:865
  177.0 76.5 %attention_backward.1 = (bf16[128,2048]{1,0:T(8,128)(2,1)}, f32[128,2048]{1,0:T(8,128)}, bf16[4,16,1536]{2,1,0:T(8,128)(2,1)}, bf16[16,2048]{1,0:T(8,128)(2,1)},...) custom-call(s32[1,4]{1,0:T(1,128)} %lengths.3, ...), custom_call_target="tpu_custom_call" | custom-call | tf_op jit(solution)/shard_map/attention_backward/pallas_call | solution.py:1402
  253.5 0.0 copy-start
  253.5 1.2 copy-done
  254.7 0.0 copy-start.1
  254.7 1.0 copy-done.1
  255.7 0.0 copy-start.2
  255.7 1.0 copy-done.2
  256.8 0.0 copy-start.3
  256.8 0.9 copy-done.3
  257.7 0.0 copy-start.4
  257.7 0.9 copy-done.4
  258.7 0.0 copy-start.5
  258.7 0.9 copy-done.5
  259.6 0.0 copy-start.6
  259.6 0.8 copy-done.6
  260.5 0.0 copy-start.7
  260.5 0.8 copy-done.7
  261.3 1.8 results.1
Async XLA Ops:
  253.5 1.2 copy-start
  254.7 1.0 copy-start.1
  255.7 1.0 copy-start.2
  256.8 0.9 copy-start.3
  257.7 0.9 copy-start.4
  258.7 0.9 copy-start.5
  259.6 0.8 copy-start.6
  260.5 0.8 copy-start.7
